TPU v7x, 32 devices: a whole 2x2x4 slice. The times are simulated.
32 devices in a mesh: row: 8 (over y, x, core), col: 4 (over z).
Axes of the slice: x: 2, y: 2, z: 4, core: 2. Of those that a mesh axis runs over, the one named last changes fastest.
Arguments:
- features: bfloat16 [12, 8, 128, 512], P(None, 'row', 'col'), may hold values from -6 to 6
Outputs:
- panels: float32 [12, 8, 128, 256], P(None, 'row')
- trailing: float32 [12, 8, 128, 24, 4, 128], P(None, 'row', None, None, 'col')
All inputs are finite; a program needn't handle non-finite values.
Results may differ from a plain program's by a relative error of at most 0.0003.
Values may be sent and summed in bfloat16 or wider, within the bound.
No kernel may reach another device: no remote copies, remote signals or barrier semaphores. Data moves between devices by JAX's collectives and lax.ppermute only.
A program may use at most 128 MiB of HBM per device.

v0:
```python
import functools

import jax
import jax.numpy as jnp
from jax import lax
from jax.experimental import pallas as pl
from jax.experimental.pallas import tpu as pltpu
from jax.sharding import PartitionSpec as P

F = 512
PANEL = 256
TILE = 128
RIDGE = 1.0
EPS = 1e-6

PV = (-2.265364170074463, -4.70527982711792, 7.536093711853027,
      0.7343835830688477, -1.7677195072174072, 0.3254770040512085)
QV = (1.8269329071044922, 3.1679749488830566, -4.871670722961426,
      0.626383364200592, 0.07849788665771484)
TINY = 1e-30
NT = (((1,), (1,)), ((), ()))
VMEM_LIMIT = 60 * 2**20


def dot_nt(a, b):
    return lax.dot_general(a, b, NT, preferred_element_type=jnp.float32)


def dot_hi(a, b, dims):
    return lax.dot_general(
        a, b, (dims, ((), ())), precision=lax.Precision.HIGHEST,
        preferred_element_type=jnp.float32,
    )


def horner(x, coefs):
    acc = coefs[-1]
    for c in coefs[-2::-1]:
        acc = acc * x + c
    return acc


def two_layers(rho):
    a = jnp.maximum(1.0 - rho, TINY)
    b = jnp.maximum(1.0 + rho, TINY)
    u = a * lax.rsqrt(a)
    v = b * lax.rsqrt(b)
    return horner(v, PV) + u * horner(v, QV)


def norm_rows(x):
    xf = x.astype(jnp.float32)
    return jnp.sum(xf * xf, axis=1, keepdims=True) / F


def norm_lanes(x):
    xf = x.astype(jnp.float32)
    sq = xf * xf
    hi = sq.astype(jnp.bfloat16)
    lo = (sq - hi.astype(jnp.float32)).astype(jnp.bfloat16)
    ones = jnp.ones((8, x.shape[1]), jnp.bfloat16)
    return (dot_nt(ones, hi) + dot_nt(ones, lo)) / F


def eye(n):
    return lax.broadcasted_iota(jnp.int32, (n, n), 0) == lax.broadcasted_iota(
        jnp.int32, (n, n), 1
    )


def eliminate(w_ref, t_ref):
    n = TILE
    sub = lax.broadcasted_iota(jnp.int32, (8, n), 0)
    for p in range(0, n, 8):
        a8 = w_ref[p : p + 8, :n]
        e8 = w_ref[p : p + 8, n:]
        cols = [jnp.broadcast_to(a8[:, p + k : p + k + 1], (8, n)) for k in range(8)]
        root = jnp.ones((8, n), jnp.float32)
        invs, ups = [], []
        for k in range(8):
            piv = cols[k][k : k + 1, :]
            inv = 1.0 / piv
            m = jnp.where(sub > k, cols[k] * inv, 0.0)
            ak, ek = a8[k : k + 1, :], e8[k : k + 1, :]
            up = [cols[j][k : k + 1, :] for j in range(k + 1, 8)]
            for j in range(k + 1, 8):
                cols[j] = cols[j] - m * up[j - k - 1]
            a8 = a8 - m * ak
            e8 = e8 - m * ek
            root = jnp.where(sub == k, lax.rsqrt(piv), root)
            invs.append(inv)
            ups.append((ak, ek, up))
        t_ref[p : p + 8, :] = e8 * root
        for g in range(p + 8, n, 8):
            a = w_ref[g : g + 8, :n]
            e = w_ref[g : g + 8, n:]
            cs = [jnp.broadcast_to(a[:, p + k : p + k + 1], (8, n)) for k in range(8)]
            for k in range(8):
                ak, ek, up = ups[k]
                m = cs[k] * invs[k]
                for j in range(k + 1, 8):
                    cs[j] = cs[j] - m * up[j - k - 1]
                a = a - m * ak
                e = e - m * ek
            w_ref[g : g + 8, :n] = a
            w_ref[g : g + 8, n:] = e


def factor_kernel(x_ref, t_ref, sp_ref, bp_ref, k_ref, w_ref, t1_ref, t2_ref):
    x = x_ref[...]
    gq_l = norm_lanes(x)
    s_l = jnp.sqrt(gq_l + EPS)
    b_l = 1.0 / s_l
    sp_ref[...] = s_l
    bp_ref[...] = b_l
    gq = norm_rows(x)
    s = jnp.sqrt(gq + EPS)
    rho = dot_nt(x, x) * ((1.0 / F) / s) * b_l[0:1, :]
    k = two_layers(rho) * (s * s_l[0:1, :])
    k_ref[...] = jnp.where(eye(PANEL), 3.0 * gq + (2.0 * EPS + RIDGE), k)
    h = PANEL // 2
    ident = jnp.where(eye(h), 1.0, 0.0)
    w_ref[:, :h] = k_ref[:h, :h]
    w_ref[:, h:] = ident
    eliminate(w_ref, t1_ref)
    t1 = t1_ref[...]
    l21 = dot_hi(k_ref[h:, :h], t1, ((1,), (1,)))
    w_ref[:, :h] = k_ref[h:, h:] - dot_hi(l21, l21, ((1,), (1,)))
    w_ref[:, h:] = ident
    eliminate(w_ref, t2_ref)
    t2 = t2_ref[...]
    t_ref[:h, :h] = t1
    t_ref[:h, h:] = jnp.zeros((h, h), jnp.float32)
    t_ref[h:, :h] = -dot_hi(t2, dot_hi(l21, t1, ((1,), (0,))), ((1,), (0,)))
    t_ref[h:, h:] = t2


def factor(points):
    full = jax.ShapeDtypeStruct((PANEL, PANEL), jnp.float32)
    vec = jax.ShapeDtypeStruct((8, PANEL), jnp.float32)
    return pl.pallas_call(
        factor_kernel,
        out_shape=[full, vec, vec],
        scratch_shapes=[
            pltpu.VMEM((PANEL, PANEL), jnp.float32),
            pltpu.VMEM((TILE, 2 * TILE), jnp.float32),
            pltpu.VMEM((TILE, TILE), jnp.float32),
            pltpu.VMEM((TILE, TILE), jnp.float32),
        ],
        compiler_params=pltpu.CompilerParams(vmem_limit_bytes=VMEM_LIMIT),
        cost_estimate=pl.CostEstimate(flops=10**9, bytes_accessed=10**7, transcendentals=0),
        name="factor",
    )(points)


def panel_kernel(is_rows, block, tau_ref, x_ref, pts_ref, t_ref, sp_ref, bp_ref, *refs):
    outs, k_ref = refs[:-1], refs[-1]
    x = x_ref[...]
    gq = norm_rows(x)
    s = jnp.sqrt(gq + EPS)
    a = (1.0 / F) / s
    diag = 3.0 * gq + (2.0 * EPS + RIDGE)
    k_ref[...] = dot_nt(x, pts_ref[...])
    sp = sp_ref[0:1, :]
    bp = bp_ref[0:1, :]
    for g in range(0, block, 16):
        rows = slice(g, g + 16)
        rho = k_ref[rows, :] * a[rows, :] * bp
        k_ref[rows, :] = two_layers(rho) * (s[rows, :] * sp)
    for half in range(PANEL // TILE):

        @pl.when((pl.program_id(0) == 0) & (tau_ref[0] == half))
        def _():
            cols = slice(half * TILE, (half + 1) * TILE)
            k_ref[:TILE, cols] = jnp.where(eye(TILE), diag[:TILE, :], k_ref[:TILE, cols])

    low = dot_hi(k_ref[...], t_ref[...], ((1,), (1,)))
    hi = low.astype(jnp.bfloat16)
    lo = (low - hi.astype(jnp.float32)).astype(jnp.bfloat16)
    if is_rows:
        l_ref, cat_ref, s_ref, a_ref, d_ref = outs
        l_ref[...] = low
        cat_ref[:, :PANEL] = hi
        cat_ref[:, PANEL : 2 * PANEL] = hi
        cat_ref[:, 2 * PANEL :] = lo
        s_ref[...] = jnp.broadcast_to(s, s_ref.shape)
        a_ref[...] = jnp.broadcast_to(a, a_ref.shape)
        left = diag - jnp.sum(low * low, axis=1, keepdims=True)
        d_ref[...] = jnp.broadcast_to(left, d_ref.shape)
    else:
        cat_ref, s_ref, b_ref = outs
        cat_ref[:, :PANEL] = hi
        cat_ref[:, PANEL : 2 * PANEL] = lo
        cat_ref[:, 2 * PANEL :] = hi
        s_l = jnp.sqrt(norm_lanes(x) + EPS)
        s_ref[...] = s_l
        b_ref[...] = 1.0 / s_l


def pick(total, options):
    for o in options:
        if total % o == 0:
            return o
    return total


def panel(is_rows, x, points, t, sp, bp, tau):
    m = x.shape[0]
    block = pick(m, (512, 384, 256, 128))
    const = lambda shape: pl.BlockSpec(shape, lambda i: (0, 0))
    by_row = lambda width: pl.BlockSpec((block, width), lambda i: (i, 0))
    by_lane = pl.BlockSpec((8, block), lambda i: (0, i))
    f32 = lambda *shape: jax.ShapeDtypeStruct(shape, jnp.float32)
    cat = jax.ShapeDtypeStruct((m, 3 * PANEL), jnp.bfloat16)
    if is_rows:
        shapes = [f32(m, PANEL), cat, f32(m, 128), f32(m, 128), f32(m, 128)]
        specs = [by_row(PANEL), by_row(3 * PANEL)] + [by_row(128)] * 3
    else:
        shapes = [cat, f32(8, m), f32(8, m)]
        specs = [by_row(3 * PANEL), by_lane, by_lane]
    return pl.pallas_call(
        functools.partial(panel_kernel, is_rows, block),
        grid=(m // block,),
        in_specs=[
            pl.BlockSpec(memory_space=pltpu.SMEM),
            by_row(F), const((PANEL, F)), const((PANEL, PANEL)),
            const((8, PANEL)), const((8, PANEL)),
        ],
        out_specs=specs,
        out_shape=shapes,
        scratch_shapes=[pltpu.VMEM((block, PANEL), jnp.float32)],
        compiler_params=pltpu.CompilerParams(vmem_limit_bytes=VMEM_LIMIT),
        cost_estimate=pl.CostEstimate(
            flops=2 * m * PANEL * (F + 6 * PANEL), bytes_accessed=m * 4096, transcendentals=0
        ),
        name="panel_rows" if is_rows else "panel_cols",
    )(tau, x, points, t, sp, bp)


def trailing_kernel(rb, cb, tb, steps, step_tiles, diag_ref, xr, xc, lr, lc, sr, ar, dr, sc, bc,
                    out, ga, ma, gb, mb):
    i = pl.program_id(0)
    r0 = pl.multiple_of(i * rb, rb)
    per = cb // TILE
    chunks = tb // per

    def multiply(row, col, g, m):
        g[...] = dot_nt(xr[pl.ds(row, rb), :], xc[pl.ds(col, cb), :])
        m[...] = dot_nt(lr[pl.ds(row, rb), :], lc[pl.ds(col, cb), :])

    def finish(n, g, m):
        for t in range(per):
            lanes = pl.ds(pl.multiple_of(n * cb + t * TILE, TILE), TILE)
            s_col = sc[0:1, lanes]
            b_col = bc[0:1, lanes]
            here = slice(t * TILE, (t + 1) * TILE)
            for k in range(0, rb, 16):
                rows = pl.ds(r0 + k, 16)
                rho = g[k : k + 16, here] * ar[rows, :] * b_col
                val = two_layers(rho) * (sr[rows, :] * s_col) - m[k : k + 16, here]
                out[pl.ds(k * tb + n * per + t, 16, stride=tb), :] = val

    @pl.when(i == 0)
    def _():
        multiply(0, 0, ga, ma)

    @pl.loop(0, chunks // 2)
    def _(h):
        n = 2 * h
        multiply(r0, pl.multiple_of((n + 1) * cb, cb), gb, mb)
        finish(n, ga, ma)
        last = n + 2 >= chunks
        row = jnp.where(last, jnp.minimum(i + 1, steps - 1) * rb, r0)
        col = jnp.where(last, 0, (n + 2) * cb)
        multiply(pl.multiple_of(row, rb), pl.multiple_of(col, cb), ga, ma)
        finish(n + 1, gb, mb)

    @pl.when(diag_ref[0] == 1)
    def _():
        for tile in range(rb // TILE):
            col = (i * (rb // TILE) + tile) * step_tiles + diag_ref[1]
            for k in range(0, TILE, 16):
                rows = pl.ds(r0 + tile * TILE + k, 16)
                same = lax.broadcasted_iota(jnp.int32, (16, TILE), 1) == (
                    lax.broadcasted_iota(jnp.int32, (16, TILE), 0) + k
                )
                at = pl.ds((tile * TILE + k) * tb + col, 16, stride=tb)
                out[at, :] = jnp.where(same, dr[rows, :], out[at, :])


def trailing(x_rows, x_cols, cat_rows, cat_cols, s, a, d, sc, bc, diag, step_tiles):
    m, n = x_rows.shape[0], x_cols.shape[0]
    tb = n // TILE
    rb = pick(m, (512, 384, 256, 128))
    cb = 2 * TILE if (tb // 2) % 2 == 0 and tb % 2 == 0 else TILE
    const = lambda shape: pl.BlockSpec(shape, lambda i: (0, 0))
    return pl.pallas_call(
        functools.partial(trailing_kernel, rb, cb, tb, m // rb, step_tiles),
        grid=(m // rb,),
        in_specs=[
            pl.BlockSpec(memory_space=pltpu.SMEM),
            const((m, F)), const((n, F)), const((m, 3 * PANEL)), const((n, 3 * PANEL)),
            const((m, 128)), const((m, 128)), const((m, 128)), const((8, n)), const((8, n)),
        ],
        out_specs=pl.BlockSpec((rb * tb, TILE), lambda i: (i, 0)),
        out_shape=jax.ShapeDtypeStruct((m * tb, TILE), jnp.float32),
        scratch_shapes=[pltpu.VMEM((rb, cb), jnp.float32)] * 4,
        compiler_params=pltpu.CompilerParams(vmem_limit_bytes=VMEM_LIMIT),
        cost_estimate=pl.CostEstimate(
            flops=2 * m * n * (F + 3 * PANEL), bytes_accessed=m * n * 4, transcendentals=0
        ),
        name="trailing",
    )(diag, x_rows, x_cols, cat_rows, cat_cols, s, a, d, sc, bc)


def spread(data, n_row, n_col, r, c):
    low = n_col.bit_length() - 1
    high = n_row.bit_length() - 1

    def send(value, bit, mask):
        pairs = [
            (i * n_col + j, (i ^ (1 << bit)) * n_col + j)
            for i in range(n_row) for j in range(n_col) if (i ^ j) & mask == 0
        ]
        return lax.ppermute(value, ("row", "col"), pairs)

    mask = n_col - 1
    for bit in range(low - 1, 0, -1):
        got = send(data, bit, mask)
        mask &= ~(1 << bit)
        data = jnp.where(((r ^ c) >> bit) & 1 == 0, data, got)
    parts = data[None]
    for bit in range(low, high):
        got = send(parts, bit, mask)
        first = (r >> bit) & 1 == 0
        parts = jnp.concatenate([jnp.where(first, parts, got), jnp.where(first, got, parts)])
    if low > 0:
        got = send(parts, 0, mask)
        parts = jnp.where((r ^ c) & 1 == 0, parts, got)
    return parts


def local(features):
    n_row, n_col = lax.axis_size("row"), lax.axis_size("col")
    r, c = lax.axis_index("row"), lax.axis_index("col")
    tiles_r, _, thin, width = features.shape
    step_tiles = n_row // n_col
    tiles_c = tiles_r * step_tiles
    tile = thin * n_col

    points = lax.all_gather(features[0, 0], "row", axis=0)[: PANEL // tile]
    points = lax.all_gather(points, "col", axis=1, tiled=True).reshape(PANEL, width)
    t, sp, bp = factor(points)

    row_feat = lax.all_gather(features, "col", axis=2, tiled=True).reshape(tiles_r, tile, width)
    x_rows = row_feat.reshape(tiles_r * tile, width)
    col_feat = spread(row_feat, n_row, n_col, r, c)
    x_cols = jnp.swapaxes(col_feat, 0, 1).reshape(tiles_c * tile, width)

    tau = lambda i: jnp.where(i < PANEL // tile, i, -1).astype(jnp.int32).reshape(1)
    low, cat_rows, s, a, d = panel(True, x_rows, points, t, sp, bp, tau(r))
    cat_cols, sc, bc = panel(False, x_cols, points, t, sp, bp, tau(c))
    on_diag = ((r - c) % n_col == 0).astype(jnp.int32)
    diag = jnp.stack([on_diag, (r - c) // n_col]).astype(jnp.int32)
    out = trailing(x_rows, x_cols, cat_rows, cat_cols, s, a, d, sc, bc, diag, step_tiles)
    return (
        low.reshape(tiles_r, 1, tile, PANEL),
        out.reshape(tiles_r, 1, tile, tiles_c, 1, tile),
    )


def solution(mesh):
    return jax.shard_map(
        local,
        mesh=mesh,
        in_specs=(P(None, "row", "col", None),),
        out_specs=(P(None, "row", None, None), P(None, "row", None, None, "col", None)),
        check_vma=False,
    )
```

profile of v0, /device:TPU:0, one launch (start us, length us, event | category | flops | bytes accessed | tf_op | source)
XLA Modules:
  0.0 208.5 jit_solution(11005917505548667139)
XLA Ops:
  7.2 0.0 all-gather.4.cloned.1.call-start
  7.2 0.7 all-gather.4.cloned.1.call-update
  7.9 41.5 %all-gather.4.cloned.1.call-done = bf16[12,1,128,512]{3,2,1,0:T(8,128)(2,1)} async-done(((bf16[12,1,32,512]{3,2,1,0:T(8,128)(2,1)}), bf16[12,1,128,512]{3,2,1,0:T(8,128)(2,1)}) %all-gather.4.cloned.1.call-update) | async-done | bytes 1572880 | tf_op jit(solution)/shard_map/all_gather | solution.py:355
  49.4 3.5 %collective-permute-start = (bf16[12,128,512]{2,1,0:T(8,128)(2,1)}, bf16[12,128,512]{2,1,0:T(8,128)(2,1)S(1)}, u32[]{:S(2)}, u32[]{:S(2)}) collective-permute-start(bf16[12,128,512]{2,1,0:T(8,128)(2,1)} %bitcast.21), channel_id=1, source_target_pairs={{0,8},{5,13},{10,2},{15,7},{16,24},{21,29},{26,18},{31,23}} | collective-permute-start | bytes 4718600 | tf_op jit(solution)/shard_map/ppermute | solution.py:325
  52.9 18.1 %collective-permute-done = bf16[12,128,512]{2,1,0:T(8,128)(2,1)S(1)} collective-permute-done((bf16[12,128,512]{2,1,0:T(8,128)(2,1)}, bf16[12,128,512]{2,1,0:T(8,128)(2,1)S(1)}, u32[]{:S(2)}, u32[]{:S(2)}) %collective-permute-start) | collective-permute-done | bytes 1572896 | tf_op jit(solution)/shard_map/ppermute | solution.py:325
  71.0 1.6 select_bitcast_fusion.1
  72.6 0.0 copy-start
  72.6 3.4 %collective-permute-start.1 = (bf16[1,12,128,512]{3,2,1,0:T(8,128)(2,1)S(1)}, bf16[1,12,128,512]{3,2,1,0:T(8,128)(2,1)}, u32[]{:S(2)}, u32[]{:S(2)}) collective-permute-start(bf16[1,12,128,512]{3,2,1,0:T(8,128)(2,1)S(1)} %select_bitcast_fusion.1), channel_id=1, source_target_pairs={{0,16},{2,18},{5,21},{7,23},{8,24},{10,26},{13,29},{15,31},{16,0},... | collective-permute-start | bytes 4718600 | tf_op jit(solution)/shard_map/ppermute | solution.py:325
  76.0 0.0 copy-done
  76.0 19.0 %collective-permute-done.1 = bf16[1,12,128,512]{3,2,1,0:T(8,128)(2,1)} collective-permute-done((bf16[1,12,128,512]{3,2,1,0:T(8,128)(2,1)S(1)}, bf16[1,12,128,512]{3,2,1,0:T(8,128)(2,1)}, u32[]{:S(2)}, u32[]{:S(2)}) %collective-permute-start.1) | collective-permute-done | bytes 1572896 | tf_op jit(solution)/shard_map/ppermute | solution.py:325
  95.0 2.1 %broadcast_select_fusion.1 = (bf16[1,12,128,512]{3,2,1,0:T(8,128)(2,1)S(1)}, bf16[1,12,128,512]{3,2,1,0:T(8,128)(2,1)S(1)}) fusion(bf16[1,12,128,512]{3,2,1,0:T(8,128)(2,1)} %copy-done, bf16[1,12,128,512]{3,2,1,0:T(8,128)(2,1)} %collective-permute-done.1, pred[]{:T(512)S(6)} %eq.16), kind=kLoop, calls=%fused_computation.4 | loop fusion | flops 1572864 | bytes 6291457 | tf_op jit(solution)/shard_map/jit(_where)/select_n | solution.py:336
  97.1 1.9 pad_maximum_fusion
  99.0 2.9 %collective-permute-start.2 = (bf16[2,12,128,512]{3,2,1,0:T(8,128)(2,1)}, bf16[2,12,128,512]{3,2,1,0:T(8,128)(2,1)}, u32[]{:S(2)}, u32[]{:S(2)}) collective-permute-start(bf16[2,12,128,512]{3,2,1,0:T(8,128)(2,1)} %pad_maximum_fusion), channel_id=1, source_target_pairs={{0,4},{2,6},{5,1},{7,3},{8,12},{10,14},{13,9},{15,11},{16,20},{18,... | collective-permute-start | bytes 9437192 | tf_op jit(solution)/shard_map/ppermute | solution.py:325
  101.9 0.8 slice.6
  102.7 10.2 %all-gather = bf16[8,1,32,512]{3,2,1,0:T(8,128)(2,1)S(1)} all-gather(bf16[1,1,32,512]{3,2,1,0:T(8,128)(2,1)S(1)} %slice.6), channel_id=2, replica_groups=mesh['row'=8,'col'=4] {'row'}, dimensions={0}, use_global_device_ids=true | all-gather | bytes 294912 | tf_op jit(solution)/shard_map/all_gather | solution.py:351
  112.9 15.1 %all-gather.1 = bf16[2,1,128,512]{3,2,1,0:T(8,128)(2,1)} all-gather(bf16[2,1,32,512]{3,2,1,0:T(8,128)(2,1)S(1)} %slice.9), channel_id=3, replica_groups=mesh['row'=8,'col'=4] {'col'}, dimensions={2}, use_global_device_ids=true | all-gather | bytes 327680 | tf_op jit(solution)/shard_map/all_gather | solution.py:352
  128.0 10.9 %factor.1 = (f32[256,256]{1,0:T(8,128)}, f32[8,256]{1,0:T(8,128)}, f32[8,256]{1,0:T(8,128)}) custom-call(bf16[256,512]{1,0:T(8,128)(2,1)} %bitcast.24), custom_call_target="tpu_custom_call" | custom-call | flops 1000000000 | bytes 10000000 | tf_op jit(solution)/shard_map/factor/pallas_call | solution.py:141
  138.9 0.6 pad_add_fusion.diag_ref
  139.5 8.0 %panel_rows.1 = (f32[1536,256]{1,0:T(8,128)}, bf16[1536,768]{1,0:T(8,128)(2,1)}, f32[1536,128]{1,0:T(8,128)}, f32[1536,128]{1,0:T(8,128)}, f32[1536,128]{1,0:T(8,128)}) custom-call(s32[1]{0:T(128)} %bitcast.tau_ref, bf16[1536,512]{1,0:T(8,128)(2,1)} %bitcast.22, bf16[256,512]{1,0:T(8,128)(2,1)} %bitcast.25, f32[256,256]{1,0:T(8,128)} %get-tuple-element.13.t_ref, ...), custom_call_target="tpu_custom_call" | custom-call | flops 1610612736 | bytes 6291456 | tf_op jit(solution)/shard_map/panel_rows/pallas_call | solution.py:221
  147.5 0.0 collective-permute-done.2
  147.5 0.4 select_bitcast_fusion
  147.9 2.0 copy.6
  149.9 14.2 %panel_cols.1 = (bf16[3072,768]{1,0:T(8,128)(2,1)}, f32[8,3072]{1,0:T(8,128)}, f32[8,3072]{1,0:T(8,128)}) custom-call(s32[1]{0:T(128)} %bitcast.11.tau_ref, bf16[3072,512]{1,0:T(8,128)(2,1)} %bitcast.19, bf16[256,512]{1,0:T(8,128)(2,1)} %bitcast.26, f32[256,256]{1,0:T(8,128)} %get-tuple-element.13.t_ref, f32[8,256]{1,0:T(8,128)} %get-tuple-element.14.sp_ref, ...), custom_call_target="tpu_custom_call" | custom-call | flops 3221225472 | bytes 12582912 | tf_op jit(solution)/shard_map/panel_cols/pallas_call | solution.py:221
  164.2 37.5 %trailing.1 = f32[36864,128]{1,0:T(8,128)} custom-call(s32[2]{0:T(128)} %pad_add_fusion.diag_ref, bf16[1536,512]{1,0:T(8,128)(2,1)} %bitcast.23, bf16[3072,512]{1,0:T(8,128)(2,1)} %bitcast.20, bf16[1536,768]{1,0:T(8,128)(2,1)} %get-tuple-element.17.lr, bf16[3072,768]{1,0:T(8,128)(2,1)} %get-tuple-element.18.lc, f32[1536,128]{1,0:T(8,128)} %get-tuple-element.19.sr, ...), custom_call_target="tpu_custom_call" | custom-call | flops 12079595520 | bytes 18874368 | tf_op jit(solution)/shard_map/trailing/pallas_call | solution.py:297
  (1 shorter events, 0.0 us)
Async XLA Ops:
  7.2 42.2 %all-gather.4.cloned.1.call-start = ((), (), s32[]{:S(2)}) async-start(), calls=%async_computation | async-start | bytes 1966080 | tf_op jit(solution)/shard_map/all_gather | solution.py:355
  49.4 21.6 %collective-permute-start = (bf16[12,128,512]{2,1,0:T(8,128)(2,1)}, bf16[12,128,512]{2,1,0:T(8,128)(2,1)S(1)}, u32[]{:S(2)}, u32[]{:S(2)}) collective-permute-start(bf16[12,128,512]{2,1,0:T(8,128)(2,1)} %bitcast.21), channel_id=1, source_target_pairs={{0,8},{5,13},{10,2},{15,7},{16,24},{21,29},{26,18},{31,23}} | collective-permute-start | bytes 4718600 | tf_op jit(solution)/shard_map/ppermute | solution.py:325
  72.6 3.4 %copy-start = (bf16[1,12,128,512]{3,2,1,0:T(8,128)(2,1)}, bf16[1,12,128,512]{3,2,1,0:T(8,128)(2,1)S(1)}, u32[]{:S(2)}) copy-start(bf16[1,12,128,512]{3,2,1,0:T(8,128)(2,1)S(1)} %select_bitcast_fusion.1) | copy-start | bytes 4718596
  72.6 22.4 %collective-permute-start.1 = (bf16[1,12,128,512]{3,2,1,0:T(8,128)(2,1)S(1)}, bf16[1,12,128,512]{3,2,1,0:T(8,128)(2,1)}, u32[]{:S(2)}, u32[]{:S(2)}) collective-permute-start(bf16[1,12,128,512]{3,2,1,0:T(8,128)(2,1)S(1)} %select_bitcast_fusion.1), channel_id=1, source_target_pairs={{0,16},{2,18},{5,21},{7,23},{8,24},{10,26},{13,29},{15,31},{16,0},... | collective-permute-start | bytes 4718600 | tf_op jit(solution)/shard_map/ppermute | solution.py:325
  99.0 48.5 %collective-permute-start.2 = (bf16[2,12,128,512]{3,2,1,0:T(8,128)(2,1)}, bf16[2,12,128,512]{3,2,1,0:T(8,128)(2,1)}, u32[]{:S(2)}, u32[]{:S(2)}) collective-permute-start(bf16[2,12,128,512]{3,2,1,0:T(8,128)(2,1)} %pad_maximum_fusion), channel_id=1, source_target_pairs={{0,4},{2,6},{5,1},{7,3},{8,12},{10,14},{13,9},{15,11},{16,20},{18,... | collective-permute-start | bytes 9437192 | tf_op jit(solution)/shard_map/ppermute | solution.py:325
Sparse Core Ops, SparseCore 0:
  9.6 39.7 all-gather.3
where the time goes:
time: 209 us; the launch traced here: 208 us
  waiting for transfers between devices  79.3 us (38%)
  Pallas kernels  70.6 us (34%)
  blocking collectives  25.3 us (12%)
  between operations  14.1 us (7%)
  starting transfers between devices  9.8 us (5%)
  other arithmetic  6.6 us (3%)
  local copies, waits for them, and re-layouts  2.75 us (1%)
    all_gather x1, waiting for transfers between devices, local(): lax.all_gather(features, 'col', axis=2, tiled=True)  41.5 us
    pallas_call x1, Pallas kernels, trailing(): pl.pallas_call(functools.partial(trailing_kernel, rb, cb, tb, m // rb, st...  37.5 us
    ppermute x3, waiting for transfers between devices, send(): return lax.ppermute(value, ('row', 'col'), pairs)  37.1 us
    pallas_call x2, Pallas kernels, panel(): pl.pallas_call(functools.partial(panel_kernel, is_rows, block), grid=(m /...  22.3 us
    all_gather x1, blocking collectives, local(): lax.all_gather(points, 'col', axis=1, tiled=True).reshape(PANEL, width)  15.1 us
    pallas_call x1, Pallas kernels, factor(): pl.pallas_call(factor_kernel, out_shape=[full, vec, vec], scratch_shapes=...  10.9 us
    all_gather x1, blocking collectives, local(): points = lax.all_gather(features[0, 0], 'row', axis=0)[:PANEL // tile]  10.2 us
    ppermute x3, starting transfers between devices, send(): return lax.ppermute(value, ('row', 'col'), pairs)  9.76 us
  transfers between devices with their start and end apart: 4, of which 3 were waited for; matrix products, arithmetic and copies ran while one was open for 1% of the time, Pallas kernels for 9%

commit v1 on v0

v1 whole, which is shorter than its diff:
```python
import functools

import jax
import jax.numpy as jnp
from jax import lax
from jax.experimental import pallas as pl
from jax.experimental.pallas import tpu as pltpu
from jax.sharding import PartitionSpec as P

F = 512
PANEL = 256
TILE = 128
RIDGE = 1.0
EPS = 1e-6

PV = (-2.265364170074463, -4.70527982711792, 7.536093711853027,
      0.7343835830688477, -1.7677195072174072, 0.3254770040512085)
QV = (1.8269329071044922, 3.1679749488830566, -4.871670722961426,
      0.626383364200592, 0.07849788665771484)
TINY = 1e-30
NT = (((1,), (1,)), ((), ()))
VMEM_LIMIT = 60 * 2**20


def dot_nt(a, b):
    return lax.dot_general(a, b, NT, preferred_element_type=jnp.float32)


def dot_hi(a, b, dims):
    return lax.dot_general(
        a, b, (dims, ((), ())), precision=lax.Precision.HIGHEST,
        preferred_element_type=jnp.float32,
    )


def horner(x, coefs):
    acc = coefs[-1]
    for c in coefs[-2::-1]:
        acc = acc * x + c
    return acc


def two_layers(rho):
    a = jnp.maximum(1.0 - rho, TINY)
    b = jnp.maximum(1.0 + rho, TINY)
    u = a * lax.rsqrt(a)
    v = b * lax.rsqrt(b)
    return horner(v, PV) + u * horner(v, QV)


def norm_rows(x):
    xf = x.astype(jnp.float32)
    return jnp.sum(xf * xf, axis=1, keepdims=True) / F


def norm_lanes(x):
    xf = x.astype(jnp.float32)
    sq = xf * xf
    hi = sq.astype(jnp.bfloat16)
    lo = (sq - hi.astype(jnp.float32)).astype(jnp.bfloat16)
    ones = jnp.ones((8, x.shape[1]), jnp.bfloat16)
    return (dot_nt(ones, hi) + dot_nt(ones, lo)) / F


def eye(n):
    return lax.broadcasted_iota(jnp.int32, (n, n), 0) == lax.broadcasted_iota(
        jnp.int32, (n, n), 1
    )


def eliminate(w_ref, t_ref):
    n = TILE
    sub = lax.broadcasted_iota(jnp.int32, (8, n), 0)
    for p in range(0, n, 8):
        a8 = w_ref[p : p + 8, :n]
        e8 = w_ref[p : p + 8, n:]
        cols = [jnp.broadcast_to(a8[:, p + k : p + k + 1], (8, n)) for k in range(8)]
        root = jnp.ones((8, n), jnp.float32)
        invs, ups = [], []
        for k in range(8):
            piv = cols[k][k : k + 1, :]
            inv = 1.0 / piv
            m = jnp.where(sub > k, cols[k] * inv, 0.0)
            ak, ek = a8[k : k + 1, :], e8[k : k + 1, :]
            up = [cols[j][k : k + 1, :] for j in range(k + 1, 8)]
            for j in range(k + 1, 8):
                cols[j] = cols[j] - m * up[j - k - 1]
            a8 = a8 - m * ak
            e8 = e8 - m * ek
            root = jnp.where(sub == k, lax.rsqrt(piv), root)
            invs.append(inv)
            ups.append((ak, ek, up))
        t_ref[p : p + 8, :] = e8 * root
        for g in range(p + 8, n, 8):
            a = w_ref[g : g + 8, :n]
            e = w_ref[g : g + 8, n:]
            cs = [jnp.broadcast_to(a[:, p + k : p + k + 1], (8, n)) for k in range(8)]
            for k in range(8):
                ak, ek, up = ups[k]
                m = cs[k] * invs[k]
                for j in range(k + 1, 8):
                    cs[j] = cs[j] - m * up[j - k - 1]
                a = a - m * ak
                e = e - m * ek
            w_ref[g : g + 8, :n] = a
            w_ref[g : g + 8, n:] = e


def factor_kernel(x_ref, t_ref, sp_ref, bp_ref, k_ref, w_ref, t1_ref, t2_ref):
    x = x_ref[...]
    gq_l = norm_lanes(x)
    s_l = jnp.sqrt(gq_l + EPS)
    b_l = 1.0 / s_l
    sp_ref[...] = s_l
    bp_ref[...] = b_l
    gq = norm_rows(x)
    s = jnp.sqrt(gq + EPS)
    rho = dot_nt(x, x) * ((1.0 / F) / s) * b_l[0:1, :]
    k = two_layers(rho) * (s * s_l[0:1, :])
    k_ref[...] = jnp.where(eye(PANEL), 3.0 * gq + (2.0 * EPS + RIDGE), k)
    h = PANEL // 2
    ident = jnp.where(eye(h), 1.0, 0.0)
    w_ref[:, :h] = k_ref[:h, :h]
    w_ref[:, h:] = ident
    eliminate(w_ref, t1_ref)
    t1 = t1_ref[...]
    l21 = dot_hi(k_ref[h:, :h], t1, ((1,), (1,)))
    w_ref[:, :h] = k_ref[h:, h:] - dot_hi(l21, l21, ((1,), (1,)))
    w_ref[:, h:] = ident
    eliminate(w_ref, t2_ref)
    t2 = t2_ref[...]
    t_ref[:h, :h] = t1
    t_ref[:h, h:] = jnp.zeros((h, h), jnp.float32)
    t_ref[h:, :h] = -dot_hi(t2, dot_hi(l21, t1, ((1,), (0,))), ((1,), (0,)))
    t_ref[h:, h:] = t2


def factor(points):
    full = jax.ShapeDtypeStruct((PANEL, PANEL), jnp.float32)
    vec = jax.ShapeDtypeStruct((8, PANEL), jnp.float32)
    return pl.pallas_call(
        factor_kernel,
        out_shape=[full, vec, vec],
        scratch_shapes=[
            pltpu.VMEM((PANEL, PANEL), jnp.float32),
            pltpu.VMEM((TILE, 2 * TILE), jnp.float32),
            pltpu.VMEM((TILE, TILE), jnp.float32),
            pltpu.VMEM((TILE, TILE), jnp.float32),
        ],
        compiler_params=pltpu.CompilerParams(vmem_limit_bytes=VMEM_LIMIT),
        cost_estimate=pl.CostEstimate(flops=10**9, bytes_accessed=10**7, transcendentals=0),
        name="factor",
    )(points)


def panel_block(x, pts, sp, bp, k_ref):
    gq = norm_rows(x)
    s = jnp.sqrt(gq + EPS)
    a = (1.0 / F) / s
    k_ref[...] = dot_nt(x, pts)
    for g in range(0, x.shape[0], 16):
        rows = slice(g, g + 16)
        rho = k_ref[rows, :] * a[rows, :] * bp
        k_ref[rows, :] = two_layers(rho) * (s[rows, :] * sp)
    return s, a, 3.0 * gq + (2.0 * EPS + RIDGE)


def set_diagonal(k_ref, diag, hit):
    for half in range(PANEL // TILE):

        @pl.when(hit == half)
        def _():
            cols = slice(half * TILE, (half + 1) * TILE)
            k_ref[:TILE, cols] = jnp.where(eye(TILE), diag[:TILE, :], k_ref[:TILE, cols])


def split(low):
    hi = low.astype(jnp.bfloat16)
    return hi, (low - hi.astype(jnp.float32)).astype(jnp.bfloat16)


def panel_kernel(tau_ref, x_ref, pts_ref, t_ref, sp_ref, bp_ref,
                 l_ref, cat_ref, s_ref, a_ref, d_ref, k_ref):
    s, a, diag = panel_block(x_ref[...], pts_ref[...], sp_ref[0:1, :], bp_ref[0:1, :], k_ref)
    set_diagonal(k_ref, diag, jnp.where(pl.program_id(0) == 0, tau_ref[0], -1))
    low = dot_hi(k_ref[...], t_ref[...], ((1,), (1,)))
    hi, lo = split(low)
    l_ref[...] = low
    cat_ref[:, :PANEL] = hi
    cat_ref[:, PANEL : 2 * PANEL] = hi
    cat_ref[:, 2 * PANEL :] = lo
    s_ref[...] = jnp.broadcast_to(s, s_ref.shape)
    a_ref[...] = jnp.broadcast_to(a, a_ref.shape)
    left = diag - jnp.sum(low * low, axis=1, keepdims=True)
    d_ref[...] = jnp.broadcast_to(left, d_ref.shape)


def pick(total, options):
    for o in options:
        if total % o == 0:
            return o
    return total


def panel_rows(x, points, t, sp, bp, tau):
    m = x.shape[0]
    block = pick(m, (512, 384, 256, 128))
    const = lambda shape: pl.BlockSpec(shape, lambda i: (0, 0))
    by_row = lambda width: pl.BlockSpec((block, width), lambda i: (i, 0))
    f32 = lambda *shape: jax.ShapeDtypeStruct(shape, jnp.float32)
    return pl.pallas_call(
        panel_kernel,
        grid=(m // block,),
        in_specs=[
            pl.BlockSpec(memory_space=pltpu.SMEM),
            by_row(F), const((PANEL, F)), const((PANEL, PANEL)),
            const((8, PANEL)), const((8, PANEL)),
        ],
        out_specs=[by_row(PANEL), by_row(3 * PANEL)] + [by_row(128)] * 3,
        out_shape=[f32(m, PANEL), jax.ShapeDtypeStruct((m, 3 * PANEL), jnp.bfloat16),
                   f32(m, 128), f32(m, 128), f32(m, 128)],
        scratch_shapes=[pltpu.VMEM((block, PANEL), jnp.float32)],
        compiler_params=pltpu.CompilerParams(vmem_limit_bytes=VMEM_LIMIT),
        cost_estimate=pl.CostEstimate(
            flops=2 * m * PANEL * (F + 6 * PANEL), bytes_accessed=m * 4096, transcendentals=0
        ),
        name="panel_rows",
    )(tau, x, points, t, sp, bp)


def trailing_kernel(rb, tb, blocks, steps, step_tiles, fold, arrays, info, *refs):
    mine, got, refs = refs[:arrays], refs[arrays : 2 * arrays], refs[2 * arrays :]
    pts, t_ref, sp_ref, bp_ref, xr, xr_next, lr, lr_next, sr, ar, dr = refs[:11]
    out, xc, lc, sc, bc, k_ref, ga, ma, gb, mb, sem = refs[-11:]
    if fold:
        out = out.reshape(rb * tb, TILE)
    q = pl.program_id(0)
    i, j = q // blocks, q % blocks
    cb = tb * TILE // 2
    per = cb // TILE

    def load(arrays):
        moves = []
        for k, src in enumerate(arrays):
            group, entry = k // step_tiles, k % step_tiles
            part = info[4] ^ entry
            width = src.shape[1]

            def move(tile):
                at = (tile * step_tiles + part) * TILE + info[5 + group] * width
                to = pl.ds(pl.multiple_of(at, width), width)
                return pltpu.make_async_copy(src.at[tile], xc.at[to], sem)

            for tile in range(src.shape[0]):
                moves.append(move(tile))
        for m in moves:
            m.start()
        for m in moves:
            m.wait()

    def columns(b):
        size = k_ref.shape[0]
        rows = pl.ds(pl.multiple_of(b * size, size), size)
        s, _, diag = panel_block(xc[rows, :], pts[...], sp_ref[0:1, :], bp_ref[0:1, :], k_ref)
        set_diagonal(k_ref, diag, jnp.where(b == 0, info[2], -1))
        hi, lo = split(dot_hi(k_ref[...], t_ref[...], ((1,), (1,))))
        lc[rows, :PANEL] = hi
        lc[rows, PANEL : 2 * PANEL] = lo
        lc[rows, 2 * PANEL :] = hi
        for g in range(0, size, TILE):
            wide = jnp.broadcast_to(s[g : g + TILE, :], (TILE, TILE)).T[0:8, :]
            lanes = pl.ds(pl.multiple_of(b * size + g, TILE), TILE)
            sc[:, lanes] = wide
            bc[:, lanes] = 1.0 / wide

    def multiply(x, l, col, g, m):
        cols = pl.ds(pl.multiple_of(col, cb), cb)
        g[...] = dot_nt(x[...], xc[cols, :])
        m[...] = dot_nt(l[...], lc[cols, :])

    def finish(half, g, m):
        for tile in range(per):
            lanes = pl.ds(pl.multiple_of(j * (tb * TILE) + half * cb + tile * TILE, TILE), TILE)
            s_col = sc[0:1, lanes]
            b_col = bc[0:1, lanes]
            here = slice(tile * TILE, (tile + 1) * TILE)
            for k in range(0, rb, 16):
                rows = slice(k, k + 16)
                rho = g[rows, here] * ar[rows, :] * b_col
                val = two_layers(rho) * (sr[rows, :] * s_col) - m[rows, here]
                out[pl.ds(k * tb + half * per + tile, 16, stride=tb), :] = val

    @pl.when(q == 0)
    def _():
        @pl.when(info[3] == 0)
        def _():
            load(mine)

        @pl.when(info[3] != 0)
        def _():
            load(got)

        @pl.loop(0, xc.shape[0] // k_ref.shape[0])
        def _(b):
            columns(b)

        multiply(xr, lr, 0, ga, ma)

    multiply(xr, lr, j * (tb * TILE) + cb, gb, mb)
    finish(0, ga, ma)
    after = jnp.minimum(q + 1, steps - 1) % blocks
    multiply(xr_next, lr_next, after * (tb * TILE), ga, ma)
    finish(1, gb, mb)

    for tile in range(rb // TILE):
        col = (i * (rb // TILE) + tile) * step_tiles + info[1] - j * tb

        @pl.when((info[0] == 1) & (col >= 0) & (col < tb))
        def _():
            for k in range(0, TILE, 16):
                rows = slice(tile * TILE + k, tile * TILE + k + 16)
                same = lax.broadcasted_iota(jnp.int32, (16, TILE), 1) == (
                    lax.broadcasted_iota(jnp.int32, (16, TILE), 0) + k
                )
                at = pl.ds((tile * TILE + k) * tb + col, 16, stride=tb)
                out[at, :] = jnp.where(same, dr[rows, :], out[at, :])


def trailing(row_args, mine, got, panel_args, info, step_tiles):
    x_rows, cat_rows, s, a, d = row_args
    m = x_rows.shape[0]
    tiles_c = m // TILE * step_tiles
    n = tiles_c * TILE
    fold = tiles_c % 8 == 0
    tb = 8 if fold else tiles_c
    rb = pick(m, (512, 384, 256, 128))
    cb = tb * TILE // 2
    blocks = n // (tb * TILE)
    steps = m // rb * blocks
    const = lambda shape: pl.BlockSpec(shape, lambda q: (0, 0))
    cur = lambda width: pl.BlockSpec((rb, width), lambda q: (q // blocks, 0))
    nxt = lambda width: pl.BlockSpec(
        (rb, width), lambda q: (jnp.minimum(q + 1, steps - 1) // blocks, 0)
    )
    hbm = pl.BlockSpec(memory_space=pl.ANY)
    if fold:
        shape = (m, tiles_c, TILE)
        spec = pl.BlockSpec((rb, tb, TILE), lambda q: (q // blocks, q % blocks, 0))
    else:
        shape = (m * tb, TILE)
        spec = pl.BlockSpec((rb * tb, TILE), lambda q: (q, 0))
    square = pltpu.VMEM((rb, cb), jnp.float32)
    return pl.pallas_call(
        functools.partial(
            trailing_kernel, rb, tb, blocks, steps, step_tiles, fold, len(mine)
        ),
        grid=(steps,),
        in_specs=[pl.BlockSpec(memory_space=pltpu.SMEM)] + [hbm] * (2 * len(mine)) + [
            const((PANEL, F)), const((PANEL, PANEL)), const((8, PANEL)), const((8, PANEL)),
            cur(F), nxt(F), cur(3 * PANEL), nxt(3 * PANEL), cur(128), cur(128), cur(128),
        ],
        out_specs=spec,
        out_shape=jax.ShapeDtypeStruct(shape, jnp.float32),
        scratch_shapes=[
            pltpu.VMEM((n, F), jnp.bfloat16),
            pltpu.VMEM((n, 3 * PANEL), jnp.bfloat16),
            pltpu.VMEM((8, n), jnp.float32),
            pltpu.VMEM((8, n), jnp.float32),
            pltpu.VMEM((pick(n, (512, 384, 256, 128)), PANEL), jnp.float32),
            square, square, square, square,
            pltpu.SemaphoreType.DMA,
        ],
        compiler_params=pltpu.CompilerParams(vmem_limit_bytes=VMEM_LIMIT),
        cost_estimate=pl.CostEstimate(
            flops=2 * m * n * (F + 3 * PANEL), bytes_accessed=m * n * 4, transcendentals=0
        ),
        name="trailing",
    )(info, *mine, *got, *panel_args, x_rows, x_rows, cat_rows, cat_rows, s, a, d)


class Grid:
    def __init__(self):
        self.n_row, self.n_col = lax.axis_size("row"), lax.axis_size("col")
        self.r, self.c = lax.axis_index("row"), lax.axis_index("col")
        self.low = self.n_col.bit_length() - 1
        self.high = self.n_row.bit_length() - 1

    def send(self, value, move):
        pairs = []
        for i in range(self.n_row):
            for j in range(self.n_col):
                to = move(i, j)
                if to is not None:
                    pairs.append((i * self.n_col + j, to[0] * self.n_col + to[1]))
        return lax.ppermute(value, ("row", "col"), pairs)

    def flip(self, value, bit, holds):
        return self.send(value, lambda i, j: (i ^ (1 << bit), j) if holds(i, j) else None)

    def turn(self, value, by, holds=lambda i, j: True):
        return self.send(value, lambda i, j: (i, (j + by) % self.n_col) if holds(i, j) else None)

    def in_order(self, own, before, after, across):
        parts = []
        for t in range(4):
            away = (t - self.c) % 4
            parts.append(jnp.where(away == 0, own, jnp.where(away == 3, before,
                         jnp.where(away == 1, after, across))))
        return jnp.concatenate(parts, axis=-2)

    def gather_rows(self, x, count):
        has = lambda i, j: i < count
        if self.n_col != 4:
            full = lax.all_gather(x, "col", axis=1, tiled=True)
            return full, [full], [jnp.int32(0)], self.share(full[0], count)
        before = self.turn(x, 1)
        after = self.turn(x, -1)
        tile = self.in_order(x[0], before[0], after[0], self.turn(x[0], 2, has))
        points = self.share(tile, count)
        across = self.turn(before, 1)
        places = [self.c, (self.c - 1) % 4, (self.c + 1) % 4, (self.c + 2) % 4]
        return self.in_order(x, before, after, across), [x, before, after, across], places, points

    def share(self, data, count):
        bits = count.bit_length() - 1
        for bit in range(self.high - 1, bits - 1, -1):
            got = self.flip(data, bit, lambda i, j: i & ~(count - 1) & ((2 << bit) - 1) == 0)
            data = jnp.where((self.r >> bit) & 1 == 0, data, got)
        data = data[None]
        for bit in range(bits):
            got = self.flip(data, bit, lambda i, j: True)
            first = (self.r >> bit) & 1 == 0
            data = jnp.concatenate([jnp.where(first, data, got), jnp.where(first, got, data)])
        return data

    def spread(self, data):
        mask = self.n_col - 1
        for bit in range(self.low - 1, 0, -1):
            got = self.flip(data, bit, lambda i, j: (i ^ j) & mask == 0)
            data = jnp.where((self.r ^ self.c) & (1 << bit) == 0, data, got)
            mask &= ~(1 << bit)
        parts = [data]
        for bit in range(self.low, self.high):
            parts += [self.flip(p, bit, lambda i, j: (i ^ j) & mask == 0) for p in parts]
        return parts, [self.flip(p, 0, lambda i, j: (i ^ j) & 1 == 0) for p in parts]


def local(features):
    grid = Grid()
    r, c = grid.r, grid.c
    tiles_r, _, thin, width = features.shape
    step_tiles = grid.n_row // grid.n_col
    tiles_c = tiles_r * step_tiles
    tile = thin * grid.n_col

    rows, pieces, places, points = grid.gather_rows(features[:, 0], PANEL // tile)
    points = points.reshape(PANEL, width)
    t, sp, bp = factor(points)
    panel_args = (points, t, sp, bp)
    mine, got = [], []
    for piece in pieces:
        here, there = grid.spread(piece)
        mine += here
        got += there

    tau = lambda i: jnp.where(i < PANEL // tile, i, -1)
    x_rows = rows.reshape(tiles_r * tile, width)
    low, *row_args = panel_rows(x_rows, *panel_args, tau(r).astype(jnp.int32).reshape(1))
    info = jnp.stack(
        [(r - c) % grid.n_col == 0, (r - c) // grid.n_col, tau(c), (r ^ c) & 1, r // grid.n_col]
        + places
    ).astype(jnp.int32)
    out = trailing((x_rows, *row_args), mine, got, panel_args, info, step_tiles)
    return (
        low.reshape(tiles_r, 1, tile, PANEL),
        out.reshape(tiles_r, 1, tile, tiles_c, 1, tile),
    )


def solution(mesh):
    return jax.shard_map(
        local,
        mesh=mesh,
        in_specs=(P(None, "row", "col", None),),
        out_specs=(P(None, "row", None, None), P(None, "row", None, None, "col", None)),
        check_vma=False,
    )
```

time: 209 us -> 139 us (0.67)
  waiting for transfers between devices: 79.3 us -> 15.1 us
  starting transfers between devices: 9.8 us -> 48.1 us
  blocking collectives: 25.3 us -> 0 us
  between operations: 14.1 us -> 1.31 us
  Pallas kernels: 70.6 us -> 64.3 us
    all_gather x1 -> x0, waiting for transfers between devices: 41.5 us -> none  [local(): lax.all_gather(features, 'col', axis=2, tiled=True)]
    ppermute x3 -> x23, starting transfers between devices: 9.76 us -> 48.1 us  [send(): return lax.ppermute(value, ('row', 'col'), pairs)]
    all_gather x2 -> x0, blocking collectives: 25.3 us -> none  [the longest x1 15.1 us: local(): lax.all_gather(points, 'col', axis=1, tiled=True).reshape(PANEL, width)]
    ppermute x3 -> x23, waiting for transfers between devices: 37.1 us -> 15.1 us  [send(): return lax.ppermute(value, ('row', 'col'), pairs)]
    pallas_call x3 -> x2, Pallas kernels: 59.7 us -> 53.4 us  [the longest x1 45.2 us: trailing(): pl.pallas_call(functools.partial(trailing_kernel, rb, tb, blocks, steps,...]
    select_n x1 -> x7, other arithmetic: 2.09 us -> 4.58 us  [the longest x3 2.64 us: in_order(): jnp.where(away == 0, own, jnp.where(away == 3, before, jnp.where(away ==...]
  transfers between devices with their start and end apart: 4 -> 23, of which waited for: 3 -> 6; matrix products, arithmetic and copies ran while one was open for 1% -> 6% of each run, Pallas kernels for 9% -> 14%
where the time goes in v1:
time: 139 us; the launch traced here: 138 us
  Pallas kernels  64.3 us (46%)
  starting transfers between devices  48.1 us (35%)
  waiting for transfers between devices  15.1 us (11%)
  other arithmetic  6.7 us (5%)
  local copies, waits for them, and re-layouts  2.47 us (2%)
    ppermute x23, starting transfers between devices, send(): return lax.ppermute(value, ('row', 'col'), pairs)  48.1 us
    pallas_call x1, Pallas kernels, trailing(): pl.pallas_call(functools.partial(trailing_kernel, rb, tb, blocks, steps,...  45.2 us
    ppermute x23, waiting for transfers between devices, send(): return lax.ppermute(value, ('row', 'col'), pairs)  15.1 us
    pallas_call x1, Pallas kernels, factor(): pl.pallas_call(factor_kernel, out_shape=[full, vec, vec], scratch_shapes=...  10.9 us
    pallas_call x1, Pallas kernels, panel_rows(): pl.pallas_call(panel_kernel, grid=(m // block,), in_specs=[pl.BlockSpec(m...  8.18 us
  transfers between devices with their start and end apart: 23, of which 6 were waited for; matrix products, arithmetic and copies ran while one was open for 6% of the time, Pallas kernels for 14%

profile of v1, /device:TPU:0, one launch (start us, length us, event | category | flops | bytes accessed | tf_op | source)
XLA Modules:
  0.0 138.0 jit_solution(17172211759150426991)
XLA Ops:
  0.6 0.0 copy-start
  0.6 5.1 %collective-permute-start.1 = (bf16[12,32,512]{2,1,0:T(8,128)(2,1)}, bf16[12,32,512]{2,1,0:T(8,128)(2,1)S(1)}, u32[]{:S(2)}, u32[]{:S(2)}) collective-permute-start(bf16[12,32,512]{2,1,0:T(8,128)(2,1)} %bitcast.56), channel_id=1, source_target_pairs={{0,3},{1,0},{2,1},{3,2},{4,7},{5,4},{6,5},{7,6},{8,11},{9,8},{10,9... | collective-permute-start | bytes 1179656 | tf_op jit(solution)/shard_map/ppermute | solution.py:395
  5.7 0.0 collective-permute-start
  5.7 0.8 slice_bitcast_fusion.2
  6.6 2.9 %collective-permute-start.3 = (bf16[32,512]{1,0:T(8,128)(2,1)S(1)}, bf16[32,512]{1,0:T(8,128)(2,1)S(1)}, u32[]{:S(2)}, u32[]{:S(2)}) collective-permute-start(bf16[32,512]{1,0:T(8,128)(2,1)S(1)} %slice_bitcast_fusion.2), channel_id=1, source_target_pairs={{0,2},{1,3},{2,0},{3,1},{4,6},{5,7},{6,4},{7,5}} | collective-permute-start | bytes 98312 | tf_op jit(solution)/shard_map/ppermute | solution.py:395
  9.5 1.3 collective-permute-start.7
  10.9 12.6 %collective-permute-done.3 = bf16[32,512]{1,0:T(8,128)(2,1)S(1)} collective-permute-done((bf16[32,512]{1,0:T(8,128)(2,1)S(1)}, bf16[32,512]{1,0:T(8,128)(2,1)S(1)}, u32[]{:S(2)}, u32[]{:S(2)}) %collective-permute-start.3) | collective-permute-done | bytes 32800 | tf_op jit(solution)/shard_map/ppermute | solution.py:395
  23.5 0.0 collective-permute-done.1
  23.5 0.5 collective-permute-done
  24.0 0.8 select_select_fusion.6
  24.8 0.8 select_select_fusion.7
  25.6 3.1 %collective-permute-start.4 = (bf16[128,512]{1,0:T(8,128)(2,1)S(1)}, bf16[128,512]{1,0:T(8,128)(2,1)S(1)}, u32[]{:S(2)}, u32[]{:S(2)}) collective-permute-start(bf16[128,512]{1,0:T(8,128)(2,1)S(1)} %pad_maximum_fusion.2), channel_id=1, source_target_pairs={{0,16},{1,17},{2,18},{3,19},{4,20},{5,21},{6,22},{7,23}} | collective-permute-start | bytes 393224 | tf_op jit(solution)/shard_map/ppermute | solution.py:395
  28.7 1.3 collective-permute-start.9
  30.0 1.0 collective-permute-start.2
  31.1 0.1 collective-permute-done.4
  31.2 1.3 collective-permute-start.5
  32.5 0.0 collective-permute-done.7
  32.5 1.0 broadcast_select_fusion.3.refs_0_
  33.6 1.3 collective-permute-start.15
  34.9 4.4 %collective-permute-start.8 = (bf16[12,32,512]{2,1,0:T(8,128)(2,1)S(1)}, bf16[12,32,512]{2,1,0:T(8,128)(2,1)}, u32[]{:S(2)}, u32[]{:S(2)}) collective-permute-start(bf16[12,32,512]{2,1,0:T(8,128)(2,1)S(1)} %broadcast_select_fusion.3.refs_0_), channel_id=1, source_target_pairs={{0,16},{2,18},{5,21},{7,23},{8,24},{10,26},{13,29},{15,31},{16,0},... | collective-permute-start | bytes 1179656 | tf_op jit(solution)/shard_map/ppermute | solution.py:395
  39.3 0.0 collective-permute-done.5
  39.3 3.2 %collective-permute-start.11 = (bf16[12,32,512]{2,1,0:T(8,128)(2,1)S(1)}, bf16[12,32,512]{2,1,0:T(8,128)(2,1)S(1)}, u32[]{:S(2)}, u32[]{:S(2)}) collective-permute-start(bf16[12,32,512]{2,1,0:T(8,128)(2,1)S(1)} %collective-permute-done.1), channel_id=1, source_target_pairs={{0,8},{5,13},{10,2},{15,7},{16,24},{21,29},{26,18},{31,23}} | collective-permute-start | bytes 1179656 | tf_op jit(solution)/shard_map/ppermute | solution.py:395
  42.5 0.0 collective-permute-done.2
  42.5 1.3 collective-permute-start.13
  43.8 0.0 collective-permute-done.9
  43.8 0.1 collective-permute-start.6
  43.9 0.8 broadcast_select_fusion.2.refs_2_
  44.8 0.3 collective-permute-done.8.refs_1_
  45.1 2.8 %collective-permute-start.17 = (bf16[12,32,512]{2,1,0:T(8,128)(2,1)}, bf16[12,32,512]{2,1,0:T(8,128)(2,1)}, u32[]{:S(2)}, u32[]{:S(2)}) collective-permute-start(bf16[12,32,512]{2,1,0:T(8,128)(2,1)} %broadcast_select_fusion.2.refs_2_), channel_id=1, source_target_pairs={{0,4},{2,6},{5,1},{7,3},{8,12},{10,14},{13,9},{15,11},{16,20},{18,... | collective-permute-start | bytes 1179656 | tf_op jit(solution)/shard_map/ppermute | solution.py:395
  47.9 0.0 collective-permute-done.11
  47.9 3.1 %collective-permute-start.10 = (bf16[12,32,512]{2,1,0:T(8,128)(2,1)}, bf16[12,32,512]{2,1,0:T(8,128)(2,1)}, u32[]{:S(2)}, u32[]{:S(2)}) collective-permute-start(bf16[12,32,512]{2,1,0:T(8,128)(2,1)} %broadcast_select_fusion.2.refs_2_), channel_id=1, source_target_pairs={{0,16},{2,18},{5,21},{7,23},{8,24},{10,26},{13,29},{15,31},{16,0},... | collective-permute-start | bytes 1179656 | tf_op jit(solution)/shard_map/ppermute | solution.py:395
  51.1 0.9 collective-permute-done.13
  51.9 2.0 %collective-permute-start.16 = (bf16[12,32,512]{2,1,0:T(8,128)(2,1)}, bf16[12,32,512]{2,1,0:T(8,128)(2,1)}, u32[]{:S(2)}, u32[]{:S(2)}) collective-permute-start(bf16[12,32,512]{2,1,0:T(8,128)(2,1)} %collective-permute-done.8.refs_1_), channel_id=1, source_target_pairs={{0,4},{2,6},{5,1},{7,3},{8,12},{10,14},{13,9},{15,11},{16,20},{18,... | collective-permute-start | bytes 1179656 | tf_op jit(solution)/shard_map/ppermute | solution.py:395
  54.0 0.0 copy-done
  54.0 1.1 select_select_fusion.3
  55.1 0.0 collective-permute-done.15.refs_8_
  55.1 2.8 %collective-permute-start.14 = (bf16[12,32,512]{2,1,0:T(8,128)(2,1)}, bf16[12,32,512]{2,1,0:T(8,128)(2,1)S(1)}, u32[]{:S(2)}, u32[]{:S(2)}) collective-permute-start(bf16[12,32,512]{2,1,0:T(8,128)(2,1)} %get-tuple-element.27.refs_6_), channel_id=1, source_target_pairs={{0,16},{2,18},{5,21},{7,23},{8,24},{10,26},{13,29},{15,31},{16,0},... | collective-permute-start | bytes 1179656 | tf_op jit(solution)/shard_map/ppermute | solution.py:395
  57.9 0.0 collective-permute-done.6
  57.9 3.1 %collective-permute-start.12 = (bf16[12,32,512]{2,1,0:T(8,128)(2,1)}, bf16[12,32,512]{2,1,0:T(8,128)(2,1)S(1)}, u32[]{:S(2)}, u32[]{:S(2)}) collective-permute-start(bf16[12,32,512]{2,1,0:T(8,128)(2,1)} %get-tuple-element.28.refs_4_), channel_id=1, source_target_pairs={{0,16},{2,18},{5,21},{7,23},{8,24},{10,26},{13,29},{15,31},{16,0},... | collective-permute-start | bytes 1179656 | tf_op jit(solution)/shard_map/ppermute | solution.py:395
  61.0 0.7 stack.43.info
  61.7 0.7 pad_maximum_fusion.1
  62.5 0.0 collective-permute-done.16.refs_9_
  62.5 1.3 collective-permute-start.21
  63.8 0.0 collective-permute-done.17.refs_10_
  63.8 1.3 collective-permute-start.19
  65.1 0.0 collective-permute-done.10.refs_3_
  65.1 1.3 collective-permute-start.18
  66.5 0.0 collective-permute-done.14.refs_7_
  66.5 2.1 %collective-permute-start.22 = (bf16[12,32,512]{2,1,0:T(8,128)(2,1)S(1)}, bf16[12,32,512]{2,1,0:T(8,128)(2,1)}, u32[]{:S(2)}, u32[]{:S(2)}) collective-permute-start(bf16[12,32,512]{2,1,0:T(8,128)(2,1)S(1)} %collective-permute-done.14.refs_7_), channel_id=1, source_target_pairs={{0,4},{2,6},{5,1},{7,3},{8,12},{10,14},{13,9},{15,11},{16,20},{18,... | collective-permute-start | bytes 1179656 | tf_op jit(solution)/shard_map/ppermute | solution.py:395
  68.6 0.6 collective-permute-done.12.refs_5_
  69.2 2.0 %collective-permute-start.20 = (bf16[12,32,512]{2,1,0:T(8,128)(2,1)S(1)}, bf16[12,32,512]{2,1,0:T(8,128)(2,1)}, u32[]{:S(2)}, u32[]{:S(2)}) collective-permute-start(bf16[12,32,512]{2,1,0:T(8,128)(2,1)S(1)} %collective-permute-done.12.refs_5_), channel_id=1, source_target_pairs={{0,4},{2,6},{5,1},{7,3},{8,12},{10,14},{13,9},{15,11},{16,20},{18,... | collective-permute-start | bytes 1179656 | tf_op jit(solution)/shard_map/ppermute | solution.py:395
  71.2 10.9 %factor.1 = (f32[256,256]{1,0:T(8,128)}, f32[8,256]{1,0:T(8,128)}, f32[8,256]{1,0:T(8,128)}) custom-call(bf16[256,512]{1,0:T(8,128)(2,1)} %bitcast.62), custom_call_target="tpu_custom_call" | custom-call | flops 1000000000 | bytes 10000000 | tf_op jit(solution)/shard_map/factor/pallas_call | solution.py:141
  82.1 1.3 pad_maximum_fusion
  83.5 8.2 %panel_rows.1 = (f32[1536,256]{1,0:T(8,128)}, bf16[1536,768]{1,0:T(8,128)(2,1)}, f32[1536,128]{1,0:T(8,128)}, f32[1536,128]{1,0:T(8,128)}, f32[1536,128]{1,0:T(8,128)}) custom-call(s32[1]{0:T(128)} %bitcast.tau_ref, bf16[1536,512]{1,0:T(8,128)(2,1)} %bitcast.59, bf16[256,512]{1,0:T(8,128)(2,1)} %bitcast.63, f32[256,256]{1,0:T(8,128)} %get-tuple-element.10.t_ref.refs_17_, ...), custom_call_target="tpu_custom_call" | custom-call | flops 1610612736 | bytes 6291456 | tf_op jit(solution)/shard_map/panel_rows/pallas_call | solution.py:211
  91.6 0.0 collective-permute-done.18.refs_11_
  91.6 0.0 copy-start.7
  91.7 0.0 collective-permute-done.21.refs_14_
  91.7 0.0 collective-permute-done.19.refs_12_
  91.7 0.0 collective-permute-done.22.refs_15_
  91.7 0.0 collective-permute-done.20.refs_13_
  91.7 0.7 copy-done.7
  92.4 0.1 copy-done.5
  92.5 0.1 copy-done.6
  92.7 45.2 %trailing.1 = f32[1536,24,128]{2,1,0:T(8,128)} custom-call(s32[9]{0:T(128)} %stack.43.info, bf16[12,32,512]{2,1,0:T(8,128)(2,1)} %copy-done.1, bf16[12,32,512]{2,1,0:T(8,128)(2,1)} %collective-permute-done.8.refs_1_, bf16[12,32,512]{2,1,0:T(8,128)(2,1)} %broadcast_select_fusion.2.refs_2_, bf16[12,32,512]{2,1,0:T(8,128)(2,1)} %collective-permute-done.10.refs_3_, ...), custom_call_target="tpu_custom_call" | custom-call | flops 12079595520 | bytes 18874368 | tf_op jit(solution)/shard_map/trailing/pallas_call | solution.py:353
  (14 shorter events, 0.1 us)
Async XLA Ops:
  0.6 53.4 %copy-start = (bf16[12,1,32,512]{3,2,1,0:T(8,128)(2,1)S(1)}, bf16[12,1,32,512]{3,2,1,0:T(8,128)(2,1)}, u32[]{:S(2)}) copy-start(bf16[12,1,32,512]{3,2,1,0:T(8,128)(2,1)} %param.1) | copy-start | bytes 1179652
  0.6 22.9 %collective-permute-start.1 = (bf16[12,32,512]{2,1,0:T(8,128)(2,1)}, bf16[12,32,512]{2,1,0:T(8,128)(2,1)S(1)}, u32[]{:S(2)}, u32[]{:S(2)}) collective-permute-start(bf16[12,32,512]{2,1,0:T(8,128)(2,1)} %bitcast.56), channel_id=1, source_target_pairs={{0,3},{1,0},{2,1},{3,2},{4,7},{5,4},{6,5},{7,6},{8,11},{9,8},{10,9... | collective-permute-start | bytes 1179656 | tf_op jit(solution)/shard_map/ppermute | solution.py:395
  5.7 18.3 %collective-permute-start = (bf16[12,32,512]{2,1,0:T(8,128)(2,1)}, bf16[12,32,512]{2,1,0:T(8,128)(2,1)S(1)}, u32[]{:S(2)}, u32[]{:S(2)}) collective-permute-start(bf16[12,32,512]{2,1,0:T(8,128)(2,1)} %bitcast.57), channel_id=1, source_target_pairs={{0,1},{1,2},{2,3},{3,0},{4,5},{5,6},{6,7},{7,4},{8,9},{9,10},{10,1... | collective-permute-start | bytes 1179656 | tf_op jit(solution)/shard_map/ppermute | solution.py:395
  6.6 16.9 %collective-permute-start.3 = (bf16[32,512]{1,0:T(8,128)(2,1)S(1)}, bf16[32,512]{1,0:T(8,128)(2,1)S(1)}, u32[]{:S(2)}, u32[]{:S(2)}) collective-permute-start(bf16[32,512]{1,0:T(8,128)(2,1)S(1)} %slice_bitcast_fusion.2), channel_id=1, source_target_pairs={{0,2},{1,3},{2,0},{3,1},{4,6},{5,7},{6,4},{7,5}} | collective-permute-start | bytes 98312 | tf_op jit(solution)/shard_map/ppermute | solution.py:395
  9.5 23.1 %collective-permute-start.7 = (bf16[12,32,512]{2,1,0:T(8,128)(2,1)}, bf16[12,32,512]{2,1,0:T(8,128)(2,1)S(1)}, u32[]{:S(2)}, u32[]{:S(2)}) collective-permute-start(bf16[12,32,512]{2,1,0:T(8,128)(2,1)} %bitcast.58), channel_id=1, source_target_pairs={{0,8},{5,13},{10,2},{15,7},{16,24},{21,29},{26,18},{31,23}} | collective-permute-start | bytes 1179656 | tf_op jit(solution)/shard_map/ppermute | solution.py:395
  25.6 5.6 %collective-permute-start.4 = (bf16[128,512]{1,0:T(8,128)(2,1)S(1)}, bf16[128,512]{1,0:T(8,128)(2,1)S(1)}, u32[]{:S(2)}, u32[]{:S(2)}) collective-permute-start(bf16[128,512]{1,0:T(8,128)(2,1)S(1)} %pad_maximum_fusion.2), channel_id=1, source_target_pairs={{0,16},{1,17},{2,18},{3,19},{4,20},{5,21},{6,22},{7,23}} | collective-permute-start | bytes 393224 | tf_op jit(solution)/shard_map/ppermute | solution.py:395
  28.7 15.2 %collective-permute-start.9 = (bf16[12,32,512]{2,1,0:T(8,128)(2,1)S(1)}, bf16[12,32,512]{2,1,0:T(8,128)(2,1)S(1)}, u32[]{:S(2)}, u32[]{:S(2)}) collective-permute-start(bf16[12,32,512]{2,1,0:T(8,128)(2,1)S(1)} %collective-permute-done), channel_id=1, source_target_pairs={{0,8},{5,13},{10,2},{15,7},{16,24},{21,29},{26,18},{31,23}} | collective-permute-start | bytes 1179656 | tf_op jit(solution)/shard_map/ppermute | solution.py:395
  30.0 12.5 %collective-permute-start.2 = (bf16[12,32,512]{2,1,0:T(8,128)(2,1)S(1)}, bf16[12,32,512]{2,1,0:T(8,128)(2,1)S(1)}, u32[]{:S(2)}, u32[]{:S(2)}) collective-permute-start(bf16[12,32,512]{2,1,0:T(8,128)(2,1)S(1)} %collective-permute-done), channel_id=1, source_target_pairs={{0,1},{1,2},{2,3},{3,0},{4,5},{5,6},{6,7},{7,4},{8,9},{9,10},{10,1... | collective-permute-start | bytes 1179656 | tf_op jit(solution)/shard_map/ppermute | solution.py:395
  31.2 8.1 %collective-permute-start.5 = (bf16[128,512]{1,0:T(8,128)(2,1)S(1)}, bf16[128,512]{1,0:T(8,128)(2,1)S(1)}, u32[]{:S(2)}, u32[]{:S(2)}) collective-permute-start(bf16[128,512]{1,0:T(8,128)(2,1)S(1)} %broadcast_select_fusion.4), channel_id=1, source_target_pairs={{0,8},{1,9},{2,10},{3,11},{4,12},{5,13},{6,14},{7,15},{16,24},{17,... | collective-permute-start | bytes 393224 | tf_op jit(solution)/shard_map/ppermute | solution.py:395
  33.6 21.5 %copy-start.1 = (bf16[12,32,512]{2,1,0:T(8,128)(2,1)}, bf16[12,32,512]{2,1,0:T(8,128)(2,1)S(1)}, u32[]{:S(2)}) copy-start(bf16[12,32,512]{2,1,0:T(8,128)(2,1)S(1)} %broadcast_select_fusion.3.refs_0_) | copy-start | bytes 1179652
  33.6 21.5 %collective-permute-start.15 = (bf16[12,32,512]{2,1,0:T(8,128)(2,1)S(1)}, bf16[12,32,512]{2,1,0:T(8,128)(2,1)S(1)}, u32[]{:S(2)}, u32[]{:S(2)}) collective-permute-start(bf16[12,32,512]{2,1,0:T(8,128)(2,1)S(1)} %broadcast_select_fusion.3.refs_0_), channel_id=1, source_target_pairs={{0,4},{2,6},{5,1},{7,3},{8,12},{10,14},{13,9},{15,11},{16,20},{18,... | collective-permute-start | bytes 1179656 | tf_op jit(solution)/shard_map/ppermute | solution.py:395
  34.9 10.2 %collective-permute-start.8 = (bf16[12,32,512]{2,1,0:T(8,128)(2,1)S(1)}, bf16[12,32,512]{2,1,0:T(8,128)(2,1)}, u32[]{:S(2)}, u32[]{:S(2)}) collective-permute-start(bf16[12,32,512]{2,1,0:T(8,128)(2,1)S(1)} %broadcast_select_fusion.3.refs_0_), channel_id=1, source_target_pairs={{0,16},{2,18},{5,21},{7,23},{8,24},{10,26},{13,29},{15,31},{16,0},... | collective-permute-start | bytes 1179656 | tf_op jit(solution)/shard_map/ppermute | solution.py:395
  39.3 8.6 %collective-permute-start.11 = (bf16[12,32,512]{2,1,0:T(8,128)(2,1)S(1)}, bf16[12,32,512]{2,1,0:T(8,128)(2,1)S(1)}, u32[]{:S(2)}, u32[]{:S(2)}) collective-permute-start(bf16[12,32,512]{2,1,0:T(8,128)(2,1)S(1)} %collective-permute-done.1), channel_id=1, source_target_pairs={{0,8},{5,13},{10,2},{15,7},{16,24},{21,29},{26,18},{31,23}} | collective-permute-start | bytes 1179656 | tf_op jit(solution)/shard_map/ppermute | solution.py:395
  42.5 9.5 %collective-permute-start.13 = (bf16[12,32,512]{2,1,0:T(8,128)(2,1)S(1)}, bf16[12,32,512]{2,1,0:T(8,128)(2,1)S(1)}, u32[]{:S(2)}, u32[]{:S(2)}) collective-permute-start(bf16[12,32,512]{2,1,0:T(8,128)(2,1)S(1)} %collective-permute-done.2), channel_id=1, source_target_pairs={{0,8},{5,13},{10,2},{15,7},{16,24},{21,29},{26,18},{31,23}} | collective-permute-start | bytes 1179656 | tf_op jit(solution)/shard_map/ppermute | solution.py:395
  43.8 14.0 %collective-permute-start.6 = (bf16[1,128,512]{2,1,0:T(8,128)(2,1)S(1)}, bf16[1,128,512]{2,1,0:T(8,128)(2,1)S(1)}, u32[]{:S(2)}, u32[]{:S(2)}) collective-permute-start(bf16[1,128,512]{2,1,0:T(8,128)(2,1)S(1)} %select_bitcast_fusion), channel_id=1, source_target_pairs={{0,4},{1,5},{2,6},{3,7},{4,0},{5,1},{6,2},{7,3},{8,12},{9,13},{10,... | collective-permute-start | bytes 393224 | tf_op jit(solution)/shard_map/ppermute | solution.py:395
  45.1 18.7 %collective-permute-start.17 = (bf16[12,32,512]{2,1,0:T(8,128)(2,1)}, bf16[12,32,512]{2,1,0:T(8,128)(2,1)}, u32[]{:S(2)}, u32[]{:S(2)}) collective-permute-start(bf16[12,32,512]{2,1,0:T(8,128)(2,1)} %broadcast_select_fusion.2.refs_2_), channel_id=1, source_target_pairs={{0,4},{2,6},{5,1},{7,3},{8,12},{10,14},{13,9},{15,11},{16,20},{18,... | collective-permute-start | bytes 1179656 | tf_op jit(solution)/shard_map/ppermute | solution.py:395
  47.9 17.2 %collective-permute-start.10 = (bf16[12,32,512]{2,1,0:T(8,128)(2,1)}, bf16[12,32,512]{2,1,0:T(8,128)(2,1)}, u32[]{:S(2)}, u32[]{:S(2)}) collective-permute-start(bf16[12,32,512]{2,1,0:T(8,128)(2,1)} %broadcast_select_fusion.2.refs_2_), channel_id=1, source_target_pairs={{0,16},{2,18},{5,21},{7,23},{8,24},{10,26},{13,29},{15,31},{16,0},... | collective-permute-start | bytes 1179656 | tf_op jit(solution)/shard_map/ppermute | solution.py:395
  51.9 10.5 %collective-permute-start.16 = (bf16[12,32,512]{2,1,0:T(8,128)(2,1)}, bf16[12,32,512]{2,1,0:T(8,128)(2,1)}, u32[]{:S(2)}, u32[]{:S(2)}) collective-permute-start(bf16[12,32,512]{2,1,0:T(8,128)(2,1)} %collective-permute-done.8.refs_1_), channel_id=1, source_target_pairs={{0,4},{2,6},{5,1},{7,3},{8,12},{10,14},{13,9},{15,11},{16,20},{18,... | collective-permute-start | bytes 1179656 | tf_op jit(solution)/shard_map/ppermute | solution.py:395
  55.1 2.8 %copy-start.2 = (bf16[12,32,512]{2,1,0:T(8,128)(2,1)}, bf16[12,32,512]{2,1,0:T(8,128)(2,1)S(1)}, u32[]{:S(2)}) copy-start(bf16[12,32,512]{2,1,0:T(8,128)(2,1)S(1)} %collective-permute-done.15.refs_8_) | copy-start | bytes 1179652
  55.1 11.4 %collective-permute-start.14 = (bf16[12,32,512]{2,1,0:T(8,128)(2,1)}, bf16[12,32,512]{2,1,0:T(8,128)(2,1)S(1)}, u32[]{:S(2)}, u32[]{:S(2)}) collective-permute-start(bf16[12,32,512]{2,1,0:T(8,128)(2,1)} %get-tuple-element.27.refs_6_), channel_id=1, source_target_pairs={{0,16},{2,18},{5,21},{7,23},{8,24},{10,26},{13,29},{15,31},{16,0},... | collective-permute-start | bytes 1179656 | tf_op jit(solution)/shard_map/ppermute | solution.py:395
  57.9 11.3 %collective-permute-start.12 = (bf16[12,32,512]{2,1,0:T(8,128)(2,1)}, bf16[12,32,512]{2,1,0:T(8,128)(2,1)S(1)}, u32[]{:S(2)}, u32[]{:S(2)}) collective-permute-start(bf16[12,32,512]{2,1,0:T(8,128)(2,1)} %get-tuple-element.28.refs_4_), channel_id=1, source_target_pairs={{0,16},{2,18},{5,21},{7,23},{8,24},{10,26},{13,29},{15,31},{16,0},... | collective-permute-start | bytes 1179656 | tf_op jit(solution)/shard_map/ppermute | solution.py:395
  62.5 29.2 %collective-permute-start.21 = (bf16[12,32,512]{2,1,0:T(8,128)(2,1)}, bf16[12,32,512]{2,1,0:T(8,128)(2,1)S(1)}, u32[]{:S(2)}, u32[]{:S(2)}) collective-permute-start(bf16[12,32,512]{2,1,0:T(8,128)(2,1)} %get-tuple-element.27.refs_6_), channel_id=1, source_target_pairs={{0,4},{2,6},{5,1},{7,3},{8,12},{10,14},{13,9},{15,11},{16,20},{18,... | collective-permute-start | bytes 1179656 | tf_op jit(solution)/shard_map/ppermute | solution.py:395
  63.8 27.9 %collective-permute-start.19 = (bf16[12,32,512]{2,1,0:T(8,128)(2,1)}, bf16[12,32,512]{2,1,0:T(8,128)(2,1)S(1)}, u32[]{:S(2)}, u32[]{:S(2)}) collective-permute-start(bf16[12,32,512]{2,1,0:T(8,128)(2,1)} %get-tuple-element.28.refs_4_), channel_id=1, source_target_pairs={{0,4},{2,6},{5,1},{7,3},{8,12},{10,14},{13,9},{15,11},{16,20},{18,... | collective-permute-start | bytes 1179656 | tf_op jit(solution)/shard_map/ppermute | solution.py:395
  65.1 26.5 %collective-permute-start.18 = (bf16[12,32,512]{2,1,0:T(8,128)(2,1)}, bf16[12,32,512]{2,1,0:T(8,128)(2,1)S(1)}, u32[]{:S(2)}, u32[]{:S(2)}) collective-permute-start(bf16[12,32,512]{2,1,0:T(8,128)(2,1)} %collective-permute-done.10.refs_3_), channel_id=1, source_target_pairs={{0,4},{2,6},{5,1},{7,3},{8,12},{10,14},{13,9},{15,11},{16,20},{18,... | collective-permute-start | bytes 1179656 | tf_op jit(solution)/shard_map/ppermute | solution.py:395
  66.5 17.0 %copy-start.3 = (bf16[12,32,512]{2,1,0:T(8,128)(2,1)}, bf16[12,32,512]{2,1,0:T(8,128)(2,1)S(1)}, u32[]{:S(2)}) copy-start(bf16[12,32,512]{2,1,0:T(8,128)(2,1)S(1)} %collective-permute-done.14.refs_7_) | copy-start | bytes 1179652
  66.5 25.2 %collective-permute-start.22 = (bf16[12,32,512]{2,1,0:T(8,128)(2,1)S(1)}, bf16[12,32,512]{2,1,0:T(8,128)(2,1)}, u32[]{:S(2)}, u32[]{:S(2)}) collective-permute-start(bf16[12,32,512]{2,1,0:T(8,128)(2,1)S(1)} %collective-permute-done.14.refs_7_), channel_id=1, source_target_pairs={{0,4},{2,6},{5,1},{7,3},{8,12},{10,14},{13,9},{15,11},{16,20},{18,... | collective-permute-start | bytes 1179656 | tf_op jit(solution)/shard_map/ppermute | solution.py:395
  69.2 14.3 %copy-start.4 = (bf16[12,32,512]{2,1,0:T(8,128)(2,1)}, bf16[12,32,512]{2,1,0:T(8,128)(2,1)S(1)}, u32[]{:S(2)}) copy-start(bf16[12,32,512]{2,1,0:T(8,128)(2,1)S(1)} %collective-permute-done.12.refs_5_) | copy-start | bytes 1179652
  69.2 22.5 %collective-permute-start.20 = (bf16[12,32,512]{2,1,0:T(8,128)(2,1)S(1)}, bf16[12,32,512]{2,1,0:T(8,128)(2,1)}, u32[]{:S(2)}, u32[]{:S(2)}) collective-permute-start(bf16[12,32,512]{2,1,0:T(8,128)(2,1)S(1)} %collective-permute-done.12.refs_5_), channel_id=1, source_target_pairs={{0,4},{2,6},{5,1},{7,3},{8,12},{10,14},{13,9},{15,11},{16,20},{18,... | collective-permute-start | bytes 1179656 | tf_op jit(solution)/shard_map/ppermute | solution.py:395
  91.6 0.7 copy-start.7
  91.7 0.9 copy-start.5
  91.7 1.0 copy-start.6

commit v2 on v1

--- a/solution.py
+++ b/solution.py
@@ -148,7 +148,7 @@
             pltpu.VMEM((TILE, TILE), jnp.float32),
         ],
         compiler_params=pltpu.CompilerParams(vmem_limit_bytes=VMEM_LIMIT),
-        cost_estimate=pl.CostEstimate(flops=10**9, bytes_accessed=10**7, transcendentals=0),
+        cost_estimate=pl.CostEstimate(flops=12 * 10**9, bytes_accessed=10**6, transcendentals=0),
         name="factor",
     )(points)
 
@@ -222,7 +222,7 @@
         scratch_shapes=[pltpu.VMEM((block, PANEL), jnp.float32)],
         compiler_params=pltpu.CompilerParams(vmem_limit_bytes=VMEM_LIMIT),
         cost_estimate=pl.CostEstimate(
-            flops=2 * m * PANEL * (F + 6 * PANEL), bytes_accessed=m * 4096, transcendentals=0
+            flops=12 * m * PANEL * (F + 6 * PANEL), bytes_accessed=m * 4096, transcendentals=0
         ),
         name="panel_rows",
     )(tau, x, points, t, sp, bp)
@@ -240,23 +240,18 @@
     per = cb // TILE
 
     def load(arrays):
-        moves = []
-        for k, src in enumerate(arrays):
-            group, entry = k // step_tiles, k % step_tiles
-            part = info[4] ^ entry
-            width = src.shape[1]
-
-            def move(tile):
-                at = (tile * step_tiles + part) * TILE + info[5 + group] * width
-                to = pl.ds(pl.multiple_of(at, width), width)
-                return pltpu.make_async_copy(src.at[tile], xc.at[to], sem)
-
-            for tile in range(src.shape[0]):
-                moves.append(move(tile))
-        for m in moves:
-            m.start()
-        for m in moves:
-            m.wait()
+        moves, base = [], 0
+        for k in range(0, len(arrays), step_tiles):
+            for entry, src in enumerate(arrays[k : k + step_tiles]):
+                for tile in range(src.shape[0]):
+                    at = ((base + tile) * step_tiles + (info[4] ^ entry)) * TILE
+                    to = xc.at[pl.ds(pl.multiple_of(at, TILE), TILE)]
+                    moves.append(pltpu.make_async_copy(src.at[tile], to, sem))
+            base += arrays[k].shape[0]
+        for move in moves:
+            move.start()
+        for move in moves:
+            move.wait()
 
     def columns(b):
         size = k_ref.shape[0]
@@ -372,7 +367,7 @@
         ],
         compiler_params=pltpu.CompilerParams(vmem_limit_bytes=VMEM_LIMIT),
         cost_estimate=pl.CostEstimate(
-            flops=2 * m * n * (F + 3 * PANEL), bytes_accessed=m * n * 4, transcendentals=0
+            flops=8 * m * n * (F + 3 * PANEL), bytes_accessed=m * n * 4, transcendentals=0
         ),
         name="trailing",
     )(info, *mine, *got, *panel_args, x_rows, x_rows, cat_rows, cat_rows, s, a, d)
@@ -412,20 +407,21 @@
         has = lambda i, j: i < count
         if self.n_col != 4:
             full = lax.all_gather(x, "col", axis=1, tiled=True)
-            return full, [full], [jnp.int32(0)], self.share(full[0], count)
+            return full, self.share(full[0], count, None)
         before = self.turn(x, 1)
         after = self.turn(x, -1)
-        tile = self.in_order(x[0], before[0], after[0], self.turn(x[0], 2, has))
-        points = self.share(tile, count)
         across = self.turn(before, 1)
-        places = [self.c, (self.c - 1) % 4, (self.c + 1) % 4, (self.c + 2) % 4]
-        return self.in_order(x, before, after, across), [x, before, after, across], places, points
-
-    def share(self, data, count):
+        tile = self.in_order(x[0], before[0], after[0], self.turn(before[0], 1, has))
+        points = self.share(tile, count, across)
+        return self.in_order(x, before, after, across), points
+
+    def share(self, data, count, gate):
         bits = count.bit_length() - 1
-        for bit in range(self.high - 1, bits - 1, -1):
-            got = self.flip(data, bit, lambda i, j: i & ~(count - 1) & ((2 << bit) - 1) == 0)
-            data = jnp.where((self.r >> bit) & 1 == 0, data, got)
+        for bit in range(bits, self.high):
+            got = self.flip(data, bit, lambda i, j: i >> bit == 0)
+            data = jnp.where(self.r >> bit == 0, data, got)
+            if bit == bits:
+                data = tie(data, gate)
         data = data[None]
         for bit in range(bits):
             got = self.flip(data, bit, lambda i, j: True)
@@ -433,16 +429,32 @@
             data = jnp.concatenate([jnp.where(first, data, got), jnp.where(first, got, data)])
         return data
 
-    def spread(self, data):
-        mask = self.n_col - 1
-        for bit in range(self.low - 1, 0, -1):
-            got = self.flip(data, bit, lambda i, j: (i ^ j) & mask == 0)
-            data = jnp.where((self.r ^ self.c) & (1 << bit) == 0, data, got)
-            mask &= ~(1 << bit)
-        parts = [data]
-        for bit in range(self.low, self.high):
-            parts += [self.flip(p, bit, lambda i, j: (i ^ j) & mask == 0) for p in parts]
+    def spread(self, data, high_first, second, last):
+        mask = [self.n_col - 1]
+
+        def copies(parts):
+            for bit in range(self.low - 1, 0, -1):
+                holds = lambda i, j: (i ^ j) & mask[0] == 0
+                own = (self.r ^ self.c) & (1 << bit) == 0
+                parts = [jnp.where(own, p, self.flip(p, bit, holds)) for p in parts]
+                mask[0] &= ~(1 << bit)
+            return parts
+
+        def swaps(parts):
+            for bit in range(self.low, self.high):
+                holds = lambda i, j: (i ^ j) & mask[0] == 0
+                parts = parts + [self.flip(p, bit, holds) for p in parts]
+            return parts
+
+        steps = (swaps, copies) if high_first else (copies, swaps)
+        parts = steps[0]([data])
+        parts = steps[1]([tie(p, second) for p in parts])
+        parts = [tie(p, last) for p in parts]
         return parts, [self.flip(p, 0, lambda i, j: (i ^ j) & 1 == 0) for p in parts]
+
+
+def tie(value, earlier):
+    return value if earlier is None else lax.optimization_barrier((value, earlier))[0]
 
 
 def local(features):
@@ -453,23 +465,24 @@
     tiles_c = tiles_r * step_tiles
     tile = thin * grid.n_col
 
-    rows, pieces, places, points = grid.gather_rows(features[:, 0], PANEL // tile)
+    rows, points = grid.gather_rows(features[:, 0], PANEL // tile)
+    x_rows = rows.reshape(tiles_r * tile, width)
     points = points.reshape(PANEL, width)
     t, sp, bp = factor(points)
     panel_args = (points, t, sp, bp)
+    tau = lambda i: jnp.where(i < PANEL // tile, i, -1)
+    low, *row_args = panel_rows(x_rows, *panel_args, tau(r).astype(jnp.int32).reshape(1))
+
+    cut = tiles_r * 2 // 3 if tiles_r % 3 == 0 else tiles_r
+    pieces = [rows[:cut], rows[cut:]] if cut < tiles_r else [rows]
     mine, got = [], []
-    for piece in pieces:
-        here, there = grid.spread(piece)
+    for k, piece in enumerate(pieces):
+        here, there = grid.spread(piece, k > 0, t, row_args[0])
         mine += here
         got += there
-
-    tau = lambda i: jnp.where(i < PANEL // tile, i, -1)
-    x_rows = rows.reshape(tiles_r * tile, width)
-    low, *row_args = panel_rows(x_rows, *panel_args, tau(r).astype(jnp.int32).reshape(1))
-    info = jnp.stack(
-        [(r - c) % grid.n_col == 0, (r - c) // grid.n_col, tau(c), (r ^ c) & 1, r // grid.n_col]
-        + places
-    ).astype(jnp.int32)
+    info = jnp.stack([
+        (r - c) % grid.n_col == 0, (r - c) // grid.n_col, tau(c), (r ^ c) & 1, r // grid.n_col,
+    ]).astype(jnp.int32)
     out = trailing((x_rows, *row_args), mine, got, panel_args, info, step_tiles)
     return (
         low.reshape(tiles_r, 1, tile, PANEL),

time: 139 us -> 133 us (0.957)
  starting transfers between devices: 48.1 us -> 42.8 us
  waiting for transfers between devices: 15.1 us -> 17.3 us
  other arithmetic: 6.7 us -> 4.93 us
    ppermute x23 -> x16, starting transfers between devices: 48.1 us -> 42.8 us  [send(): return lax.ppermute(value, ('row', 'col'), pairs)]
    ppermute x23 -> x16, waiting for transfers between devices: 15.1 us -> 17.3 us  [send(): return lax.ppermute(value, ('row', 'col'), pairs)]
  transfers between devices with their start and end apart: 23 -> 16, of which waited for: 6 -> 5; matrix products, arithmetic and copies ran while one was open for 6% -> 4% of each run, Pallas kernels for 14% -> 14%
where the time goes in v2:
time: 133 us; the launch traced here: 132 us
  Pallas kernels  64.2 us (48%)
  starting transfers between devices  42.8 us (32%)
  waiting for transfers between devices  17.3 us (13%)
  other arithmetic  4.93 us (4%)
  local copies, waits for them, and re-layouts  1.53 us (1%)
    pallas_call x1, Pallas kernels, trailing(): pl.pallas_call(functools.partial(trailing_kernel, rb, tb, blocks, steps,...  45.3 us
    ppermute x16, starting transfers between devices, send(): return lax.ppermute(value, ('row', 'col'), pairs)  42.8 us
    ppermute x16, waiting for transfers between devices, send(): return lax.ppermute(value, ('row', 'col'), pairs)  17.3 us
    pallas_call x1, Pallas kernels, factor(): pl.pallas_call(factor_kernel, out_shape=[full, vec, vec], scratch_shapes=...  10.9 us
    pallas_call x1, Pallas kernels, panel_rows(): pl.pallas_call(panel_kernel, grid=(m // block,), in_specs=[pl.BlockSpec(m...  8.02 us
    select_n x3, other arithmetic, in_order(): jnp.where(away == 0, own, jnp.where(away == 3, before, jnp.where(away ==...  2.74 us
  transfers between devices with their start and end apart: 16, of which 5 were waited for; matrix products, arithmetic and copies ran while one was open for 4% of the time, Pallas kernels for 14%

profile of v2, /device:TPU:0, one launch (start us, length us, event | category | flops | bytes accessed | tf_op | source)
XLA Modules:
  0.0 132.0 jit_solution(14490323972873021304)
XLA Ops:
  0.6 3.1 %collective-permute-start = (bf16[12,32,512]{2,1,0:T(8,128)(2,1)}, bf16[12,32,512]{2,1,0:T(8,128)(2,1)S(1)}, u32[]{:S(2)}, u32[]{:S(2)}) collective-permute-start(bf16[12,32,512]{2,1,0:T(8,128)(2,1)} %bitcast.49), channel_id=1, source_target_pairs={{0,1},{1,2},{2,3},{3,0},{4,5},{5,6},{6,7},{7,4},{8,9},{9,10},{10,1... | collective-permute-start | bytes 1179656 | tf_op jit(solution)/shard_map/ppermute | solution.py:390
  3.7 2.1 %collective-permute-start.1 = (bf16[12,32,512]{2,1,0:T(8,128)(2,1)}, bf16[12,32,512]{2,1,0:T(8,128)(2,1)S(1)}, u32[]{:S(2)}, u32[]{:S(2)}) collective-permute-start(bf16[12,32,512]{2,1,0:T(8,128)(2,1)} %bitcast.50), channel_id=1, source_target_pairs={{0,3},{1,0},{2,1},{3,2},{4,7},{5,4},{6,5},{7,6},{8,11},{9,8},{10,9... | collective-permute-start | bytes 1179656 | tf_op jit(solution)/shard_map/ppermute | solution.py:390
  5.8 10.1 %collective-permute-done = bf16[12,32,512]{2,1,0:T(8,128)(2,1)S(1)} collective-permute-done((bf16[12,32,512]{2,1,0:T(8,128)(2,1)}, bf16[12,32,512]{2,1,0:T(8,128)(2,1)S(1)}, u32[]{:S(2)}, u32[]{:S(2)}) %collective-permute-start) | collective-permute-done | bytes 393248 | tf_op jit(solution)/shard_map/ppermute | solution.py:390
  15.9 1.9 %collective-permute-start.3 = (bf16[32,512]{1,0:T(8,128)(2,1)S(1)}, bf16[32,512]{1,0:T(8,128)(2,1)S(1)}, u32[]{:S(2)}, u32[]{:S(2)}) collective-permute-start(bf16[32,512]{1,0:T(8,128)(2,1)S(1)} %slice_bitcast_fusion.1), channel_id=1, source_target_pairs={{0,1},{1,2},{2,3},{3,0},{4,5},{5,6},{6,7},{7,4}} | collective-permute-start | bytes 98312 | tf_op jit(solution)/shard_map/ppermute | solution.py:390
  17.9 7.8 %collective-permute-start.2 = (bf16[12,32,512]{2,1,0:T(8,128)(2,1)S(1)}, bf16[12,32,512]{2,1,0:T(8,128)(2,1)S(1)}, u32[]{:S(2)}, u32[]{:S(2)}) collective-permute-start(bf16[12,32,512]{2,1,0:T(8,128)(2,1)S(1)} %collective-permute-done), channel_id=1, source_target_pairs={{0,1},{1,2},{2,3},{3,0},{4,5},{5,6},{6,7},{7,4},{8,9},{9,10},{10,1... | collective-permute-start | bytes 1179656 | tf_op jit(solution)/shard_map/ppermute | solution.py:390
  25.7 0.0 collective-permute-done.1
  25.7 2.7 %collective-permute-done.3 = bf16[32,512]{1,0:T(8,128)(2,1)S(1)} collective-permute-done((bf16[32,512]{1,0:T(8,128)(2,1)S(1)}, bf16[32,512]{1,0:T(8,128)(2,1)S(1)}, u32[]{:S(2)}, u32[]{:S(2)}) %collective-permute-start.3) | collective-permute-done | bytes 32800 | tf_op jit(solution)/shard_map/ppermute | solution.py:390
  28.4 0.8 bitcast_select_fusion.2
  29.2 0.8 bitcast_select_fusion.3
  30.0 1.3 collective-permute-start.4
  31.3 2.5 %collective-permute-done.4 = bf16[128,512]{1,0:T(8,128)(2,1)S(1)} collective-permute-done((bf16[128,512]{1,0:T(8,128)(2,1)S(1)}, bf16[128,512]{1,0:T(8,128)(2,1)S(1)}, u32[]{:S(2)}, u32[]{:S(2)}) %collective-permute-start.4) | collective-permute-done | bytes 131104 | tf_op jit(solution)/shard_map/ppermute | solution.py:390
  33.9 0.0 collective-permute-done.2
  33.9 1.5 %collective-permute-start.5 = (bf16[128,512]{1,0:T(8,128)(2,1)S(1)}, bf16[128,512]{1,0:T(8,128)(2,1)S(1)}, u32[]{:S(2)}, u32[]{:S(2)}) collective-permute-start(bf16[128,512]{1,0:T(8,128)(2,1)S(1)} %broadcast_select_fusion.3), channel_id=1, source_target_pairs={{0,16},{1,17},{2,18},{3,19},{4,20},{5,21},{6,22},{7,23},{8,24},{9,... | collective-permute-start | bytes 393224 | tf_op jit(solution)/shard_map/ppermute | solution.py:390
  35.4 1.2 select_select_fusion.3
  36.6 1.3 collective-permute-done.5
  37.9 0.1 collective-permute-start.6
  38.0 0.1 pad_maximum_fusion
  38.1 0.0 copy-start
  38.1 0.1 slice.24
  38.2 4.4 %collective-permute-start.10 = (bf16[4,128,512]{2,1,0:T(8,128)(2,1)S(1)}, bf16[4,128,512]{2,1,0:T(8,128)(2,1)}, u32[]{:S(2)}, u32[]{:S(2)}) collective-permute-start(bf16[4,128,512]{2,1,0:T(8,128)(2,1)S(1)} %slice.25), channel_id=1, source_target_pairs={{0,16},{5,21},{10,26},{15,31},{16,0},{21,5},{26,10},{31,15}} | collective-permute-start | bytes 1572872 | tf_op jit(solution)/shard_map/ppermute | solution.py:390
  42.6 2.3 %collective-permute-start.7 = (bf16[8,128,512]{2,1,0:T(8,128)(2,1)S(1)}, bf16[8,128,512]{2,1,0:T(8,128)(2,1)}, u32[]{:S(2)}, u32[]{:S(2)}) collective-permute-start(bf16[8,128,512]{2,1,0:T(8,128)(2,1)S(1)} %slice.24), channel_id=1, source_target_pairs={{0,8},{5,13},{10,2},{15,7},{16,24},{21,29},{26,18},{31,23}} | collective-permute-start | bytes 3145736 | tf_op jit(solution)/shard_map/ppermute | solution.py:390
  44.9 0.0 collective-permute-done.6
  44.9 0.7 pad_maximum_fusion.1
  45.7 10.9 %factor.1 = (f32[256,256]{1,0:T(8,128)}, f32[8,256]{1,0:T(8,128)}, f32[8,256]{1,0:T(8,128)}) custom-call(bf16[256,512]{1,0:T(8,128)(2,1)} %bitcast.51), custom_call_target="tpu_custom_call" | custom-call | flops 12000000000 | bytes 1000000 | tf_op jit(solution)/shard_map/factor/pallas_call | solution.py:141
  56.6 0.0 collective-permute-done.7
  56.6 0.0 copy-done
  56.6 0.1 broadcast_select_fusion.refs_0_
  56.7 0.0 copy-start.1
  56.7 4.3 %collective-permute-start.8 = (bf16[8,128,512]{2,1,0:T(8,128)(2,1)S(1)}, bf16[8,128,512]{2,1,0:T(8,128)(2,1)}, u32[]{:S(2)}, u32[]{:S(2)}) collective-permute-start(bf16[8,128,512]{2,1,0:T(8,128)(2,1)S(1)} %broadcast_select_fusion.refs_0_), channel_id=1, source_target_pairs={{0,16},{2,18},{5,21},{7,23},{8,24},{10,26},{13,29},{15,31},{16,0},... | collective-permute-start | bytes 3145736 | tf_op jit(solution)/shard_map/ppermute | solution.py:390
  61.0 5.4 %collective-permute-start.9 = (bf16[4,128,512]{2,1,0:T(8,128)(2,1)S(1)}, bf16[4,128,512]{2,1,0:T(8,128)(2,1)S(1)}, u32[]{:S(2)}, u32[]{:S(2)}) collective-permute-start(bf16[4,128,512]{2,1,0:T(8,128)(2,1)S(1)} %slice.25), channel_id=1, source_target_pairs={{0,8},{5,13},{10,2},{15,7},{16,24},{21,29},{26,18},{31,23}} | collective-permute-start | bytes 1572872 | tf_op jit(solution)/shard_map/ppermute | solution.py:390
  66.4 0.0 collective-permute-done.10
  66.4 1.3 %collective-permute-start.11 = (bf16[4,128,512]{2,1,0:T(8,128)(2,1)}, bf16[4,128,512]{2,1,0:T(8,128)(2,1)S(1)}, u32[]{:S(2)}, u32[]{:S(2)}) collective-permute-start(bf16[4,128,512]{2,1,0:T(8,128)(2,1)} %collective-permute-done.10), channel_id=1, source_target_pairs={{0,8},{5,13},{10,2},{15,7},{16,24},{21,29},{26,18},{31,23}} | collective-permute-start | bytes 1572872 | tf_op jit(solution)/shard_map/ppermute | solution.py:390
  67.7 8.0 %panel_rows.1 = (f32[1536,256]{1,0:T(8,128)}, bf16[1536,768]{1,0:T(8,128)(2,1)}, f32[1536,128]{1,0:T(8,128)}, f32[1536,128]{1,0:T(8,128)}, f32[1536,128]{1,0:T(8,128)}) custom-call(s32[1]{0:T(128)} %bitcast.tau_ref, bf16[1536,512]{1,0:T(8,128)(2,1)} %bitcast.46, bf16[256,512]{1,0:T(8,128)(2,1)} %bitcast.52, f32[256,256]{1,0:T(8,128)} %get-tuple-element.19.t_ref.refs_9_, ...), custom_call_target="tpu_custom_call" | custom-call | flops 9663676416 | bytes 6291456 | tf_op jit(solution)/shard_map/panel_rows/pallas_call | solution.py:211
  75.7 0.0 copy-done.1
  75.8 2.3 %collective-permute-start.12 = (bf16[8,128,512]{2,1,0:T(8,128)(2,1)S(1)}, bf16[8,128,512]{2,1,0:T(8,128)(2,1)}, u32[]{:S(2)}, u32[]{:S(2)}) collective-permute-start(bf16[8,128,512]{2,1,0:T(8,128)(2,1)S(1)} %broadcast_select_fusion.refs_0_), channel_id=1, source_target_pairs={{0,4},{2,6},{5,1},{7,3},{8,12},{10,14},{13,9},{15,11},{16,20},{18,... | collective-permute-start | bytes 3145736 | tf_op jit(solution)/shard_map/ppermute | solution.py:390
  78.0 0.0 collective-permute-done.8.refs_1_
  78.0 2.3 %collective-permute-start.13 = (bf16[8,128,512]{2,1,0:T(8,128)(2,1)}, bf16[8,128,512]{2,1,0:T(8,128)(2,1)}, u32[]{:S(2)}, u32[]{:S(2)}) collective-permute-start(bf16[8,128,512]{2,1,0:T(8,128)(2,1)} %collective-permute-done.8.refs_1_), channel_id=1, source_target_pairs={{0,4},{2,6},{5,1},{7,3},{8,12},{10,14},{13,9},{15,11},{16,20},{18,... | collective-permute-start | bytes 3145736 | tf_op jit(solution)/shard_map/ppermute | solution.py:390
  80.4 0.0 collective-permute-done.9
  80.4 0.0 collective-permute-done.11
  80.4 1.1 broadcast_select_fusion.1
  81.5 0.0 copy-start.2
  81.5 0.0 copy-start.3
  81.5 1.3 %collective-permute-start.14 = (bf16[4,128,512]{2,1,0:T(8,128)(2,1)S(1)}, bf16[4,128,512]{2,1,0:T(8,128)(2,1)S(1)}, u32[]{:S(2)}, u32[]{:S(2)}) collective-permute-start(bf16[4,128,512]{2,1,0:T(8,128)(2,1)S(1)} %get-tuple-element.28.refs_2_), channel_id=1, source_target_pairs={{0,4},{2,6},{5,1},{7,3},{8,12},{10,14},{13,9},{15,11},{16,20},{18,... | collective-permute-start | bytes 1572872 | tf_op jit(solution)/shard_map/ppermute | solution.py:390
  82.9 1.5 %collective-permute-start.15 = (bf16[4,128,512]{2,1,0:T(8,128)(2,1)S(1)}, bf16[4,128,512]{2,1,0:T(8,128)(2,1)S(1)}, u32[]{:S(2)}, u32[]{:S(2)}) collective-permute-start(bf16[4,128,512]{2,1,0:T(8,128)(2,1)S(1)} %get-tuple-element.30.refs_3_), channel_id=1, source_target_pairs={{0,4},{2,6},{5,1},{7,3},{8,12},{10,14},{13,9},{15,11},{16,20},{18,... | collective-permute-start | bytes 1572872 | tf_op jit(solution)/shard_map/ppermute | solution.py:390
  84.4 0.6 stack.27.info
  85.0 0.0 collective-permute-done.14.refs_6_
  85.0 0.0 copy-start.4
  85.0 0.6 collective-permute-done.15.refs_7_
  85.7 0.0 copy-start.5
  85.7 0.0 collective-permute-done.12.refs_4_
  85.7 0.0 collective-permute-done.13.refs_5_
  85.7 0.0 copy-done.2
  85.7 0.0 copy-done.3
  85.7 0.1 copy-done.4
  85.8 0.7 copy-done.5
  86.5 45.3 %trailing.1 = f32[1536,24,128]{2,1,0:T(8,128)} custom-call(s32[5]{0:T(128)} %stack.27.info, bf16[8,128,512]{2,1,0:T(8,128)(2,1)} %copy-done.1, bf16[8,128,512]{2,1,0:T(8,128)(2,1)} %collective-permute-done.8.refs_1_, bf16[4,128,512]{2,1,0:T(8,128)(2,1)} %copy-done.3, bf16[4,128,512]{2,1,0:T(8,128)(2,1)} %copy-done.2, ...), custom_call_target="tpu_custom_call" | custom-call | flops 48318382080 | bytes 18874368 | tf_op jit(solution)/shard_map/trailing/pallas_call | solution.py:348
  (6 shorter events, 0.1 us)
Async XLA Ops:
  0.6 15.3 %collective-permute-start = (bf16[12,32,512]{2,1,0:T(8,128)(2,1)}, bf16[12,32,512]{2,1,0:T(8,128)(2,1)S(1)}, u32[]{:S(2)}, u32[]{:S(2)}) collective-permute-start(bf16[12,32,512]{2,1,0:T(8,128)(2,1)} %bitcast.49), channel_id=1, source_target_pairs={{0,1},{1,2},{2,3},{3,0},{4,5},{5,6},{6,7},{7,4},{8,9},{9,10},{10,1... | collective-permute-start | bytes 1179656 | tf_op jit(solution)/shard_map/ppermute | solution.py:390
  3.7 22.0 %collective-permute-start.1 = (bf16[12,32,512]{2,1,0:T(8,128)(2,1)}, bf16[12,32,512]{2,1,0:T(8,128)(2,1)S(1)}, u32[]{:S(2)}, u32[]{:S(2)}) collective-permute-start(bf16[12,32,512]{2,1,0:T(8,128)(2,1)} %bitcast.50), channel_id=1, source_target_pairs={{0,3},{1,0},{2,1},{3,2},{4,7},{5,4},{6,5},{7,6},{8,11},{9,8},{10,9... | collective-permute-start | bytes 1179656 | tf_op jit(solution)/shard_map/ppermute | solution.py:390
  15.9 12.5 %collective-permute-start.3 = (bf16[32,512]{1,0:T(8,128)(2,1)S(1)}, bf16[32,512]{1,0:T(8,128)(2,1)S(1)}, u32[]{:S(2)}, u32[]{:S(2)}) collective-permute-start(bf16[32,512]{1,0:T(8,128)(2,1)S(1)} %slice_bitcast_fusion.1), channel_id=1, source_target_pairs={{0,1},{1,2},{2,3},{3,0},{4,5},{5,6},{6,7},{7,4}} | collective-permute-start | bytes 98312 | tf_op jit(solution)/shard_map/ppermute | solution.py:390
  17.9 15.9 %collective-permute-start.2 = (bf16[12,32,512]{2,1,0:T(8,128)(2,1)S(1)}, bf16[12,32,512]{2,1,0:T(8,128)(2,1)S(1)}, u32[]{:S(2)}, u32[]{:S(2)}) collective-permute-start(bf16[12,32,512]{2,1,0:T(8,128)(2,1)S(1)} %collective-permute-done), channel_id=1, source_target_pairs={{0,1},{1,2},{2,3},{3,0},{4,5},{5,6},{6,7},{7,4},{8,9},{9,10},{10,1... | collective-permute-start | bytes 1179656 | tf_op jit(solution)/shard_map/ppermute | solution.py:390
  30.0 3.8 %collective-permute-start.4 = (bf16[128,512]{1,0:T(8,128)(2,1)S(1)}, bf16[128,512]{1,0:T(8,128)(2,1)S(1)}, u32[]{:S(2)}, u32[]{:S(2)}) collective-permute-start(bf16[128,512]{1,0:T(8,128)(2,1)S(1)} %pad_maximum_fusion.2), channel_id=1, source_target_pairs={{0,8},{1,9},{2,10},{3,11},{4,12},{5,13},{6,14},{7,15}} | collective-permute-start | bytes 393224 | tf_op jit(solution)/shard_map/ppermute | solution.py:390
  33.9 4.0 %collective-permute-start.5 = (bf16[128,512]{1,0:T(8,128)(2,1)S(1)}, bf16[128,512]{1,0:T(8,128)(2,1)S(1)}, u32[]{:S(2)}, u32[]{:S(2)}) collective-permute-start(bf16[128,512]{1,0:T(8,128)(2,1)S(1)} %broadcast_select_fusion.3), channel_id=1, source_target_pairs={{0,16},{1,17},{2,18},{3,19},{4,20},{5,21},{6,22},{7,23},{8,24},{9,... | collective-permute-start | bytes 393224 | tf_op jit(solution)/shard_map/ppermute | solution.py:390
  37.9 7.0 %collective-permute-start.6 = (bf16[1,128,512]{2,1,0:T(8,128)(2,1)S(1)}, bf16[1,128,512]{2,1,0:T(8,128)(2,1)S(1)}, u32[]{:S(2)}, u32[]{:S(2)}) collective-permute-start(bf16[1,128,512]{2,1,0:T(8,128)(2,1)S(1)} %select_bitcast_fusion), channel_id=1, source_target_pairs={{0,4},{1,5},{2,6},{3,7},{4,0},{5,1},{6,2},{7,3},{8,12},{9,13},{10,... | collective-permute-start | bytes 393224 | tf_op jit(solution)/shard_map/ppermute | solution.py:390
  38.1 18.5 %copy-start = (bf16[12,128,512]{2,1,0:T(8,128)(2,1)}, bf16[12,128,512]{2,1,0:T(8,128)(2,1)S(1)}, u32[]{:S(2)}) copy-start(bf16[12,128,512]{2,1,0:T(8,128)(2,1)S(1)} %pad_maximum_fusion) | copy-start | bytes 4718596
  38.2 28.2 %collective-permute-start.10 = (bf16[4,128,512]{2,1,0:T(8,128)(2,1)S(1)}, bf16[4,128,512]{2,1,0:T(8,128)(2,1)}, u32[]{:S(2)}, u32[]{:S(2)}) collective-permute-start(bf16[4,128,512]{2,1,0:T(8,128)(2,1)S(1)} %slice.25), channel_id=1, source_target_pairs={{0,16},{5,21},{10,26},{15,31},{16,0},{21,5},{26,10},{31,15}} | collective-permute-start | bytes 1572872 | tf_op jit(solution)/shard_map/ppermute | solution.py:390
  42.6 14.0 %collective-permute-start.7 = (bf16[8,128,512]{2,1,0:T(8,128)(2,1)S(1)}, bf16[8,128,512]{2,1,0:T(8,128)(2,1)}, u32[]{:S(2)}, u32[]{:S(2)}) collective-permute-start(bf16[8,128,512]{2,1,0:T(8,128)(2,1)S(1)} %slice.24), channel_id=1, source_target_pairs={{0,8},{5,13},{10,2},{15,7},{16,24},{21,29},{26,18},{31,23}} | collective-permute-start | bytes 3145736 | tf_op jit(solution)/shard_map/ppermute | solution.py:390
  56.7 19.1 %copy-start.1 = (bf16[8,128,512]{2,1,0:T(8,128)(2,1)}, bf16[8,128,512]{2,1,0:T(8,128)(2,1)S(1)}, u32[]{:S(2)}) copy-start(bf16[8,128,512]{2,1,0:T(8,128)(2,1)S(1)} %broadcast_select_fusion.refs_0_) | copy-start | bytes 3145732
  56.7 21.3 %collective-permute-start.8 = (bf16[8,128,512]{2,1,0:T(8,128)(2,1)S(1)}, bf16[8,128,512]{2,1,0:T(8,128)(2,1)}, u32[]{:S(2)}, u32[]{:S(2)}) collective-permute-start(bf16[8,128,512]{2,1,0:T(8,128)(2,1)S(1)} %broadcast_select_fusion.refs_0_), channel_id=1, source_target_pairs={{0,16},{2,18},{5,21},{7,23},{8,24},{10,26},{13,29},{15,31},{16,0},... | collective-permute-start | bytes 3145736 | tf_op jit(solution)/shard_map/ppermute | solution.py:390
  61.0 19.3 %collective-permute-start.9 = (bf16[4,128,512]{2,1,0:T(8,128)(2,1)S(1)}, bf16[4,128,512]{2,1,0:T(8,128)(2,1)S(1)}, u32[]{:S(2)}, u32[]{:S(2)}) collective-permute-start(bf16[4,128,512]{2,1,0:T(8,128)(2,1)S(1)} %slice.25), channel_id=1, source_target_pairs={{0,8},{5,13},{10,2},{15,7},{16,24},{21,29},{26,18},{31,23}} | collective-permute-start | bytes 1572872 | tf_op jit(solution)/shard_map/ppermute | solution.py:390
  66.4 14.0 %collective-permute-start.11 = (bf16[4,128,512]{2,1,0:T(8,128)(2,1)}, bf16[4,128,512]{2,1,0:T(8,128)(2,1)S(1)}, u32[]{:S(2)}, u32[]{:S(2)}) collective-permute-start(bf16[4,128,512]{2,1,0:T(8,128)(2,1)} %collective-permute-done.10), channel_id=1, source_target_pairs={{0,8},{5,13},{10,2},{15,7},{16,24},{21,29},{26,18},{31,23}} | collective-permute-start | bytes 1572872 | tf_op jit(solution)/shard_map/ppermute | solution.py:390
  75.8 9.9 %collective-permute-start.12 = (bf16[8,128,512]{2,1,0:T(8,128)(2,1)S(1)}, bf16[8,128,512]{2,1,0:T(8,128)(2,1)}, u32[]{:S(2)}, u32[]{:S(2)}) collective-permute-start(bf16[8,128,512]{2,1,0:T(8,128)(2,1)S(1)} %broadcast_select_fusion.refs_0_), channel_id=1, source_target_pairs={{0,4},{2,6},{5,1},{7,3},{8,12},{10,14},{13,9},{15,11},{16,20},{18,... | collective-permute-start | bytes 3145736 | tf_op jit(solution)/shard_map/ppermute | solution.py:390
  78.0 7.6 %collective-permute-start.13 = (bf16[8,128,512]{2,1,0:T(8,128)(2,1)}, bf16[8,128,512]{2,1,0:T(8,128)(2,1)}, u32[]{:S(2)}, u32[]{:S(2)}) collective-permute-start(bf16[8,128,512]{2,1,0:T(8,128)(2,1)} %collective-permute-done.8.refs_1_), channel_id=1, source_target_pairs={{0,4},{2,6},{5,1},{7,3},{8,12},{10,14},{13,9},{15,11},{16,20},{18,... | collective-permute-start | bytes 3145736 | tf_op jit(solution)/shard_map/ppermute | solution.py:390
  81.5 4.2 %copy-start.2 = (bf16[4,128,512]{2,1,0:T(8,128)(2,1)}, bf16[4,128,512]{2,1,0:T(8,128)(2,1)S(1)}, u32[]{:S(2)}) copy-start(bf16[4,128,512]{2,1,0:T(8,128)(2,1)S(1)} %get-tuple-element.30.refs_3_) | copy-start | bytes 1572868
  81.5 4.2 %copy-start.3 = (bf16[4,128,512]{2,1,0:T(8,128)(2,1)}, bf16[4,128,512]{2,1,0:T(8,128)(2,1)S(1)}, u32[]{:S(2)}) copy-start(bf16[4,128,512]{2,1,0:T(8,128)(2,1)S(1)} %get-tuple-element.28.refs_2_) | copy-start | bytes 1572868
  81.5 3.5 %collective-permute-start.14 = (bf16[4,128,512]{2,1,0:T(8,128)(2,1)S(1)}, bf16[4,128,512]{2,1,0:T(8,128)(2,1)S(1)}, u32[]{:S(2)}, u32[]{:S(2)}) collective-permute-start(bf16[4,128,512]{2,1,0:T(8,128)(2,1)S(1)} %get-tuple-element.28.refs_2_), channel_id=1, source_target_pairs={{0,4},{2,6},{5,1},{7,3},{8,12},{10,14},{13,9},{15,11},{16,20},{18,... | collective-permute-start | bytes 1572872 | tf_op jit(solution)/shard_map/ppermute | solution.py:390
  82.9 2.8 %collective-permute-start.15 = (bf16[4,128,512]{2,1,0:T(8,128)(2,1)S(1)}, bf16[4,128,512]{2,1,0:T(8,128)(2,1)S(1)}, u32[]{:S(2)}, u32[]{:S(2)}) collective-permute-start(bf16[4,128,512]{2,1,0:T(8,128)(2,1)S(1)} %get-tuple-element.30.refs_3_), channel_id=1, source_target_pairs={{0,4},{2,6},{5,1},{7,3},{8,12},{10,14},{13,9},{15,11},{16,20},{18,... | collective-permute-start | bytes 1572872 | tf_op jit(solution)/shard_map/ppermute | solution.py:390
  85.0 0.8 copy-start.4
  85.7 0.8 copy-start.5

commit v3 on v2

--- a/solution.py
+++ b/solution.py
@@ -80,7 +80,7 @@
         for k in range(8):
             piv = cols[k][k : k + 1, :]
             inv = 1.0 / piv
-            m = jnp.where(sub > k, cols[k] * inv, 0.0)
+            m = jnp.where(sub > k, cols[k], 0.0) * inv
             ak, ek = a8[k : k + 1, :], e8[k : k + 1, :]
             up = [cols[j][k : k + 1, :] for j in range(k + 1, 8)]
             for j in range(k + 1, 8):
@@ -109,8 +109,8 @@
 def factor_kernel(x_ref, t_ref, sp_ref, bp_ref, k_ref, w_ref, t1_ref, t2_ref):
     x = x_ref[...]
     gq_l = norm_lanes(x)
-    s_l = jnp.sqrt(gq_l + EPS)
-    b_l = 1.0 / s_l
+    b_l = lax.rsqrt(gq_l + EPS)
+    s_l = (gq_l + EPS) * b_l
     sp_ref[...] = s_l
     bp_ref[...] = b_l
     gq = norm_rows(x)
@@ -153,25 +153,31 @@
     )(points)
 
 
-def panel_block(x, pts, sp, bp, k_ref):
-    gq = norm_rows(x)
-    s = jnp.sqrt(gq + EPS)
-    a = (1.0 / F) / s
-    k_ref[...] = dot_nt(x, pts)
-    for g in range(0, x.shape[0], 16):
-        rows = slice(g, g + 16)
-        rho = k_ref[rows, :] * a[rows, :] * bp
-        k_ref[rows, :] = two_layers(rho) * (s[rows, :] * sp)
-    return s, a, 3.0 * gq + (2.0 * EPS + RIDGE)
+def panel_block(x_ref, pts, sp, bp, k_ref):
+    m = x_ref.shape[0]
+    part = m // 2 if m % 32 == 0 else m
+    norms = []
+    for h in range(0, m, part):
+        x = x_ref[h : h + part, :]
+        gq = norm_rows(x)
+        q = gq + EPS
+        inv = lax.rsqrt(q)
+        s = q * inv
+        a = inv * (1.0 / F)
+        k_ref[h : h + part, :] = dot_nt(x, pts)
+        for g in range(0, part, 16):
+            rows = slice(h + g, h + g + 16)
+            rho = k_ref[rows, :] * a[g : g + 16, :] * bp
+            k_ref[rows, :] = two_layers(rho) * (s[g : g + 16, :] * sp)
+        norms.append((h, part, s, a, 3.0 * gq + (2.0 * EPS + RIDGE)))
+    return norms
 
 
 def set_diagonal(k_ref, diag, hit):
     for half in range(PANEL // TILE):
-
-        @pl.when(hit == half)
-        def _():
-            cols = slice(half * TILE, (half + 1) * TILE)
-            k_ref[:TILE, cols] = jnp.where(eye(TILE), diag[:TILE, :], k_ref[:TILE, cols])
+        cols = slice(half * TILE, (half + 1) * TILE)
+        here = eye(TILE) & (hit == half)
+        k_ref[:TILE, cols] = jnp.where(here, diag[:TILE, :], k_ref[:TILE, cols])
 
 
 def split(low):
@@ -181,18 +187,20 @@
 
 def panel_kernel(tau_ref, x_ref, pts_ref, t_ref, sp_ref, bp_ref,
                  l_ref, cat_ref, s_ref, a_ref, d_ref, k_ref):
-    s, a, diag = panel_block(x_ref[...], pts_ref[...], sp_ref[0:1, :], bp_ref[0:1, :], k_ref)
-    set_diagonal(k_ref, diag, jnp.where(pl.program_id(0) == 0, tau_ref[0], -1))
-    low = dot_hi(k_ref[...], t_ref[...], ((1,), (1,)))
-    hi, lo = split(low)
-    l_ref[...] = low
-    cat_ref[:, :PANEL] = hi
-    cat_ref[:, PANEL : 2 * PANEL] = hi
-    cat_ref[:, 2 * PANEL :] = lo
-    s_ref[...] = jnp.broadcast_to(s, s_ref.shape)
-    a_ref[...] = jnp.broadcast_to(a, a_ref.shape)
-    left = diag - jnp.sum(low * low, axis=1, keepdims=True)
-    d_ref[...] = jnp.broadcast_to(left, d_ref.shape)
+    norms = panel_block(x_ref, pts_ref[...], sp_ref[0:1, :], bp_ref[0:1, :], k_ref)
+    set_diagonal(k_ref, norms[0][4], jnp.where(pl.program_id(0) == 0, tau_ref[0], -1))
+    for h, part, s, a, diag in norms:
+        rows = slice(h, h + part)
+        low = dot_hi(k_ref[rows, :], t_ref[...], ((1,), (1,)))
+        hi, lo = split(low)
+        l_ref[rows, :] = low
+        cat_ref[rows, :PANEL] = hi
+        cat_ref[rows, PANEL : 2 * PANEL] = hi
+        cat_ref[rows, 2 * PANEL :] = lo
+        s_ref[rows, :] = jnp.broadcast_to(s, (part, 128))
+        a_ref[rows, :] = jnp.broadcast_to(a, (part, 128))
+        left = diag - jnp.sum(low * low, axis=1, keepdims=True)
+        d_ref[rows, :] = jnp.broadcast_to(left, (part, 128))
 
 
 def pick(total, options):
@@ -239,34 +247,34 @@
     cb = tb * TILE // 2
     per = cb // TILE
 
+    size = k_ref.shape[0]
+
     def load(arrays):
-        moves, base = [], 0
+        base = 0
         for k in range(0, len(arrays), step_tiles):
-            for entry, src in enumerate(arrays[k : k + step_tiles]):
-                for tile in range(src.shape[0]):
+            for tile in range(arrays[k].shape[0]):
+                for entry, src in enumerate(arrays[k : k + step_tiles]):
                     at = ((base + tile) * step_tiles + (info[4] ^ entry)) * TILE
                     to = xc.at[pl.ds(pl.multiple_of(at, TILE), TILE)]
-                    moves.append(pltpu.make_async_copy(src.at[tile], to, sem))
+                    pltpu.make_async_copy(src.at[tile], to, sem.at[at // size]).start()
             base += arrays[k].shape[0]
-        for move in moves:
-            move.start()
-        for move in moves:
-            move.wait()
 
     def columns(b):
-        size = k_ref.shape[0]
         rows = pl.ds(pl.multiple_of(b * size, size), size)
-        s, _, diag = panel_block(xc[rows, :], pts[...], sp_ref[0:1, :], bp_ref[0:1, :], k_ref)
-        set_diagonal(k_ref, diag, jnp.where(b == 0, info[2], -1))
-        hi, lo = split(dot_hi(k_ref[...], t_ref[...], ((1,), (1,))))
-        lc[rows, :PANEL] = hi
-        lc[rows, PANEL : 2 * PANEL] = lo
-        lc[rows, 2 * PANEL :] = hi
-        for g in range(0, size, TILE):
-            wide = jnp.broadcast_to(s[g : g + TILE, :], (TILE, TILE)).T[0:8, :]
-            lanes = pl.ds(pl.multiple_of(b * size + g, TILE), TILE)
-            sc[:, lanes] = wide
-            bc[:, lanes] = 1.0 / wide
+        pltpu.make_async_copy(xc.at[rows], xc.at[rows], sem.at[b]).wait()
+        norms = panel_block(xc.at[rows], pts[...], sp_ref[0:1, :], bp_ref[0:1, :], k_ref)
+        set_diagonal(k_ref, norms[0][4], jnp.where(b == 0, info[2], -1))
+        for h, part, s, _, _ in norms:
+            hi, lo = split(dot_hi(k_ref[h : h + part, :], t_ref[...], ((1,), (1,))))
+            to = pl.ds(pl.multiple_of(b * size + h, part), part)
+            lc[to, :PANEL] = hi
+            lc[to, PANEL : 2 * PANEL] = lo
+            lc[to, 2 * PANEL :] = hi
+            for g in range(0, part, TILE):
+                wide = jnp.broadcast_to(s[g : g + TILE, :], (TILE, TILE)).T[0:8, :]
+                lanes = pl.ds(pl.multiple_of(b * size + h + g, TILE), TILE)
+                sc[:, lanes] = wide
+                bc[:, lanes] = 1.0 / wide
 
     def multiply(x, l, col, g, m):
         cols = pl.ds(pl.multiple_of(col, cb), cb)
@@ -295,7 +303,7 @@
         def _():
             load(got)
 
-        @pl.loop(0, xc.shape[0] // k_ref.shape[0])
+        @pl.loop(0, xc.shape[0] // size)
         def _(b):
             columns(b)
 
@@ -332,6 +340,7 @@
     cb = tb * TILE // 2
     blocks = n // (tb * TILE)
     steps = m // rb * blocks
+    size = pick(n, (512, 256))
     const = lambda shape: pl.BlockSpec(shape, lambda q: (0, 0))
     cur = lambda width: pl.BlockSpec((rb, width), lambda q: (q // blocks, 0))
     nxt = lambda width: pl.BlockSpec(
@@ -361,9 +370,9 @@
             pltpu.VMEM((n, 3 * PANEL), jnp.bfloat16),
             pltpu.VMEM((8, n), jnp.float32),
             pltpu.VMEM((8, n), jnp.float32),
-            pltpu.VMEM((pick(n, (512, 384, 256, 128)), PANEL), jnp.float32),
+            pltpu.VMEM((size, PANEL), jnp.float32),
             square, square, square, square,
-            pltpu.SemaphoreType.DMA,
+            pltpu.SemaphoreType.DMA((n // size,)),
         ],
         compiler_params=pltpu.CompilerParams(vmem_limit_bytes=VMEM_LIMIT),
         cost_estimate=pl.CostEstimate(
@@ -436,7 +445,9 @@
             for bit in range(self.low - 1, 0, -1):
                 holds = lambda i, j: (i ^ j) & mask[0] == 0
                 own = (self.r ^ self.c) & (1 << bit) == 0
-                parts = [jnp.where(own, p, self.flip(p, bit, holds)) for p in parts]
+                data = parts[0] if len(parts) == 1 else jnp.stack(parts)
+                data = jnp.where(own, data, self.flip(data, bit, holds))
+                parts = [data] if len(parts) == 1 else list(data)
                 mask[0] &= ~(1 << bit)
             return parts
 

time: 133 us -> 130 us (0.977)
  Pallas kernels: 64.2 us -> 60.8 us
  starting transfers between devices: 42.8 us -> 41 us
    pallas_call x1, Pallas kernels: 45.3 us -> 42.9 us  [trailing(): pl.pallas_call(functools.partial(trailing_kernel, rb, tb, blocks, steps,...]
    ppermute x16 -> x15, starting transfers between devices: 42.8 us -> 41 us  [send(): return lax.ppermute(value, ('row', 'col'), pairs)]
    ppermute x16 -> x15, waiting for transfers between devices: 17.3 us -> 18.2 us  [send(): return lax.ppermute(value, ('row', 'col'), pairs)]
  transfers between devices with their start and end apart: 16 -> 15, of which waited for: 5 -> 7; matrix products, arithmetic and copies ran while one was open for 4% -> 5% of each run, Pallas kernels for 14% -> 14%
where the time goes in v3:
time: 130 us
  Pallas kernels  60.8 us (47%)
  starting transfers between devices  41 us (32%)
  waiting for transfers between devices  18.2 us (14%)
  other arithmetic  5.94 us (5%)
  local copies, waits for them, and re-layouts  2.71 us (2%)
    pallas_call x1, Pallas kernels, trailing(): pl.pallas_call(functools.partial(trailing_kernel, rb, tb, blocks, steps,...  42.9 us
    ppermute x15, starting transfers between devices, send(): return lax.ppermute(value, ('row', 'col'), pairs)  41 us
    ppermute x15, waiting for transfers between devices, send(): return lax.ppermute(value, ('row', 'col'), pairs)  18.2 us
    pallas_call x1, Pallas kernels, factor(): pl.pallas_call(factor_kernel, out_shape=[full, vec, vec], scratch_shapes=...  10.6 us
    pallas_call x1, Pallas kernels, panel_rows(): pl.pallas_call(panel_kernel, grid=(m // block,), in_specs=[pl.BlockSpec(m...  7.25 us
    select_n x3, other arithmetic, in_order(): jnp.where(away == 0, own, jnp.where(away == 3, before, jnp.where(away ==...  2.74 us
  transfers between devices with their start and end apart: 15, of which 7 were waited for; matrix products, arithmetic and copies ran while one was open for 5% of the time, Pallas kernels for 14%

profile of v3, /device:TPU:0, one launch (start us, length us, event | category | flops | bytes accessed | tf_op | source)
XLA Modules:
  0.0 129.8 jit_solution(13756314376639785095)
XLA Ops:
  0.6 3.1 %collective-permute-start = (bf16[12,32,512]{2,1,0:T(8,128)(2,1)}, bf16[12,32,512]{2,1,0:T(8,128)(2,1)S(1)}, u32[]{:S(2)}, u32[]{:S(2)}) collective-permute-start(bf16[12,32,512]{2,1,0:T(8,128)(2,1)} %bitcast.59), channel_id=1, source_target_pairs={{0,1},{1,2},{2,3},{3,0},{4,5},{5,6},{6,7},{7,4},{8,9},{9,10},{10,1... | collective-permute-start | bytes 1179656 | tf_op jit(solution)/shard_map/ppermute | solution.py:399
  3.7 2.1 %collective-permute-start.1 = (bf16[12,32,512]{2,1,0:T(8,128)(2,1)}, bf16[12,32,512]{2,1,0:T(8,128)(2,1)S(1)}, u32[]{:S(2)}, u32[]{:S(2)}) collective-permute-start(bf16[12,32,512]{2,1,0:T(8,128)(2,1)} %bitcast.60), channel_id=1, source_target_pairs={{0,3},{1,0},{2,1},{3,2},{4,7},{5,4},{6,5},{7,6},{8,11},{9,8},{10,9... | collective-permute-start | bytes 1179656 | tf_op jit(solution)/shard_map/ppermute | solution.py:399
  5.8 10.1 %collective-permute-done = bf16[12,32,512]{2,1,0:T(8,128)(2,1)S(1)} collective-permute-done((bf16[12,32,512]{2,1,0:T(8,128)(2,1)}, bf16[12,32,512]{2,1,0:T(8,128)(2,1)S(1)}, u32[]{:S(2)}, u32[]{:S(2)}) %collective-permute-start) | collective-permute-done | bytes 393248 | tf_op jit(solution)/shard_map/ppermute | solution.py:399
  15.9 1.9 %collective-permute-start.3 = (bf16[32,512]{1,0:T(8,128)(2,1)S(1)}, bf16[32,512]{1,0:T(8,128)(2,1)S(1)}, u32[]{:S(2)}, u32[]{:S(2)}) collective-permute-start(bf16[32,512]{1,0:T(8,128)(2,1)S(1)} %slice_bitcast_fusion.3), channel_id=1, source_target_pairs={{0,1},{1,2},{2,3},{3,0},{4,5},{5,6},{6,7},{7,4}} | collective-permute-start | bytes 98312 | tf_op jit(solution)/shard_map/ppermute | solution.py:399
  17.9 7.8 %collective-permute-start.2 = (bf16[12,32,512]{2,1,0:T(8,128)(2,1)S(1)}, bf16[12,32,512]{2,1,0:T(8,128)(2,1)S(1)}, u32[]{:S(2)}, u32[]{:S(2)}) collective-permute-start(bf16[12,32,512]{2,1,0:T(8,128)(2,1)S(1)} %collective-permute-done), channel_id=1, source_target_pairs={{0,1},{1,2},{2,3},{3,0},{4,5},{5,6},{6,7},{7,4},{8,9},{9,10},{10,1... | collective-permute-start | bytes 1179656 | tf_op jit(solution)/shard_map/ppermute | solution.py:399
  25.7 0.0 collective-permute-done.1
  25.7 2.7 %collective-permute-done.3 = bf16[32,512]{1,0:T(8,128)(2,1)S(1)} collective-permute-done((bf16[32,512]{1,0:T(8,128)(2,1)S(1)}, bf16[32,512]{1,0:T(8,128)(2,1)S(1)}, u32[]{:S(2)}, u32[]{:S(2)}) %collective-permute-start.3) | collective-permute-done | bytes 32800 | tf_op jit(solution)/shard_map/ppermute | solution.py:399
  28.4 0.8 bitcast_select_fusion.2
  29.2 0.8 bitcast_select_fusion.3
  30.0 1.3 collective-permute-start.4
  31.3 2.5 %collective-permute-done.4 = bf16[128,512]{1,0:T(8,128)(2,1)S(1)} collective-permute-done((bf16[128,512]{1,0:T(8,128)(2,1)S(1)}, bf16[128,512]{1,0:T(8,128)(2,1)S(1)}, u32[]{:S(2)}, u32[]{:S(2)}) %collective-permute-start.4) | collective-permute-done | bytes 131104 | tf_op jit(solution)/shard_map/ppermute | solution.py:399
  33.9 0.0 collective-permute-done.2
  33.9 1.5 %collective-permute-start.5 = (bf16[128,512]{1,0:T(8,128)(2,1)S(1)}, bf16[128,512]{1,0:T(8,128)(2,1)S(1)}, u32[]{:S(2)}, u32[]{:S(2)}) collective-permute-start(bf16[128,512]{1,0:T(8,128)(2,1)S(1)} %broadcast_select_fusion.2), channel_id=1, source_target_pairs={{0,16},{1,17},{2,18},{3,19},{4,20},{5,21},{6,22},{7,23},{8,24},{9,... | collective-permute-start | bytes 393224 | tf_op jit(solution)/shard_map/ppermute | solution.py:399
  35.4 1.2 select_select_fusion.3
  36.6 1.3 %collective-permute-done.5 = bf16[128,512]{1,0:T(8,128)(2,1)S(1)} collective-permute-done((bf16[128,512]{1,0:T(8,128)(2,1)S(1)}, bf16[128,512]{1,0:T(8,128)(2,1)S(1)}, u32[]{:S(2)}, u32[]{:S(2)}) %collective-permute-start.5) | collective-permute-done | bytes 131104 | tf_op jit(solution)/shard_map/ppermute | solution.py:399
  37.9 0.1 collective-permute-start.6
  38.0 0.1 pad_maximum_fusion
  38.1 0.0 copy-start
  38.1 1.2 slice.24
  39.3 4.3 %collective-permute-start.9 = (bf16[4,128,512]{2,1,0:T(8,128)(2,1)S(1)}, bf16[4,128,512]{2,1,0:T(8,128)(2,1)S(1)}, u32[]{:S(2)}, u32[]{:S(2)}) collective-permute-start(bf16[4,128,512]{2,1,0:T(8,128)(2,1)S(1)} %slice.25), channel_id=1, source_target_pairs={{0,16},{5,21},{10,26},{15,31},{16,0},{21,5},{26,10},{31,15}} | collective-permute-start | bytes 1572872 | tf_op jit(solution)/shard_map/ppermute | solution.py:399
  43.7 2.3 %collective-permute-start.7 = (bf16[8,128,512]{2,1,0:T(8,128)(2,1)}, bf16[8,128,512]{2,1,0:T(8,128)(2,1)}, u32[]{:S(2)}, u32[]{:S(2)}) collective-permute-start(bf16[8,128,512]{2,1,0:T(8,128)(2,1)} %slice.24), channel_id=1, source_target_pairs={{0,8},{5,13},{10,2},{15,7},{16,24},{21,29},{26,18},{31,23}} | collective-permute-start | bytes 3145736 | tf_op jit(solution)/shard_map/ppermute | solution.py:399
  46.0 0.0 collective-permute-done.6
  46.0 0.7 pad_maximum_fusion.2
  46.8 10.6 %factor.1 = (f32[256,256]{1,0:T(8,128)}, f32[8,256]{1,0:T(8,128)}, f32[8,256]{1,0:T(8,128)}) custom-call(bf16[256,512]{1,0:T(8,128)(2,1)} %bitcast.61), custom_call_target="tpu_custom_call" | custom-call | flops 12000000000 | bytes 1000000 | tf_op jit(solution)/shard_map/factor/pallas_call | solution.py:141
  57.4 0.0 collective-permute-done.9
  57.4 0.2 collective-permute-done.7
  57.6 0.0 copy-done
  57.6 1.1 broadcast_select_fusion.1.refs_0_
  58.7 3.5 %collective-permute-start.8 = (bf16[8,128,512]{2,1,0:T(8,128)(2,1)}, bf16[8,128,512]{2,1,0:T(8,128)(2,1)}, u32[]{:S(2)}, u32[]{:S(2)}) collective-permute-start(bf16[8,128,512]{2,1,0:T(8,128)(2,1)} %broadcast_select_fusion.1.refs_0_), channel_id=1, source_target_pairs={{0,16},{2,18},{5,21},{7,23},{8,24},{10,26},{13,29},{15,31},{16,0},... | collective-permute-start | bytes 3145736 | tf_op jit(solution)/shard_map/ppermute | solution.py:399
  62.2 1.1 pad_maximum_fusion.1
  63.3 5.7 %collective-permute-start.10 = (bf16[2,4,128,512]{3,2,1,0:T(8,128)(2,1)}, bf16[2,4,128,512]{3,2,1,0:T(8,128)(2,1)S(1)}, u32[]{:S(2)}, u32[]{:S(2)}) collective-permute-start(bf16[2,4,128,512]{3,2,1,0:T(8,128)(2,1)} %pad_maximum_fusion.1), channel_id=1, source_target_pairs={{0,8},{5,13},{10,2},{15,7},{16,24},{21,29},{26,18},{31,23}} | collective-permute-start | bytes 3145736 | tf_op jit(solution)/shard_map/ppermute | solution.py:399
  69.0 7.2 %panel_rows.1 = (f32[1536,256]{1,0:T(8,128)}, bf16[1536,768]{1,0:T(8,128)(2,1)}, f32[1536,128]{1,0:T(8,128)}, f32[1536,128]{1,0:T(8,128)}, f32[1536,128]{1,0:T(8,128)}) custom-call(s32[1]{0:T(128)} %bitcast.tau_ref, bf16[1536,512]{1,0:T(8,128)(2,1)} %bitcast.52, bf16[256,512]{1,0:T(8,128)(2,1)} %bitcast.62, f32[256,256]{1,0:T(8,128)} %get-tuple-element.19.t_ref.refs_9_, ...), custom_call_target="tpu_custom_call" | custom-call | flops 9663676416 | bytes 6291456 | tf_op jit(solution)/shard_map/panel_rows/pallas_call | solution.py:219
  76.2 2.3 %collective-permute-start.11 = (bf16[8,128,512]{2,1,0:T(8,128)(2,1)}, bf16[8,128,512]{2,1,0:T(8,128)(2,1)}, u32[]{:S(2)}, u32[]{:S(2)}) collective-permute-start(bf16[8,128,512]{2,1,0:T(8,128)(2,1)} %broadcast_select_fusion.1.refs_0_), channel_id=1, source_target_pairs={{0,4},{2,6},{5,1},{7,3},{8,12},{10,14},{13,9},{15,11},{16,20},{18,... | collective-permute-start | bytes 3145736 | tf_op jit(solution)/shard_map/ppermute | solution.py:399
  78.5 0.0 collective-permute-done.8.refs_1_
  78.5 2.3 %collective-permute-start.12 = (bf16[8,128,512]{2,1,0:T(8,128)(2,1)}, bf16[8,128,512]{2,1,0:T(8,128)(2,1)}, u32[]{:S(2)}, u32[]{:S(2)}) collective-permute-start(bf16[8,128,512]{2,1,0:T(8,128)(2,1)} %collective-permute-done.8.refs_1_), channel_id=1, source_target_pairs={{0,4},{2,6},{5,1},{7,3},{8,12},{10,14},{13,9},{15,11},{16,20},{18,... | collective-permute-start | bytes 3145736 | tf_op jit(solution)/shard_map/ppermute | solution.py:399
  80.8 0.7 collective-permute-done.10
  81.5 0.1 broadcast_select_fusion
  81.7 0.1 slice_bitcast_fusion
  81.7 0.0 copy-start.1
  81.7 0.0 copy-start.2
  81.8 1.3 %collective-permute-start.13 = (bf16[4,128,512]{2,1,0:T(8,128)(2,1)S(1)}, bf16[4,128,512]{2,1,0:T(8,128)(2,1)S(1)}, u32[]{:S(2)}, u32[]{:S(2)}) collective-permute-start(bf16[4,128,512]{2,1,0:T(8,128)(2,1)S(1)} %get-tuple-element.29.refs_2_), channel_id=1, source_target_pairs={{0,4},{2,6},{5,1},{7,3},{8,12},{10,14},{13,9},{15,11},{16,20},{18,... | collective-permute-start | bytes 1572872 | tf_op jit(solution)/shard_map/ppermute | solution.py:399
  83.1 1.5 %collective-permute-start.14 = (bf16[4,128,512]{2,1,0:T(8,128)(2,1)S(1)}, bf16[4,128,512]{2,1,0:T(8,128)(2,1)S(1)}, u32[]{:S(2)}, u32[]{:S(2)}) collective-permute-start(bf16[4,128,512]{2,1,0:T(8,128)(2,1)S(1)} %get-tuple-element.30.refs_3_), channel_id=1, source_target_pairs={{0,4},{2,6},{5,1},{7,3},{8,12},{10,14},{13,9},{15,11},{16,20},{18,... | collective-permute-start | bytes 1572872 | tf_op jit(solution)/shard_map/ppermute | solution.py:399
  84.6 0.6 stack.36.info
  85.2 0.0 collective-permute-done.13.refs_6_
  85.2 0.0 copy-start.3
  85.2 0.7 collective-permute-done.14.refs_7_
  85.9 0.0 copy-start.4
  85.9 0.0 collective-permute-done.11.refs_4_
  85.9 0.0 collective-permute-done.12.refs_5_
  85.9 0.0 copy-done.1
  85.9 0.0 copy-done.2
  85.9 0.1 copy-done.3
  86.0 0.7 copy-done.4
  86.7 42.9 %trailing.1 = f32[1536,24,128]{2,1,0:T(8,128)} custom-call(s32[5]{0:T(128)} %stack.36.info, bf16[8,128,512]{2,1,0:T(8,128)(2,1)} %broadcast_select_fusion.1.refs_0_, bf16[8,128,512]{2,1,0:T(8,128)(2,1)} %collective-permute-done.8.refs_1_, bf16[4,128,512]{2,1,0:T(8,128)(2,1)} %copy-done.2, bf16[4,128,512]{2,1,0:T(8,128)(2,1)} %copy-done.1, ...), custom_call_target="tpu_custom_call" | custom-call | flops 48318382080 | bytes 18874368 | tf_op jit(solution)/shard_map/trailing/pallas_call | solution.py:357
  (6 shorter events, 0.1 us)
Async XLA Ops:
  0.6 15.3 %collective-permute-start = (bf16[12,32,512]{2,1,0:T(8,128)(2,1)}, bf16[12,32,512]{2,1,0:T(8,128)(2,1)S(1)}, u32[]{:S(2)}, u32[]{:S(2)}) collective-permute-start(bf16[12,32,512]{2,1,0:T(8,128)(2,1)} %bitcast.59), channel_id=1, source_target_pairs={{0,1},{1,2},{2,3},{3,0},{4,5},{5,6},{6,7},{7,4},{8,9},{9,10},{10,1... | collective-permute-start | bytes 1179656 | tf_op jit(solution)/shard_map/ppermute | solution.py:399
  3.7 22.0 %collective-permute-start.1 = (bf16[12,32,512]{2,1,0:T(8,128)(2,1)}, bf16[12,32,512]{2,1,0:T(8,128)(2,1)S(1)}, u32[]{:S(2)}, u32[]{:S(2)}) collective-permute-start(bf16[12,32,512]{2,1,0:T(8,128)(2,1)} %bitcast.60), channel_id=1, source_target_pairs={{0,3},{1,0},{2,1},{3,2},{4,7},{5,4},{6,5},{7,6},{8,11},{9,8},{10,9... | collective-permute-start | bytes 1179656 | tf_op jit(solution)/shard_map/ppermute | solution.py:399
  15.9 12.5 %collective-permute-start.3 = (bf16[32,512]{1,0:T(8,128)(2,1)S(1)}, bf16[32,512]{1,0:T(8,128)(2,1)S(1)}, u32[]{:S(2)}, u32[]{:S(2)}) collective-permute-start(bf16[32,512]{1,0:T(8,128)(2,1)S(1)} %slice_bitcast_fusion.3), channel_id=1, source_target_pairs={{0,1},{1,2},{2,3},{3,0},{4,5},{5,6},{6,7},{7,4}} | collective-permute-start | bytes 98312 | tf_op jit(solution)/shard_map/ppermute | solution.py:399
  17.9 15.9 %collective-permute-start.2 = (bf16[12,32,512]{2,1,0:T(8,128)(2,1)S(1)}, bf16[12,32,512]{2,1,0:T(8,128)(2,1)S(1)}, u32[]{:S(2)}, u32[]{:S(2)}) collective-permute-start(bf16[12,32,512]{2,1,0:T(8,128)(2,1)S(1)} %collective-permute-done), channel_id=1, source_target_pairs={{0,1},{1,2},{2,3},{3,0},{4,5},{5,6},{6,7},{7,4},{8,9},{9,10},{10,1... | collective-permute-start | bytes 1179656 | tf_op jit(solution)/shard_map/ppermute | solution.py:399
  30.0 3.8 %collective-permute-start.4 = (bf16[128,512]{1,0:T(8,128)(2,1)S(1)}, bf16[128,512]{1,0:T(8,128)(2,1)S(1)}, u32[]{:S(2)}, u32[]{:S(2)}) collective-permute-start(bf16[128,512]{1,0:T(8,128)(2,1)S(1)} %pad_maximum_fusion.3), channel_id=1, source_target_pairs={{0,8},{1,9},{2,10},{3,11},{4,12},{5,13},{6,14},{7,15}} | collective-permute-start | bytes 393224 | tf_op jit(solution)/shard_map/ppermute | solution.py:399
  33.9 4.0 %collective-permute-start.5 = (bf16[128,512]{1,0:T(8,128)(2,1)S(1)}, bf16[128,512]{1,0:T(8,128)(2,1)S(1)}, u32[]{:S(2)}, u32[]{:S(2)}) collective-permute-start(bf16[128,512]{1,0:T(8,128)(2,1)S(1)} %broadcast_select_fusion.2), channel_id=1, source_target_pairs={{0,16},{1,17},{2,18},{3,19},{4,20},{5,21},{6,22},{7,23},{8,24},{9,... | collective-permute-start | bytes 393224 | tf_op jit(solution)/shard_map/ppermute | solution.py:399
  37.9 8.1 %collective-permute-start.6 = (bf16[1,128,512]{2,1,0:T(8,128)(2,1)S(1)}, bf16[1,128,512]{2,1,0:T(8,128)(2,1)S(1)}, u32[]{:S(2)}, u32[]{:S(2)}) collective-permute-start(bf16[1,128,512]{2,1,0:T(8,128)(2,1)S(1)} %select_bitcast_fusion), channel_id=1, source_target_pairs={{0,4},{1,5},{2,6},{3,7},{4,0},{5,1},{6,2},{7,3},{8,12},{9,13},{10,... | collective-permute-start | bytes 393224 | tf_op jit(solution)/shard_map/ppermute | solution.py:399
  38.1 19.5 %copy-start = (bf16[12,128,512]{2,1,0:T(8,128)(2,1)}, bf16[12,128,512]{2,1,0:T(8,128)(2,1)S(1)}, u32[]{:S(2)}) copy-start(bf16[12,128,512]{2,1,0:T(8,128)(2,1)S(1)} %pad_maximum_fusion) | copy-start | bytes 4718596
  39.3 18.1 %collective-permute-start.9 = (bf16[4,128,512]{2,1,0:T(8,128)(2,1)S(1)}, bf16[4,128,512]{2,1,0:T(8,128)(2,1)S(1)}, u32[]{:S(2)}, u32[]{:S(2)}) collective-permute-start(bf16[4,128,512]{2,1,0:T(8,128)(2,1)S(1)} %slice.25), channel_id=1, source_target_pairs={{0,16},{5,21},{10,26},{15,31},{16,0},{21,5},{26,10},{31,15}} | collective-permute-start | bytes 1572872 | tf_op jit(solution)/shard_map/ppermute | solution.py:399
  43.7 13.9 %collective-permute-start.7 = (bf16[8,128,512]{2,1,0:T(8,128)(2,1)}, bf16[8,128,512]{2,1,0:T(8,128)(2,1)}, u32[]{:S(2)}, u32[]{:S(2)}) collective-permute-start(bf16[8,128,512]{2,1,0:T(8,128)(2,1)} %slice.24), channel_id=1, source_target_pairs={{0,8},{5,13},{10,2},{15,7},{16,24},{21,29},{26,18},{31,23}} | collective-permute-start | bytes 3145736 | tf_op jit(solution)/shard_map/ppermute | solution.py:399
  58.7 19.8 %collective-permute-start.8 = (bf16[8,128,512]{2,1,0:T(8,128)(2,1)}, bf16[8,128,512]{2,1,0:T(8,128)(2,1)}, u32[]{:S(2)}, u32[]{:S(2)}) collective-permute-start(bf16[8,128,512]{2,1,0:T(8,128)(2,1)} %broadcast_select_fusion.1.refs_0_), channel_id=1, source_target_pairs={{0,16},{2,18},{5,21},{7,23},{8,24},{10,26},{13,29},{15,31},{16,0},... | collective-permute-start | bytes 3145736 | tf_op jit(solution)/shard_map/ppermute | solution.py:399
  63.3 18.2 %collective-permute-start.10 = (bf16[2,4,128,512]{3,2,1,0:T(8,128)(2,1)}, bf16[2,4,128,512]{3,2,1,0:T(8,128)(2,1)S(1)}, u32[]{:S(2)}, u32[]{:S(2)}) collective-permute-start(bf16[2,4,128,512]{3,2,1,0:T(8,128)(2,1)} %pad_maximum_fusion.1), channel_id=1, source_target_pairs={{0,8},{5,13},{10,2},{15,7},{16,24},{21,29},{26,18},{31,23}} | collective-permute-start | bytes 3145736 | tf_op jit(solution)/shard_map/ppermute | solution.py:399
  76.2 9.7 %collective-permute-start.11 = (bf16[8,128,512]{2,1,0:T(8,128)(2,1)}, bf16[8,128,512]{2,1,0:T(8,128)(2,1)}, u32[]{:S(2)}, u32[]{:S(2)}) collective-permute-start(bf16[8,128,512]{2,1,0:T(8,128)(2,1)} %broadcast_select_fusion.1.refs_0_), channel_id=1, source_target_pairs={{0,4},{2,6},{5,1},{7,3},{8,12},{10,14},{13,9},{15,11},{16,20},{18,... | collective-permute-start | bytes 3145736 | tf_op jit(solution)/shard_map/ppermute | solution.py:399
  78.5 7.4 %collective-permute-start.12 = (bf16[8,128,512]{2,1,0:T(8,128)(2,1)}, bf16[8,128,512]{2,1,0:T(8,128)(2,1)}, u32[]{:S(2)}, u32[]{:S(2)}) collective-permute-start(bf16[8,128,512]{2,1,0:T(8,128)(2,1)} %collective-permute-done.8.refs_1_), channel_id=1, source_target_pairs={{0,4},{2,6},{5,1},{7,3},{8,12},{10,14},{13,9},{15,11},{16,20},{18,... | collective-permute-start | bytes 3145736 | tf_op jit(solution)/shard_map/ppermute | solution.py:399
  81.7 4.2 %copy-start.1 = (bf16[4,128,512]{2,1,0:T(8,128)(2,1)}, bf16[4,128,512]{2,1,0:T(8,128)(2,1)S(1)}, u32[]{:S(2)}) copy-start(bf16[4,128,512]{2,1,0:T(8,128)(2,1)S(1)} %get-tuple-element.30.refs_3_) | copy-start | bytes 1572868
  81.7 4.2 %copy-start.2 = (bf16[4,128,512]{2,1,0:T(8,128)(2,1)}, bf16[4,128,512]{2,1,0:T(8,128)(2,1)S(1)}, u32[]{:S(2)}) copy-start(bf16[4,128,512]{2,1,0:T(8,128)(2,1)S(1)} %get-tuple-element.29.refs_2_) | copy-start | bytes 1572868
  81.8 3.5 %collective-permute-start.13 = (bf16[4,128,512]{2,1,0:T(8,128)(2,1)S(1)}, bf16[4,128,512]{2,1,0:T(8,128)(2,1)S(1)}, u32[]{:S(2)}, u32[]{:S(2)}) collective-permute-start(bf16[4,128,512]{2,1,0:T(8,128)(2,1)S(1)} %get-tuple-element.29.refs_2_), channel_id=1, source_target_pairs={{0,4},{2,6},{5,1},{7,3},{8,12},{10,14},{13,9},{15,11},{16,20},{18,... | collective-permute-start | bytes 1572872 | tf_op jit(solution)/shard_map/ppermute | solution.py:399
  83.1 2.8 %collective-permute-start.14 = (bf16[4,128,512]{2,1,0:T(8,128)(2,1)S(1)}, bf16[4,128,512]{2,1,0:T(8,128)(2,1)S(1)}, u32[]{:S(2)}, u32[]{:S(2)}) collective-permute-start(bf16[4,128,512]{2,1,0:T(8,128)(2,1)S(1)} %get-tuple-element.30.refs_3_), channel_id=1, source_target_pairs={{0,4},{2,6},{5,1},{7,3},{8,12},{10,14},{13,9},{15,11},{16,20},{18,... | collective-permute-start | bytes 1572872 | tf_op jit(solution)/shard_map/ppermute | solution.py:399
  85.2 0.8 copy-start.3
  85.9 0.8 copy-start.4

commit v4 on v3

--- a/solution.py
+++ b/solution.py
@@ -250,14 +250,17 @@
     size = k_ref.shape[0]
 
     def load(arrays):
+        views = []
+        for src in arrays:
+            views += [src] if len(src.shape) == 3 else [src.at[e] for e in range(src.shape[0])]
         base = 0
-        for k in range(0, len(arrays), step_tiles):
-            for tile in range(arrays[k].shape[0]):
-                for entry, src in enumerate(arrays[k : k + step_tiles]):
+        for k in range(0, len(views), step_tiles):
+            for tile in range(views[k].shape[0]):
+                for entry, src in enumerate(views[k : k + step_tiles]):
                     at = ((base + tile) * step_tiles + (info[4] ^ entry)) * TILE
                     to = xc.at[pl.ds(pl.multiple_of(at, TILE), TILE)]
                     pltpu.make_async_copy(src.at[tile], to, sem.at[at // size]).start()
-            base += arrays[k].shape[0]
+            base += views[k].shape[0]
 
     def columns(b):
         rows = pl.ds(pl.multiple_of(b * size, size), size)
@@ -447,7 +450,7 @@
                 own = (self.r ^ self.c) & (1 << bit) == 0
                 data = parts[0] if len(parts) == 1 else jnp.stack(parts)
                 data = jnp.where(own, data, self.flip(data, bit, holds))
-                parts = [data] if len(parts) == 1 else list(data)
+                parts = [data]
                 mask[0] &= ~(1 << bit)
             return parts
 
@@ -484,7 +487,7 @@
     tau = lambda i: jnp.where(i < PANEL // tile, i, -1)
     low, *row_args = panel_rows(x_rows, *panel_args, tau(r).astype(jnp.int32).reshape(1))
 
-    cut = tiles_r * 2 // 3 if tiles_r % 3 == 0 else tiles_r
+    cut = tiles_r * 3 // 4 if tiles_r % 12 == 0 else tiles_r
     pieces = [rows[:cut], rows[cut:]] if cut < tiles_r else [rows]
     mine, got = [], []
     for k, piece in enumerate(pieces):

time: 130 us -> 128 us (0.985)
  other arithmetic: 5.94 us -> 3.99 us
    ppermute x15 -> x14, starting transfers between devices: 41 us -> 40 us  [send(): return lax.ppermute(value, ('row', 'col'), pairs)]
    ppermute x15 -> x14, waiting for transfers between devices: 18.2 us -> 18.9 us  [send(): return lax.ppermute(value, ('row', 'col'), pairs)]
  transfers between devices with their start and end apart: 15 -> 14, of which waited for: 7 -> 6; matrix products, arithmetic and copies ran while one was open for 5% -> 4% of each run, Pallas kernels for 14% -> 14%
where the time goes in v4:
time: 128 us; the launch traced here: 127 us
  Pallas kernels  61.1 us (48%)
  starting transfers between devices  40 us (31%)
  waiting for transfers between devices  18.9 us (15%)
  other arithmetic  3.99 us (3%)
  local copies, waits for them, and re-layouts  1.62 us (1%)
    pallas_call x1, Pallas kernels, trailing(): pl.pallas_call(functools.partial(trailing_kernel, rb, tb, blocks, steps,...  43.2 us
    ppermute x14, starting transfers between devices, send(): return lax.ppermute(value, ('row', 'col'), pairs)  40 us
    ppermute x14, waiting for transfers between devices, send(): return lax.ppermute(value, ('row', 'col'), pairs)  18.9 us
    pallas_call x1, Pallas kernels, factor(): pl.pallas_call(factor_kernel, out_shape=[full, vec, vec], scratch_shapes=...  10.6 us
    pallas_call x1, Pallas kernels, panel_rows(): pl.pallas_call(panel_kernel, grid=(m // block,), in_specs=[pl.BlockSpec(m...  7.25 us
    select_n x3, other arithmetic, in_order(): jnp.where(away == 0, own, jnp.where(away == 3, before, jnp.where(away ==...  2.74 us
  transfers between devices with their start and end apart: 14, of which 6 were waited for; matrix products, arithmetic and copies ran while one was open for 4% of the time, Pallas kernels for 14%

profile of v4, /device:TPU:0, one launch (start us, length us, event | category | flops | bytes accessed | tf_op | source)
XLA Modules:
  0.0 126.7 jit_solution(9216466341833371173)
XLA Ops:
  0.6 3.1 %collective-permute-start = (bf16[12,32,512]{2,1,0:T(8,128)(2,1)}, bf16[12,32,512]{2,1,0:T(8,128)(2,1)S(1)}, u32[]{:S(2)}, u32[]{:S(2)}) collective-permute-start(bf16[12,32,512]{2,1,0:T(8,128)(2,1)} %bitcast.55), channel_id=1, source_target_pairs={{0,1},{1,2},{2,3},{3,0},{4,5},{5,6},{6,7},{7,4},{8,9},{9,10},{10,1... | collective-permute-start | bytes 1179656 | tf_op jit(solution)/shard_map/ppermute | solution.py:402
  3.7 2.1 %collective-permute-start.1 = (bf16[12,32,512]{2,1,0:T(8,128)(2,1)}, bf16[12,32,512]{2,1,0:T(8,128)(2,1)S(1)}, u32[]{:S(2)}, u32[]{:S(2)}) collective-permute-start(bf16[12,32,512]{2,1,0:T(8,128)(2,1)} %bitcast.56), channel_id=1, source_target_pairs={{0,3},{1,0},{2,1},{3,2},{4,7},{5,4},{6,5},{7,6},{8,11},{9,8},{10,9... | collective-permute-start | bytes 1179656 | tf_op jit(solution)/shard_map/ppermute | solution.py:402
  5.8 10.1 %collective-permute-done = bf16[12,32,512]{2,1,0:T(8,128)(2,1)S(1)} collective-permute-done((bf16[12,32,512]{2,1,0:T(8,128)(2,1)}, bf16[12,32,512]{2,1,0:T(8,128)(2,1)S(1)}, u32[]{:S(2)}, u32[]{:S(2)}) %collective-permute-start) | collective-permute-done | bytes 393248 | tf_op jit(solution)/shard_map/ppermute | solution.py:402
  15.9 1.9 %collective-permute-start.3 = (bf16[32,512]{1,0:T(8,128)(2,1)S(1)}, bf16[32,512]{1,0:T(8,128)(2,1)S(1)}, u32[]{:S(2)}, u32[]{:S(2)}) collective-permute-start(bf16[32,512]{1,0:T(8,128)(2,1)S(1)} %slice_bitcast_fusion.1), channel_id=1, source_target_pairs={{0,1},{1,2},{2,3},{3,0},{4,5},{5,6},{6,7},{7,4}} | collective-permute-start | bytes 98312 | tf_op jit(solution)/shard_map/ppermute | solution.py:402
  17.9 7.8 %collective-permute-start.2 = (bf16[12,32,512]{2,1,0:T(8,128)(2,1)S(1)}, bf16[12,32,512]{2,1,0:T(8,128)(2,1)S(1)}, u32[]{:S(2)}, u32[]{:S(2)}) collective-permute-start(bf16[12,32,512]{2,1,0:T(8,128)(2,1)S(1)} %collective-permute-done), channel_id=1, source_target_pairs={{0,1},{1,2},{2,3},{3,0},{4,5},{5,6},{6,7},{7,4},{8,9},{9,10},{10,1... | collective-permute-start | bytes 1179656 | tf_op jit(solution)/shard_map/ppermute | solution.py:402
  25.7 0.0 collective-permute-done.1
  25.7 2.7 %collective-permute-done.3 = bf16[32,512]{1,0:T(8,128)(2,1)S(1)} collective-permute-done((bf16[32,512]{1,0:T(8,128)(2,1)S(1)}, bf16[32,512]{1,0:T(8,128)(2,1)S(1)}, u32[]{:S(2)}, u32[]{:S(2)}) %collective-permute-start.3) | collective-permute-done | bytes 32800 | tf_op jit(solution)/shard_map/ppermute | solution.py:402
  28.4 0.8 bitcast_select_fusion.2
  29.2 0.8 bitcast_select_fusion.3
  30.0 1.3 %collective-permute-start.4 = (bf16[128,512]{1,0:T(8,128)(2,1)S(1)}, bf16[128,512]{1,0:T(8,128)(2,1)S(1)}, u32[]{:S(2)}, u32[]{:S(2)}) collective-permute-start(bf16[128,512]{1,0:T(8,128)(2,1)S(1)} %pad_maximum_fusion.3), channel_id=1, source_target_pairs={{0,8},{1,9},{2,10},{3,11},{4,12},{5,13},{6,14},{7,15}} | collective-permute-start | bytes 393224 | tf_op jit(solution)/shard_map/ppermute | solution.py:402
  31.3 2.5 %collective-permute-done.4 = bf16[128,512]{1,0:T(8,128)(2,1)S(1)} collective-permute-done((bf16[128,512]{1,0:T(8,128)(2,1)S(1)}, bf16[128,512]{1,0:T(8,128)(2,1)S(1)}, u32[]{:S(2)}, u32[]{:S(2)}) %collective-permute-start.4) | collective-permute-done | bytes 131104 | tf_op jit(solution)/shard_map/ppermute | solution.py:402
  33.9 0.0 collective-permute-done.2
  33.9 1.5 %collective-permute-start.5 = (bf16[128,512]{1,0:T(8,128)(2,1)S(1)}, bf16[128,512]{1,0:T(8,128)(2,1)S(1)}, u32[]{:S(2)}, u32[]{:S(2)}) collective-permute-start(bf16[128,512]{1,0:T(8,128)(2,1)S(1)} %broadcast_select_fusion.2), channel_id=1, source_target_pairs={{0,16},{1,17},{2,18},{3,19},{4,20},{5,21},{6,22},{7,23},{8,24},{9,... | collective-permute-start | bytes 393224 | tf_op jit(solution)/shard_map/ppermute | solution.py:402
  35.4 1.2 select_select_fusion.3
  36.6 1.3 %collective-permute-done.5 = bf16[128,512]{1,0:T(8,128)(2,1)S(1)} collective-permute-done((bf16[128,512]{1,0:T(8,128)(2,1)S(1)}, bf16[128,512]{1,0:T(8,128)(2,1)S(1)}, u32[]{:S(2)}, u32[]{:S(2)}) %collective-permute-start.5) | collective-permute-done | bytes 131104 | tf_op jit(solution)/shard_map/ppermute | solution.py:402
  37.9 0.1 collective-permute-start.6
  38.0 0.1 pad_maximum_fusion
  38.1 0.0 copy-start
  38.1 0.1 slice.24
  38.2 4.4 %collective-permute-start.9 = (bf16[3,128,512]{2,1,0:T(8,128)(2,1)S(1)}, bf16[3,128,512]{2,1,0:T(8,128)(2,1)S(1)}, u32[]{:S(2)}, u32[]{:S(2)}) collective-permute-start(bf16[3,128,512]{2,1,0:T(8,128)(2,1)S(1)} %slice.25), channel_id=1, source_target_pairs={{0,16},{5,21},{10,26},{15,31},{16,0},{21,5},{26,10},{31,15}} | collective-permute-start | bytes 1179656 | tf_op jit(solution)/shard_map/ppermute | solution.py:402
  42.6 2.3 %collective-permute-start.7 = (bf16[9,128,512]{2,1,0:T(8,128)(2,1)S(1)}, bf16[9,128,512]{2,1,0:T(8,128)(2,1)}, u32[]{:S(2)}, u32[]{:S(2)}) collective-permute-start(bf16[9,128,512]{2,1,0:T(8,128)(2,1)S(1)} %slice.24), channel_id=1, source_target_pairs={{0,8},{5,13},{10,2},{15,7},{16,24},{21,29},{26,18},{31,23}} | collective-permute-start | bytes 3538952 | tf_op jit(solution)/shard_map/ppermute | solution.py:402
  44.9 0.0 collective-permute-done.6
  44.9 0.8 pad_maximum_fusion.2
  45.7 10.6 %factor.1 = (f32[256,256]{1,0:T(8,128)}, f32[8,256]{1,0:T(8,128)}, f32[8,256]{1,0:T(8,128)}) custom-call(bf16[256,512]{1,0:T(8,128)(2,1)} %bitcast.57), custom_call_target="tpu_custom_call" | custom-call | flops 12000000000 | bytes 1000000 | tf_op jit(solution)/shard_map/factor/pallas_call | solution.py:141
  56.3 1.2 collective-permute-done.7
  57.6 0.0 copy-done
  57.6 0.1 broadcast_select_fusion.refs_0_
  57.7 0.0 copy-start.1
  57.7 3.5 %collective-permute-start.8 = (bf16[9,128,512]{2,1,0:T(8,128)(2,1)S(1)}, bf16[9,128,512]{2,1,0:T(8,128)(2,1)}, u32[]{:S(2)}, u32[]{:S(2)}) collective-permute-start(bf16[9,128,512]{2,1,0:T(8,128)(2,1)S(1)} %broadcast_select_fusion.refs_0_), channel_id=1, source_target_pairs={{0,16},{2,18},{5,21},{7,23},{8,24},{10,26},{13,29},{15,31},{16,0},... | collective-permute-start | bytes 3538952 | tf_op jit(solution)/shard_map/ppermute | solution.py:402
  61.3 0.0 collective-permute-done.9
  61.3 0.1 pad_maximum_fusion.1
  61.4 5.8 %collective-permute-start.10 = (bf16[2,3,128,512]{3,2,1,0:T(8,128)(2,1)S(1)}, bf16[2,3,128,512]{3,2,1,0:T(8,128)(2,1)S(1)}, u32[]{:S(2)}, u32[]{:S(2)}) collective-permute-start(bf16[2,3,128,512]{3,2,1,0:T(8,128)(2,1)S(1)} %pad_maximum_fusion.1), channel_id=1, source_target_pairs={{0,8},{5,13},{10,2},{15,7},{16,24},{21,29},{26,18},{31,23}} | collective-permute-start | bytes 2359304 | tf_op jit(solution)/shard_map/ppermute | solution.py:402
  67.2 7.3 %panel_rows.1 = (f32[1536,256]{1,0:T(8,128)}, bf16[1536,768]{1,0:T(8,128)(2,1)}, f32[1536,128]{1,0:T(8,128)}, f32[1536,128]{1,0:T(8,128)}, f32[1536,128]{1,0:T(8,128)}) custom-call(s32[1]{0:T(128)} %bitcast.tau_ref, bf16[1536,512]{1,0:T(8,128)(2,1)} %bitcast.48, bf16[256,512]{1,0:T(8,128)(2,1)} %bitcast.58, f32[256,256]{1,0:T(8,128)} %get-tuple-element.18.t_ref.refs_7_, ...), custom_call_target="tpu_custom_call" | custom-call | flops 9663676416 | bytes 6291456 | tf_op jit(solution)/shard_map/panel_rows/pallas_call | solution.py:219
  74.4 0.0 copy-done.1
  74.4 2.3 %collective-permute-start.11 = (bf16[9,128,512]{2,1,0:T(8,128)(2,1)S(1)}, bf16[9,128,512]{2,1,0:T(8,128)(2,1)}, u32[]{:S(2)}, u32[]{:S(2)}) collective-permute-start(bf16[9,128,512]{2,1,0:T(8,128)(2,1)S(1)} %broadcast_select_fusion.refs_0_), channel_id=1, source_target_pairs={{0,4},{2,6},{5,1},{7,3},{8,12},{10,14},{13,9},{15,11},{16,20},{18,... | collective-permute-start | bytes 3538952 | tf_op jit(solution)/shard_map/ppermute | solution.py:402
  76.8 0.0 collective-permute-done.8.refs_1_
  76.8 2.4 %collective-permute-start.12 = (bf16[9,128,512]{2,1,0:T(8,128)(2,1)}, bf16[9,128,512]{2,1,0:T(8,128)(2,1)}, u32[]{:S(2)}, u32[]{:S(2)}) collective-permute-start(bf16[9,128,512]{2,1,0:T(8,128)(2,1)} %collective-permute-done.8.refs_1_), channel_id=1, source_target_pairs={{0,4},{2,6},{5,1},{7,3},{8,12},{10,14},{13,9},{15,11},{16,20},{18,... | collective-permute-start | bytes 3538952 | tf_op jit(solution)/shard_map/ppermute | solution.py:402
  79.2 0.0 collective-permute-done.10
  79.2 0.1 broadcast_select_fusion.1.refs_2_
  79.3 0.0 copy-start.2
  79.3 1.5 %collective-permute-start.13 = (bf16[2,3,128,512]{3,2,1,0:T(8,128)(2,1)S(1)}, bf16[2,3,128,512]{3,2,1,0:T(8,128)(2,1)S(1)}, u32[]{:S(2)}, u32[]{:S(2)}) collective-permute-start(bf16[2,3,128,512]{3,2,1,0:T(8,128)(2,1)S(1)} %broadcast_select_fusion.1.refs_2_), channel_id=1, source_target_pairs={{0,4},{2,6},{5,1},{7,3},{8,12},{10,14},{13,9},{15,11},{16,20},{18,... | collective-permute-start | bytes 2359304 | tf_op jit(solution)/shard_map/ppermute | solution.py:402
  80.9 0.6 stack.36.info
  81.5 1.0 collective-permute-done.13.refs_5_
  82.5 0.0 copy-start.3
  82.5 0.0 collective-permute-done.11.refs_3_
  82.5 0.0 collective-permute-done.12.refs_4_
  82.5 0.0 copy-done.2
  82.5 0.9 copy-done.3
  83.4 43.2 %trailing.1 = f32[1536,24,128]{2,1,0:T(8,128)} custom-call(s32[5]{0:T(128)} %stack.36.info, bf16[9,128,512]{2,1,0:T(8,128)(2,1)} %copy-done.1, bf16[9,128,512]{2,1,0:T(8,128)(2,1)} %collective-permute-done.8.refs_1_, bf16[2,3,128,512]{3,2,1,0:T(8,128)(2,1)} %copy-done.2, bf16[9,128,512]{2,1,0:T(8,128)(2,1)} %collective-permute-done.11.refs_3_, ...), custom_call_target="tpu_custom_call" | custom-call | flops 48318382080 | bytes 18874368 | tf_op jit(solution)/shard_map/trailing/pallas_call | solution.py:360
  (6 shorter events, 0.1 us)
Async XLA Ops:
  0.6 15.3 %collective-permute-start = (bf16[12,32,512]{2,1,0:T(8,128)(2,1)}, bf16[12,32,512]{2,1,0:T(8,128)(2,1)S(1)}, u32[]{:S(2)}, u32[]{:S(2)}) collective-permute-start(bf16[12,32,512]{2,1,0:T(8,128)(2,1)} %bitcast.55), channel_id=1, source_target_pairs={{0,1},{1,2},{2,3},{3,0},{4,5},{5,6},{6,7},{7,4},{8,9},{9,10},{10,1... | collective-permute-start | bytes 1179656 | tf_op jit(solution)/shard_map/ppermute | solution.py:402
  3.7 22.0 %collective-permute-start.1 = (bf16[12,32,512]{2,1,0:T(8,128)(2,1)}, bf16[12,32,512]{2,1,0:T(8,128)(2,1)S(1)}, u32[]{:S(2)}, u32[]{:S(2)}) collective-permute-start(bf16[12,32,512]{2,1,0:T(8,128)(2,1)} %bitcast.56), channel_id=1, source_target_pairs={{0,3},{1,0},{2,1},{3,2},{4,7},{5,4},{6,5},{7,6},{8,11},{9,8},{10,9... | collective-permute-start | bytes 1179656 | tf_op jit(solution)/shard_map/ppermute | solution.py:402
  15.9 12.5 %collective-permute-start.3 = (bf16[32,512]{1,0:T(8,128)(2,1)S(1)}, bf16[32,512]{1,0:T(8,128)(2,1)S(1)}, u32[]{:S(2)}, u32[]{:S(2)}) collective-permute-start(bf16[32,512]{1,0:T(8,128)(2,1)S(1)} %slice_bitcast_fusion.1), channel_id=1, source_target_pairs={{0,1},{1,2},{2,3},{3,0},{4,5},{5,6},{6,7},{7,4}} | collective-permute-start | bytes 98312 | tf_op jit(solution)/shard_map/ppermute | solution.py:402
  17.9 15.9 %collective-permute-start.2 = (bf16[12,32,512]{2,1,0:T(8,128)(2,1)S(1)}, bf16[12,32,512]{2,1,0:T(8,128)(2,1)S(1)}, u32[]{:S(2)}, u32[]{:S(2)}) collective-permute-start(bf16[12,32,512]{2,1,0:T(8,128)(2,1)S(1)} %collective-permute-done), channel_id=1, source_target_pairs={{0,1},{1,2},{2,3},{3,0},{4,5},{5,6},{6,7},{7,4},{8,9},{9,10},{10,1... | collective-permute-start | bytes 1179656 | tf_op jit(solution)/shard_map/ppermute | solution.py:402
  30.0 3.8 %collective-permute-start.4 = (bf16[128,512]{1,0:T(8,128)(2,1)S(1)}, bf16[128,512]{1,0:T(8,128)(2,1)S(1)}, u32[]{:S(2)}, u32[]{:S(2)}) collective-permute-start(bf16[128,512]{1,0:T(8,128)(2,1)S(1)} %pad_maximum_fusion.3), channel_id=1, source_target_pairs={{0,8},{1,9},{2,10},{3,11},{4,12},{5,13},{6,14},{7,15}} | collective-permute-start | bytes 393224 | tf_op jit(solution)/shard_map/ppermute | solution.py:402
  33.9 4.0 %collective-permute-start.5 = (bf16[128,512]{1,0:T(8,128)(2,1)S(1)}, bf16[128,512]{1,0:T(8,128)(2,1)S(1)}, u32[]{:S(2)}, u32[]{:S(2)}) collective-permute-start(bf16[128,512]{1,0:T(8,128)(2,1)S(1)} %broadcast_select_fusion.2), channel_id=1, source_target_pairs={{0,16},{1,17},{2,18},{3,19},{4,20},{5,21},{6,22},{7,23},{8,24},{9,... | collective-permute-start | bytes 393224 | tf_op jit(solution)/shard_map/ppermute | solution.py:402
  37.9 7.0 %collective-permute-start.6 = (bf16[1,128,512]{2,1,0:T(8,128)(2,1)S(1)}, bf16[1,128,512]{2,1,0:T(8,128)(2,1)S(1)}, u32[]{:S(2)}, u32[]{:S(2)}) collective-permute-start(bf16[1,128,512]{2,1,0:T(8,128)(2,1)S(1)} %select_bitcast_fusion), channel_id=1, source_target_pairs={{0,4},{1,5},{2,6},{3,7},{4,0},{5,1},{6,2},{7,3},{8,12},{9,13},{10,... | collective-permute-start | bytes 393224 | tf_op jit(solution)/shard_map/ppermute | solution.py:402
  38.1 19.5 %copy-start = (bf16[12,128,512]{2,1,0:T(8,128)(2,1)}, bf16[12,128,512]{2,1,0:T(8,128)(2,1)S(1)}, u32[]{:S(2)}) copy-start(bf16[12,128,512]{2,1,0:T(8,128)(2,1)S(1)} %pad_maximum_fusion) | copy-start | bytes 4718596
  38.2 23.1 %collective-permute-start.9 = (bf16[3,128,512]{2,1,0:T(8,128)(2,1)S(1)}, bf16[3,128,512]{2,1,0:T(8,128)(2,1)S(1)}, u32[]{:S(2)}, u32[]{:S(2)}) collective-permute-start(bf16[3,128,512]{2,1,0:T(8,128)(2,1)S(1)} %slice.25), channel_id=1, source_target_pairs={{0,16},{5,21},{10,26},{15,31},{16,0},{21,5},{26,10},{31,15}} | collective-permute-start | bytes 1179656 | tf_op jit(solution)/shard_map/ppermute | solution.py:402
  42.6 15.0 %collective-permute-start.7 = (bf16[9,128,512]{2,1,0:T(8,128)(2,1)S(1)}, bf16[9,128,512]{2,1,0:T(8,128)(2,1)}, u32[]{:S(2)}, u32[]{:S(2)}) collective-permute-start(bf16[9,128,512]{2,1,0:T(8,128)(2,1)S(1)} %slice.24), channel_id=1, source_target_pairs={{0,8},{5,13},{10,2},{15,7},{16,24},{21,29},{26,18},{31,23}} | collective-permute-start | bytes 3538952 | tf_op jit(solution)/shard_map/ppermute | solution.py:402
  57.7 16.7 %copy-start.1 = (bf16[9,128,512]{2,1,0:T(8,128)(2,1)}, bf16[9,128,512]{2,1,0:T(8,128)(2,1)S(1)}, u32[]{:S(2)}) copy-start(bf16[9,128,512]{2,1,0:T(8,128)(2,1)S(1)} %broadcast_select_fusion.refs_0_) | copy-start | bytes 3538948
  57.7 19.0 %collective-permute-start.8 = (bf16[9,128,512]{2,1,0:T(8,128)(2,1)S(1)}, bf16[9,128,512]{2,1,0:T(8,128)(2,1)}, u32[]{:S(2)}, u32[]{:S(2)}) collective-permute-start(bf16[9,128,512]{2,1,0:T(8,128)(2,1)S(1)} %broadcast_select_fusion.refs_0_), channel_id=1, source_target_pairs={{0,16},{2,18},{5,21},{7,23},{8,24},{10,26},{13,29},{15,31},{16,0},... | collective-permute-start | bytes 3538952 | tf_op jit(solution)/shard_map/ppermute | solution.py:402
  61.4 17.8 %collective-permute-start.10 = (bf16[2,3,128,512]{3,2,1,0:T(8,128)(2,1)S(1)}, bf16[2,3,128,512]{3,2,1,0:T(8,128)(2,1)S(1)}, u32[]{:S(2)}, u32[]{:S(2)}) collective-permute-start(bf16[2,3,128,512]{3,2,1,0:T(8,128)(2,1)S(1)} %pad_maximum_fusion.1), channel_id=1, source_target_pairs={{0,8},{5,13},{10,2},{15,7},{16,24},{21,29},{26,18},{31,23}} | collective-permute-start | bytes 2359304 | tf_op jit(solution)/shard_map/ppermute | solution.py:402
  74.4 8.0 %collective-permute-start.11 = (bf16[9,128,512]{2,1,0:T(8,128)(2,1)S(1)}, bf16[9,128,512]{2,1,0:T(8,128)(2,1)}, u32[]{:S(2)}, u32[]{:S(2)}) collective-permute-start(bf16[9,128,512]{2,1,0:T(8,128)(2,1)S(1)} %broadcast_select_fusion.refs_0_), channel_id=1, source_target_pairs={{0,4},{2,6},{5,1},{7,3},{8,12},{10,14},{13,9},{15,11},{16,20},{18,... | collective-permute-start | bytes 3538952 | tf_op jit(solution)/shard_map/ppermute | solution.py:402
  76.8 5.7 %collective-permute-start.12 = (bf16[9,128,512]{2,1,0:T(8,128)(2,1)}, bf16[9,128,512]{2,1,0:T(8,128)(2,1)}, u32[]{:S(2)}, u32[]{:S(2)}) collective-permute-start(bf16[9,128,512]{2,1,0:T(8,128)(2,1)} %collective-permute-done.8.refs_1_), channel_id=1, source_target_pairs={{0,4},{2,6},{5,1},{7,3},{8,12},{10,14},{13,9},{15,11},{16,20},{18,... | collective-permute-start | bytes 3538952 | tf_op jit(solution)/shard_map/ppermute | solution.py:402
  79.3 3.2 %copy-start.2 = (bf16[2,3,128,512]{3,2,1,0:T(8,128)(2,1)}, bf16[2,3,128,512]{3,2,1,0:T(8,128)(2,1)S(1)}, u32[]{:S(2)}) copy-start(bf16[2,3,128,512]{3,2,1,0:T(8,128)(2,1)S(1)} %broadcast_select_fusion.1.refs_2_) | copy-start | bytes 2359300
  79.3 3.2 %collective-permute-start.13 = (bf16[2,3,128,512]{3,2,1,0:T(8,128)(2,1)S(1)}, bf16[2,3,128,512]{3,2,1,0:T(8,128)(2,1)S(1)}, u32[]{:S(2)}, u32[]{:S(2)}) collective-permute-start(bf16[2,3,128,512]{3,2,1,0:T(8,128)(2,1)S(1)} %broadcast_select_fusion.1.refs_2_), channel_id=1, source_target_pairs={{0,4},{2,6},{5,1},{7,3},{8,12},{10,14},{13,9},{15,11},{16,20},{18,... | collective-permute-start | bytes 2359304 | tf_op jit(solution)/shard_map/ppermute | solution.py:402
  82.5 0.9 copy-start.3

commit v5 on v4

--- a/solution.py
+++ b/solution.py
@@ -262,22 +262,29 @@
                     pltpu.make_async_copy(src.at[tile], to, sem.at[at // size]).start()
             base += views[k].shape[0]
 
-    def columns(b):
+    def arrive(b):
+        rows = xc.at[pl.ds(pl.multiple_of(b * size, size), size)]
+        pltpu.make_async_copy(rows, rows, sem.at[b]).wait()
+
+    def kernel_values(b):
         rows = pl.ds(pl.multiple_of(b * size, size), size)
-        pltpu.make_async_copy(xc.at[rows], xc.at[rows], sem.at[b]).wait()
         norms = panel_block(xc.at[rows], pts[...], sp_ref[0:1, :], bp_ref[0:1, :], k_ref)
         set_diagonal(k_ref, norms[0][4], jnp.where(b == 0, info[2], -1))
         for h, part, s, _, _ in norms:
+            for g in range(0, part, TILE):
+                wide = jnp.broadcast_to(s[g : g + TILE, :], (TILE, TILE)).T[0:8, :]
+                lanes = pl.ds(pl.multiple_of(b * size + h + g, TILE), TILE)
+                sc[:, lanes] = wide
+                bc[:, lanes] = 1.0 / wide
+
+    def lower_columns(b):
+        part = size // 2
+        for h in range(0, size, part):
             hi, lo = split(dot_hi(k_ref[h : h + part, :], t_ref[...], ((1,), (1,))))
             to = pl.ds(pl.multiple_of(b * size + h, part), part)
             lc[to, :PANEL] = hi
             lc[to, PANEL : 2 * PANEL] = lo
             lc[to, 2 * PANEL :] = hi
-            for g in range(0, part, TILE):
-                wide = jnp.broadcast_to(s[g : g + TILE, :], (TILE, TILE)).T[0:8, :]
-                lanes = pl.ds(pl.multiple_of(b * size + h + g, TILE), TILE)
-                sc[:, lanes] = wide
-                bc[:, lanes] = 1.0 / wide
 
     def multiply(x, l, col, g, m):
         cols = pl.ds(pl.multiple_of(col, cb), cb)
@@ -306,10 +313,17 @@
         def _():
             load(got)
 
-        @pl.loop(0, xc.shape[0] // size)
+        count = xc.shape[0] // size
+        arrive(0)
+        kernel_values(0)
+
+        @pl.loop(0, count - 1)
         def _(b):
-            columns(b)
-
+            arrive(b + 1)
+            lower_columns(b)
+            kernel_values(b + 1)
+
+        lower_columns(count - 1)
         multiply(xr, lr, 0, ga, ma)
 
     multiply(xr, lr, j * (tb * TILE) + cb, gb, mb)

time: 128 us -> 127 us (level)
  no operation moved by 1% of the time
where the time goes in v5:
time: 127 us; the launch traced here: 126 us
  Pallas kernels  59.9 us (47%)
  starting transfers between devices  40 us (31%)
  waiting for transfers between devices  18.9 us (15%)
  other arithmetic  3.99 us (3%)
  local copies, waits for them, and re-layouts  1.62 us (1%)
    pallas_call x1, Pallas kernels, trailing(): pl.pallas_call(functools.partial(trailing_kernel, rb, tb, blocks, steps,...  42 us
    ppermute x14, starting transfers between devices, send(): return lax.ppermute(value, ('row', 'col'), pairs)  40 us
    ppermute x14, waiting for transfers between devices, send(): return lax.ppermute(value, ('row', 'col'), pairs)  18.9 us
    pallas_call x1, Pallas kernels, factor(): pl.pallas_call(factor_kernel, out_shape=[full, vec, vec], scratch_shapes=...  10.6 us
    pallas_call x1, Pallas kernels, panel_rows(): pl.pallas_call(panel_kernel, grid=(m // block,), in_specs=[pl.BlockSpec(m...  7.25 us
    select_n x3, other arithmetic, in_order(): jnp.where(away == 0, own, jnp.where(away == 3, before, jnp.where(away ==...  2.74 us
  transfers between devices with their start and end apart: 14, of which 6 were waited for; matrix products, arithmetic and copies ran while one was open for 4% of the time, Pallas kernels for 14%

profile of v5, /device:TPU:0, one launch (start us, length us, event | category | flops | bytes accessed | tf_op | source)
XLA Modules:
  0.0 125.5 jit_solution(1694191110272342830)
XLA Ops:
  0.6 3.1 %collective-permute-start = (bf16[12,32,512]{2,1,0:T(8,128)(2,1)}, bf16[12,32,512]{2,1,0:T(8,128)(2,1)S(1)}, u32[]{:S(2)}, u32[]{:S(2)}) collective-permute-start(bf16[12,32,512]{2,1,0:T(8,128)(2,1)} %bitcast.55), channel_id=1, source_target_pairs={{0,1},{1,2},{2,3},{3,0},{4,5},{5,6},{6,7},{7,4},{8,9},{9,10},{10,1... | collective-permute-start | bytes 1179656 | tf_op jit(solution)/shard_map/ppermute | solution.py:416
  3.7 2.1 %collective-permute-start.1 = (bf16[12,32,512]{2,1,0:T(8,128)(2,1)}, bf16[12,32,512]{2,1,0:T(8,128)(2,1)S(1)}, u32[]{:S(2)}, u32[]{:S(2)}) collective-permute-start(bf16[12,32,512]{2,1,0:T(8,128)(2,1)} %bitcast.56), channel_id=1, source_target_pairs={{0,3},{1,0},{2,1},{3,2},{4,7},{5,4},{6,5},{7,6},{8,11},{9,8},{10,9... | collective-permute-start | bytes 1179656 | tf_op jit(solution)/shard_map/ppermute | solution.py:416
  5.8 10.1 %collective-permute-done = bf16[12,32,512]{2,1,0:T(8,128)(2,1)S(1)} collective-permute-done((bf16[12,32,512]{2,1,0:T(8,128)(2,1)}, bf16[12,32,512]{2,1,0:T(8,128)(2,1)S(1)}, u32[]{:S(2)}, u32[]{:S(2)}) %collective-permute-start) | collective-permute-done | bytes 393248 | tf_op jit(solution)/shard_map/ppermute | solution.py:416
  15.9 1.9 %collective-permute-start.3 = (bf16[32,512]{1,0:T(8,128)(2,1)S(1)}, bf16[32,512]{1,0:T(8,128)(2,1)S(1)}, u32[]{:S(2)}, u32[]{:S(2)}) collective-permute-start(bf16[32,512]{1,0:T(8,128)(2,1)S(1)} %slice_bitcast_fusion.1), channel_id=1, source_target_pairs={{0,1},{1,2},{2,3},{3,0},{4,5},{5,6},{6,7},{7,4}} | collective-permute-start | bytes 98312 | tf_op jit(solution)/shard_map/ppermute | solution.py:416
  17.9 7.8 %collective-permute-start.2 = (bf16[12,32,512]{2,1,0:T(8,128)(2,1)S(1)}, bf16[12,32,512]{2,1,0:T(8,128)(2,1)S(1)}, u32[]{:S(2)}, u32[]{:S(2)}) collective-permute-start(bf16[12,32,512]{2,1,0:T(8,128)(2,1)S(1)} %collective-permute-done), channel_id=1, source_target_pairs={{0,1},{1,2},{2,3},{3,0},{4,5},{5,6},{6,7},{7,4},{8,9},{9,10},{10,1... | collective-permute-start | bytes 1179656 | tf_op jit(solution)/shard_map/ppermute | solution.py:416
  25.7 0.0 collective-permute-done.1
  25.7 2.7 %collective-permute-done.3 = bf16[32,512]{1,0:T(8,128)(2,1)S(1)} collective-permute-done((bf16[32,512]{1,0:T(8,128)(2,1)S(1)}, bf16[32,512]{1,0:T(8,128)(2,1)S(1)}, u32[]{:S(2)}, u32[]{:S(2)}) %collective-permute-start.3) | collective-permute-done | bytes 32800 | tf_op jit(solution)/shard_map/ppermute | solution.py:416
  28.4 0.8 bitcast_select_fusion.2
  29.2 0.8 bitcast_select_fusion.3
  30.0 1.3 %collective-permute-start.4 = (bf16[128,512]{1,0:T(8,128)(2,1)S(1)}, bf16[128,512]{1,0:T(8,128)(2,1)S(1)}, u32[]{:S(2)}, u32[]{:S(2)}) collective-permute-start(bf16[128,512]{1,0:T(8,128)(2,1)S(1)} %pad_maximum_fusion.3), channel_id=1, source_target_pairs={{0,8},{1,9},{2,10},{3,11},{4,12},{5,13},{6,14},{7,15}} | collective-permute-start | bytes 393224 | tf_op jit(solution)/shard_map/ppermute | solution.py:416
  31.3 2.5 %collective-permute-done.4 = bf16[128,512]{1,0:T(8,128)(2,1)S(1)} collective-permute-done((bf16[128,512]{1,0:T(8,128)(2,1)S(1)}, bf16[128,512]{1,0:T(8,128)(2,1)S(1)}, u32[]{:S(2)}, u32[]{:S(2)}) %collective-permute-start.4) | collective-permute-done | bytes 131104 | tf_op jit(solution)/shard_map/ppermute | solution.py:416
  33.9 0.0 collective-permute-done.2
  33.9 1.5 %collective-permute-start.5 = (bf16[128,512]{1,0:T(8,128)(2,1)S(1)}, bf16[128,512]{1,0:T(8,128)(2,1)S(1)}, u32[]{:S(2)}, u32[]{:S(2)}) collective-permute-start(bf16[128,512]{1,0:T(8,128)(2,1)S(1)} %broadcast_select_fusion.2), channel_id=1, source_target_pairs={{0,16},{1,17},{2,18},{3,19},{4,20},{5,21},{6,22},{7,23},{8,24},{9,... | collective-permute-start | bytes 393224 | tf_op jit(solution)/shard_map/ppermute | solution.py:416
  35.4 1.2 select_select_fusion.3
  36.6 1.3 %collective-permute-done.5 = bf16[128,512]{1,0:T(8,128)(2,1)S(1)} collective-permute-done((bf16[128,512]{1,0:T(8,128)(2,1)S(1)}, bf16[128,512]{1,0:T(8,128)(2,1)S(1)}, u32[]{:S(2)}, u32[]{:S(2)}) %collective-permute-start.5) | collective-permute-done | bytes 131104 | tf_op jit(solution)/shard_map/ppermute | solution.py:416
  37.9 0.1 collective-permute-start.6
  38.0 0.1 pad_maximum_fusion
  38.1 0.0 copy-start
  38.1 0.1 slice.24
  38.2 4.4 %collective-permute-start.9 = (bf16[3,128,512]{2,1,0:T(8,128)(2,1)S(1)}, bf16[3,128,512]{2,1,0:T(8,128)(2,1)S(1)}, u32[]{:S(2)}, u32[]{:S(2)}) collective-permute-start(bf16[3,128,512]{2,1,0:T(8,128)(2,1)S(1)} %slice.25), channel_id=1, source_target_pairs={{0,16},{5,21},{10,26},{15,31},{16,0},{21,5},{26,10},{31,15}} | collective-permute-start | bytes 1179656 | tf_op jit(solution)/shard_map/ppermute | solution.py:416
  42.6 2.3 %collective-permute-start.7 = (bf16[9,128,512]{2,1,0:T(8,128)(2,1)S(1)}, bf16[9,128,512]{2,1,0:T(8,128)(2,1)}, u32[]{:S(2)}, u32[]{:S(2)}) collective-permute-start(bf16[9,128,512]{2,1,0:T(8,128)(2,1)S(1)} %slice.24), channel_id=1, source_target_pairs={{0,8},{5,13},{10,2},{15,7},{16,24},{21,29},{26,18},{31,23}} | collective-permute-start | bytes 3538952 | tf_op jit(solution)/shard_map/ppermute | solution.py:416
  44.9 0.0 collective-permute-done.6
  44.9 0.8 pad_maximum_fusion.2
  45.7 10.6 %factor.1 = (f32[256,256]{1,0:T(8,128)}, f32[8,256]{1,0:T(8,128)}, f32[8,256]{1,0:T(8,128)}) custom-call(bf16[256,512]{1,0:T(8,128)(2,1)} %bitcast.57), custom_call_target="tpu_custom_call" | custom-call | flops 12000000000 | bytes 1000000 | tf_op jit(solution)/shard_map/factor/pallas_call | solution.py:141
  56.3 1.2 collective-permute-done.7
  57.6 0.0 copy-done
  57.6 0.1 broadcast_select_fusion.refs_0_
  57.7 0.0 copy-start.1
  57.7 3.5 %collective-permute-start.8 = (bf16[9,128,512]{2,1,0:T(8,128)(2,1)S(1)}, bf16[9,128,512]{2,1,0:T(8,128)(2,1)}, u32[]{:S(2)}, u32[]{:S(2)}) collective-permute-start(bf16[9,128,512]{2,1,0:T(8,128)(2,1)S(1)} %broadcast_select_fusion.refs_0_), channel_id=1, source_target_pairs={{0,16},{2,18},{5,21},{7,23},{8,24},{10,26},{13,29},{15,31},{16,0},... | collective-permute-start | bytes 3538952 | tf_op jit(solution)/shard_map/ppermute | solution.py:416
  61.3 0.0 collective-permute-done.9
  61.3 0.1 pad_maximum_fusion.1
  61.4 5.8 %collective-permute-start.10 = (bf16[2,3,128,512]{3,2,1,0:T(8,128)(2,1)S(1)}, bf16[2,3,128,512]{3,2,1,0:T(8,128)(2,1)S(1)}, u32[]{:S(2)}, u32[]{:S(2)}) collective-permute-start(bf16[2,3,128,512]{3,2,1,0:T(8,128)(2,1)S(1)} %pad_maximum_fusion.1), channel_id=1, source_target_pairs={{0,8},{5,13},{10,2},{15,7},{16,24},{21,29},{26,18},{31,23}} | collective-permute-start | bytes 2359304 | tf_op jit(solution)/shard_map/ppermute | solution.py:416
  67.2 7.3 %panel_rows.1 = (f32[1536,256]{1,0:T(8,128)}, bf16[1536,768]{1,0:T(8,128)(2,1)}, f32[1536,128]{1,0:T(8,128)}, f32[1536,128]{1,0:T(8,128)}, f32[1536,128]{1,0:T(8,128)}) custom-call(s32[1]{0:T(128)} %bitcast.tau_ref, bf16[1536,512]{1,0:T(8,128)(2,1)} %bitcast.48, bf16[256,512]{1,0:T(8,128)(2,1)} %bitcast.58, f32[256,256]{1,0:T(8,128)} %get-tuple-element.18.t_ref.refs_7_, ...), custom_call_target="tpu_custom_call" | custom-call | flops 9663676416 | bytes 6291456 | tf_op jit(solution)/shard_map/panel_rows/pallas_call | solution.py:219
  74.4 0.0 copy-done.1
  74.4 2.3 %collective-permute-start.11 = (bf16[9,128,512]{2,1,0:T(8,128)(2,1)S(1)}, bf16[9,128,512]{2,1,0:T(8,128)(2,1)}, u32[]{:S(2)}, u32[]{:S(2)}) collective-permute-start(bf16[9,128,512]{2,1,0:T(8,128)(2,1)S(1)} %broadcast_select_fusion.refs_0_), channel_id=1, source_target_pairs={{0,4},{2,6},{5,1},{7,3},{8,12},{10,14},{13,9},{15,11},{16,20},{18,... | collective-permute-start | bytes 3538952 | tf_op jit(solution)/shard_map/ppermute | solution.py:416
  76.8 0.0 collective-permute-done.8.refs_1_
  76.8 2.4 %collective-permute-start.12 = (bf16[9,128,512]{2,1,0:T(8,128)(2,1)}, bf16[9,128,512]{2,1,0:T(8,128)(2,1)}, u32[]{:S(2)}, u32[]{:S(2)}) collective-permute-start(bf16[9,128,512]{2,1,0:T(8,128)(2,1)} %collective-permute-done.8.refs_1_), channel_id=1, source_target_pairs={{0,4},{2,6},{5,1},{7,3},{8,12},{10,14},{13,9},{15,11},{16,20},{18,... | collective-permute-start | bytes 3538952 | tf_op jit(solution)/shard_map/ppermute | solution.py:416
  79.2 0.0 collective-permute-done.10
  79.2 0.1 broadcast_select_fusion.1.refs_2_
  79.3 0.0 copy-start.2
  79.3 1.5 %collective-permute-start.13 = (bf16[2,3,128,512]{3,2,1,0:T(8,128)(2,1)S(1)}, bf16[2,3,128,512]{3,2,1,0:T(8,128)(2,1)S(1)}, u32[]{:S(2)}, u32[]{:S(2)}) collective-permute-start(bf16[2,3,128,512]{3,2,1,0:T(8,128)(2,1)S(1)} %broadcast_select_fusion.1.refs_2_), channel_id=1, source_target_pairs={{0,4},{2,6},{5,1},{7,3},{8,12},{10,14},{13,9},{15,11},{16,20},{18,... | collective-permute-start | bytes 2359304 | tf_op jit(solution)/shard_map/ppermute | solution.py:416
  80.9 0.6 stack.36.info
  81.5 1.0 collective-permute-done.13.refs_5_
  82.5 0.0 copy-start.3
  82.5 0.0 collective-permute-done.11.refs_3_
  82.5 0.0 collective-permute-done.12.refs_4_
  82.5 0.0 copy-done.2
  82.5 0.9 copy-done.3
  83.4 42.0 %trailing.1 = f32[1536,24,128]{2,1,0:T(8,128)} custom-call(s32[5]{0:T(128)} %stack.36.info, bf16[9,128,512]{2,1,0:T(8,128)(2,1)} %copy-done.1, bf16[9,128,512]{2,1,0:T(8,128)(2,1)} %collective-permute-done.8.refs_1_, bf16[2,3,128,512]{3,2,1,0:T(8,128)(2,1)} %copy-done.2, bf16[9,128,512]{2,1,0:T(8,128)(2,1)} %collective-permute-done.11.refs_3_, ...), custom_call_target="tpu_custom_call" | custom-call | flops 48318382080 | bytes 18874368 | tf_op jit(solution)/shard_map/trailing/pallas_call | solution.py:374
  (6 shorter events, 0.1 us)
Async XLA Ops:
  0.6 15.3 %collective-permute-start = (bf16[12,32,512]{2,1,0:T(8,128)(2,1)}, bf16[12,32,512]{2,1,0:T(8,128)(2,1)S(1)}, u32[]{:S(2)}, u32[]{:S(2)}) collective-permute-start(bf16[12,32,512]{2,1,0:T(8,128)(2,1)} %bitcast.55), channel_id=1, source_target_pairs={{0,1},{1,2},{2,3},{3,0},{4,5},{5,6},{6,7},{7,4},{8,9},{9,10},{10,1... | collective-permute-start | bytes 1179656 | tf_op jit(solution)/shard_map/ppermute | solution.py:416
  3.7 22.0 %collective-permute-start.1 = (bf16[12,32,512]{2,1,0:T(8,128)(2,1)}, bf16[12,32,512]{2,1,0:T(8,128)(2,1)S(1)}, u32[]{:S(2)}, u32[]{:S(2)}) collective-permute-start(bf16[12,32,512]{2,1,0:T(8,128)(2,1)} %bitcast.56), channel_id=1, source_target_pairs={{0,3},{1,0},{2,1},{3,2},{4,7},{5,4},{6,5},{7,6},{8,11},{9,8},{10,9... | collective-permute-start | bytes 1179656 | tf_op jit(solution)/shard_map/ppermute | solution.py:416
  15.9 12.5 %collective-permute-start.3 = (bf16[32,512]{1,0:T(8,128)(2,1)S(1)}, bf16[32,512]{1,0:T(8,128)(2,1)S(1)}, u32[]{:S(2)}, u32[]{:S(2)}) collective-permute-start(bf16[32,512]{1,0:T(8,128)(2,1)S(1)} %slice_bitcast_fusion.1), channel_id=1, source_target_pairs={{0,1},{1,2},{2,3},{3,0},{4,5},{5,6},{6,7},{7,4}} | collective-permute-start | bytes 98312 | tf_op jit(solution)/shard_map/ppermute | solution.py:416
  17.9 15.9 %collective-permute-start.2 = (bf16[12,32,512]{2,1,0:T(8,128)(2,1)S(1)}, bf16[12,32,512]{2,1,0:T(8,128)(2,1)S(1)}, u32[]{:S(2)}, u32[]{:S(2)}) collective-permute-start(bf16[12,32,512]{2,1,0:T(8,128)(2,1)S(1)} %collective-permute-done), channel_id=1, source_target_pairs={{0,1},{1,2},{2,3},{3,0},{4,5},{5,6},{6,7},{7,4},{8,9},{9,10},{10,1... | collective-permute-start | bytes 1179656 | tf_op jit(solution)/shard_map/ppermute | solution.py:416
  30.0 3.8 %collective-permute-start.4 = (bf16[128,512]{1,0:T(8,128)(2,1)S(1)}, bf16[128,512]{1,0:T(8,128)(2,1)S(1)}, u32[]{:S(2)}, u32[]{:S(2)}) collective-permute-start(bf16[128,512]{1,0:T(8,128)(2,1)S(1)} %pad_maximum_fusion.3), channel_id=1, source_target_pairs={{0,8},{1,9},{2,10},{3,11},{4,12},{5,13},{6,14},{7,15}} | collective-permute-start | bytes 393224 | tf_op jit(solution)/shard_map/ppermute | solution.py:416
  33.9 4.0 %collective-permute-start.5 = (bf16[128,512]{1,0:T(8,128)(2,1)S(1)}, bf16[128,512]{1,0:T(8,128)(2,1)S(1)}, u32[]{:S(2)}, u32[]{:S(2)}) collective-permute-start(bf16[128,512]{1,0:T(8,128)(2,1)S(1)} %broadcast_select_fusion.2), channel_id=1, source_target_pairs={{0,16},{1,17},{2,18},{3,19},{4,20},{5,21},{6,22},{7,23},{8,24},{9,... | collective-permute-start | bytes 393224 | tf_op jit(solution)/shard_map/ppermute | solution.py:416
  37.9 7.0 %collective-permute-start.6 = (bf16[1,128,512]{2,1,0:T(8,128)(2,1)S(1)}, bf16[1,128,512]{2,1,0:T(8,128)(2,1)S(1)}, u32[]{:S(2)}, u32[]{:S(2)}) collective-permute-start(bf16[1,128,512]{2,1,0:T(8,128)(2,1)S(1)} %select_bitcast_fusion), channel_id=1, source_target_pairs={{0,4},{1,5},{2,6},{3,7},{4,0},{5,1},{6,2},{7,3},{8,12},{9,13},{10,... | collective-permute-start | bytes 393224 | tf_op jit(solution)/shard_map/ppermute | solution.py:416
  38.1 19.5 %copy-start = (bf16[12,128,512]{2,1,0:T(8,128)(2,1)}, bf16[12,128,512]{2,1,0:T(8,128)(2,1)S(1)}, u32[]{:S(2)}) copy-start(bf16[12,128,512]{2,1,0:T(8,128)(2,1)S(1)} %pad_maximum_fusion) | copy-start | bytes 4718596
  38.2 23.1 %collective-permute-start.9 = (bf16[3,128,512]{2,1,0:T(8,128)(2,1)S(1)}, bf16[3,128,512]{2,1,0:T(8,128)(2,1)S(1)}, u32[]{:S(2)}, u32[]{:S(2)}) collective-permute-start(bf16[3,128,512]{2,1,0:T(8,128)(2,1)S(1)} %slice.25), channel_id=1, source_target_pairs={{0,16},{5,21},{10,26},{15,31},{16,0},{21,5},{26,10},{31,15}} | collective-permute-start | bytes 1179656 | tf_op jit(solution)/shard_map/ppermute | solution.py:416
  42.6 15.0 %collective-permute-start.7 = (bf16[9,128,512]{2,1,0:T(8,128)(2,1)S(1)}, bf16[9,128,512]{2,1,0:T(8,128)(2,1)}, u32[]{:S(2)}, u32[]{:S(2)}) collective-permute-start(bf16[9,128,512]{2,1,0:T(8,128)(2,1)S(1)} %slice.24), channel_id=1, source_target_pairs={{0,8},{5,13},{10,2},{15,7},{16,24},{21,29},{26,18},{31,23}} | collective-permute-start | bytes 3538952 | tf_op jit(solution)/shard_map/ppermute | solution.py:416
  57.7 16.7 %copy-start.1 = (bf16[9,128,512]{2,1,0:T(8,128)(2,1)}, bf16[9,128,512]{2,1,0:T(8,128)(2,1)S(1)}, u32[]{:S(2)}) copy-start(bf16[9,128,512]{2,1,0:T(8,128)(2,1)S(1)} %broadcast_select_fusion.refs_0_) | copy-start | bytes 3538948
  57.7 19.0 %collective-permute-start.8 = (bf16[9,128,512]{2,1,0:T(8,128)(2,1)S(1)}, bf16[9,128,512]{2,1,0:T(8,128)(2,1)}, u32[]{:S(2)}, u32[]{:S(2)}) collective-permute-start(bf16[9,128,512]{2,1,0:T(8,128)(2,1)S(1)} %broadcast_select_fusion.refs_0_), channel_id=1, source_target_pairs={{0,16},{2,18},{5,21},{7,23},{8,24},{10,26},{13,29},{15,31},{16,0},... | collective-permute-start | bytes 3538952 | tf_op jit(solution)/shard_map/ppermute | solution.py:416
  61.4 17.8 %collective-permute-start.10 = (bf16[2,3,128,512]{3,2,1,0:T(8,128)(2,1)S(1)}, bf16[2,3,128,512]{3,2,1,0:T(8,128)(2,1)S(1)}, u32[]{:S(2)}, u32[]{:S(2)}) collective-permute-start(bf16[2,3,128,512]{3,2,1,0:T(8,128)(2,1)S(1)} %pad_maximum_fusion.1), channel_id=1, source_target_pairs={{0,8},{5,13},{10,2},{15,7},{16,24},{21,29},{26,18},{31,23}} | collective-permute-start | bytes 2359304 | tf_op jit(solution)/shard_map/ppermute | solution.py:416
  74.4 8.0 %collective-permute-start.11 = (bf16[9,128,512]{2,1,0:T(8,128)(2,1)S(1)}, bf16[9,128,512]{2,1,0:T(8,128)(2,1)}, u32[]{:S(2)}, u32[]{:S(2)}) collective-permute-start(bf16[9,128,512]{2,1,0:T(8,128)(2,1)S(1)} %broadcast_select_fusion.refs_0_), channel_id=1, source_target_pairs={{0,4},{2,6},{5,1},{7,3},{8,12},{10,14},{13,9},{15,11},{16,20},{18,... | collective-permute-start | bytes 3538952 | tf_op jit(solution)/shard_map/ppermute | solution.py:416
  76.8 5.7 %collective-permute-start.12 = (bf16[9,128,512]{2,1,0:T(8,128)(2,1)}, bf16[9,128,512]{2,1,0:T(8,128)(2,1)}, u32[]{:S(2)}, u32[]{:S(2)}) collective-permute-start(bf16[9,128,512]{2,1,0:T(8,128)(2,1)} %collective-permute-done.8.refs_1_), channel_id=1, source_target_pairs={{0,4},{2,6},{5,1},{7,3},{8,12},{10,14},{13,9},{15,11},{16,20},{18,... | collective-permute-start | bytes 3538952 | tf_op jit(solution)/shard_map/ppermute | solution.py:416
  79.3 3.2 %copy-start.2 = (bf16[2,3,128,512]{3,2,1,0:T(8,128)(2,1)}, bf16[2,3,128,512]{3,2,1,0:T(8,128)(2,1)S(1)}, u32[]{:S(2)}) copy-start(bf16[2,3,128,512]{3,2,1,0:T(8,128)(2,1)S(1)} %broadcast_select_fusion.1.refs_2_) | copy-start | bytes 2359300
  79.3 3.2 %collective-permute-start.13 = (bf16[2,3,128,512]{3,2,1,0:T(8,128)(2,1)S(1)}, bf16[2,3,128,512]{3,2,1,0:T(8,128)(2,1)S(1)}, u32[]{:S(2)}, u32[]{:S(2)}) collective-permute-start(bf16[2,3,128,512]{3,2,1,0:T(8,128)(2,1)S(1)} %broadcast_select_fusion.1.refs_2_), channel_id=1, source_target_pairs={{0,4},{2,6},{5,1},{7,3},{8,12},{10,14},{13,9},{15,11},{16,20},{18,... | collective-permute-start | bytes 2359304 | tf_op jit(solution)/shard_map/ppermute | solution.py:416
  82.5 0.9 copy-start.3

commit v6 on v5

--- a/solution.py
+++ b/solution.py
@@ -106,7 +106,15 @@
             w_ref[g : g + 8, n:] = e
 
 
-def factor_kernel(x_ref, t_ref, sp_ref, bp_ref, k_ref, w_ref, t1_ref, t2_ref):
+def factor_kernel(odd_ref, own_ref, other_ref, t_ref, sp_ref, bp_ref, x_ref, k_ref, w_ref, t1_ref,
+                  t2_ref):
+    for odd in range(2):
+
+        @pl.when(odd_ref[0] == odd)
+        def _():
+            x_ref[odd * TILE : (odd + 1) * TILE, :] = own_ref[...]
+            x_ref[(1 - odd) * TILE : (2 - odd) * TILE, :] = other_ref[...]
+
     x = x_ref[...]
     gq_l = norm_lanes(x)
     b_l = lax.rsqrt(gq_l + EPS)
@@ -135,12 +143,13 @@
     t_ref[h:, h:] = t2
 
 
-def factor(points):
+def factor(odd, own, other):
     full = jax.ShapeDtypeStruct((PANEL, PANEL), jnp.float32)
     vec = jax.ShapeDtypeStruct((8, PANEL), jnp.float32)
     return pl.pallas_call(
         factor_kernel,
-        out_shape=[full, vec, vec],
+        in_specs=[pl.BlockSpec(memory_space=pltpu.SMEM)] + [pl.BlockSpec(memory_space=pltpu.VMEM)] * 2,
+        out_shape=[full, vec, vec, jax.ShapeDtypeStruct((PANEL, F), own.dtype)],
         scratch_shapes=[
             pltpu.VMEM((PANEL, PANEL), jnp.float32),
             pltpu.VMEM((TILE, 2 * TILE), jnp.float32),
@@ -150,7 +159,7 @@
         compiler_params=pltpu.CompilerParams(vmem_limit_bytes=VMEM_LIMIT),
         cost_estimate=pl.CostEstimate(flops=12 * 10**9, bytes_accessed=10**6, transcendentals=0),
         name="factor",
-    )(points)
+    )(odd, own, other)
 
 
 def panel_block(x_ref, pts, sp, bp, k_ref):
@@ -448,12 +457,7 @@
             data = jnp.where(self.r >> bit == 0, data, got)
             if bit == bits:
                 data = tie(data, gate)
-        data = data[None]
-        for bit in range(bits):
-            got = self.flip(data, bit, lambda i, j: True)
-            first = (self.r >> bit) & 1 == 0
-            data = jnp.concatenate([jnp.where(first, data, got), jnp.where(first, got, data)])
-        return data
+        return data, self.flip(data, 0, lambda i, j: True)
 
     def spread(self, data, high_first, second, last):
         mask = [self.n_col - 1]
@@ -495,8 +499,7 @@
 
     rows, points = grid.gather_rows(features[:, 0], PANEL // tile)
     x_rows = rows.reshape(tiles_r * tile, width)
-    points = points.reshape(PANEL, width)
-    t, sp, bp = factor(points)
+    t, sp, bp, points = factor((r & 1).astype(jnp.int32).reshape(1), *points)
     panel_args = (points, t, sp, bp)
     tau = lambda i: jnp.where(i < PANEL // tile, i, -1)
     low, *row_args = panel_rows(x_rows, *panel_args, tau(r).astype(jnp.int32).reshape(1))

time: 127 us -> 127 us (level)
  transfers between devices with their start and end apart: 14 -> 14, of which waited for: 6 -> 6; matrix products, arithmetic and copies ran while one was open for 4% -> 3% of each run, Pallas kernels for 14% -> 14%
where the time goes in v6:
time: 127 us; the launch traced here: 126 us
  Pallas kernels  60 us (47%)
  starting transfers between devices  41.2 us (32%)
  waiting for transfers between devices  18.4 us (14%)
  other arithmetic  3.87 us (3%)
  local copies, waits for them, and re-layouts  1.67 us (1%)
    pallas_call x1, Pallas kernels, trailing(): pl.pallas_call(functools.partial(trailing_kernel, rb, tb, blocks, steps,...  42 us
    ppermute x14, starting transfers between devices, send(): return lax.ppermute(value, ('row', 'col'), pairs)  41.2 us
    ppermute x14, waiting for transfers between devices, send(): return lax.ppermute(value, ('row', 'col'), pairs)  18.4 us
    pallas_call x1, Pallas kernels, factor(): pl.pallas_call(factor_kernel, in_specs=[pl.BlockSpec(memory_space=pltpu.S...  10.7 us
    pallas_call x1, Pallas kernels, panel_rows(): pl.pallas_call(panel_kernel, grid=(m // block,), in_specs=[pl.BlockSpec(m...  7.25 us
    select_n x3, other arithmetic, in_order(): jnp.where(away == 0, own, jnp.where(away == 3, before, jnp.where(away ==...  2.74 us
  transfers between devices with their start and end apart: 14, of which 6 were waited for; matrix products, arithmetic and copies ran while one was open for 3% of the time, Pallas kernels for 14%

profile of v6, /device:TPU:0, one launch (start us, length us, event | category | flops | bytes accessed | tf_op | source)
XLA Modules:
  0.0 126.2 jit_solution(1568015659917465457)
XLA Ops:
  0.6 3.1 %collective-permute-start = (bf16[12,32,512]{2,1,0:T(8,128)(2,1)}, bf16[12,32,512]{2,1,0:T(8,128)(2,1)S(1)}, u32[]{:S(2)}, u32[]{:S(2)}) collective-permute-start(bf16[12,32,512]{2,1,0:T(8,128)(2,1)} %bitcast.53), channel_id=1, source_target_pairs={{0,1},{1,2},{2,3},{3,0},{4,5},{5,6},{6,7},{7,4},{8,9},{9,10},{10,1... | collective-permute-start | bytes 1179656 | tf_op jit(solution)/shard_map/ppermute | solution.py:425
  3.7 2.1 %collective-permute-start.1 = (bf16[12,32,512]{2,1,0:T(8,128)(2,1)}, bf16[12,32,512]{2,1,0:T(8,128)(2,1)S(1)}, u32[]{:S(2)}, u32[]{:S(2)}) collective-permute-start(bf16[12,32,512]{2,1,0:T(8,128)(2,1)} %bitcast.54), channel_id=1, source_target_pairs={{0,3},{1,0},{2,1},{3,2},{4,7},{5,4},{6,5},{7,6},{8,11},{9,8},{10,9... | collective-permute-start | bytes 1179656 | tf_op jit(solution)/shard_map/ppermute | solution.py:425
  5.8 10.1 %collective-permute-done = bf16[12,32,512]{2,1,0:T(8,128)(2,1)S(1)} collective-permute-done((bf16[12,32,512]{2,1,0:T(8,128)(2,1)}, bf16[12,32,512]{2,1,0:T(8,128)(2,1)S(1)}, u32[]{:S(2)}, u32[]{:S(2)}) %collective-permute-start) | collective-permute-done | bytes 393248 | tf_op jit(solution)/shard_map/ppermute | solution.py:425
  15.9 1.9 %collective-permute-start.3 = (bf16[32,512]{1,0:T(8,128)(2,1)S(1)}, bf16[32,512]{1,0:T(8,128)(2,1)S(1)}, u32[]{:S(2)}, u32[]{:S(2)}) collective-permute-start(bf16[32,512]{1,0:T(8,128)(2,1)S(1)} %slice_bitcast_fusion.1), channel_id=1, source_target_pairs={{0,1},{1,2},{2,3},{3,0},{4,5},{5,6},{6,7},{7,4}} | collective-permute-start | bytes 98312 | tf_op jit(solution)/shard_map/ppermute | solution.py:425
  17.9 7.8 %collective-permute-start.2 = (bf16[12,32,512]{2,1,0:T(8,128)(2,1)S(1)}, bf16[12,32,512]{2,1,0:T(8,128)(2,1)S(1)}, u32[]{:S(2)}, u32[]{:S(2)}) collective-permute-start(bf16[12,32,512]{2,1,0:T(8,128)(2,1)S(1)} %collective-permute-done), channel_id=1, source_target_pairs={{0,1},{1,2},{2,3},{3,0},{4,5},{5,6},{6,7},{7,4},{8,9},{9,10},{10,1... | collective-permute-start | bytes 1179656 | tf_op jit(solution)/shard_map/ppermute | solution.py:425
  25.7 0.0 collective-permute-done.1
  25.7 2.7 %collective-permute-done.3 = bf16[32,512]{1,0:T(8,128)(2,1)S(1)} collective-permute-done((bf16[32,512]{1,0:T(8,128)(2,1)S(1)}, bf16[32,512]{1,0:T(8,128)(2,1)S(1)}, u32[]{:S(2)}, u32[]{:S(2)}) %collective-permute-start.3) | collective-permute-done | bytes 32800 | tf_op jit(solution)/shard_map/ppermute | solution.py:425
  28.4 0.8 bitcast_select_fusion.2
  29.2 0.8 bitcast_select_fusion.3
  30.0 1.3 %collective-permute-start.4 = (bf16[128,512]{1,0:T(8,128)(2,1)S(1)}, bf16[128,512]{1,0:T(8,128)(2,1)S(1)}, u32[]{:S(2)}, u32[]{:S(2)}) collective-permute-start(bf16[128,512]{1,0:T(8,128)(2,1)S(1)} %pad_maximum_fusion.2), channel_id=1, source_target_pairs={{0,8},{1,9},{2,10},{3,11},{4,12},{5,13},{6,14},{7,15}} | collective-permute-start | bytes 393224 | tf_op jit(solution)/shard_map/ppermute | solution.py:425
  31.3 2.5 %collective-permute-done.4 = bf16[128,512]{1,0:T(8,128)(2,1)S(1)} collective-permute-done((bf16[128,512]{1,0:T(8,128)(2,1)S(1)}, bf16[128,512]{1,0:T(8,128)(2,1)S(1)}, u32[]{:S(2)}, u32[]{:S(2)}) %collective-permute-start.4) | collective-permute-done | bytes 131104 | tf_op jit(solution)/shard_map/ppermute | solution.py:425
  33.9 0.0 collective-permute-done.2
  33.9 1.5 %collective-permute-start.5 = (bf16[128,512]{1,0:T(8,128)(2,1)S(1)}, bf16[128,512]{1,0:T(8,128)(2,1)S(1)}, u32[]{:S(2)}, u32[]{:S(2)}) collective-permute-start(bf16[128,512]{1,0:T(8,128)(2,1)S(1)} %broadcast_select_fusion.2), channel_id=1, source_target_pairs={{0,16},{1,17},{2,18},{3,19},{4,20},{5,21},{6,22},{7,23},{8,24},{9,... | collective-permute-start | bytes 393224 | tf_op jit(solution)/shard_map/ppermute | solution.py:425
  35.4 1.2 select_select_fusion.3
  36.6 1.3 %collective-permute-done.5 = bf16[128,512]{1,0:T(8,128)(2,1)S(1)} collective-permute-done((bf16[128,512]{1,0:T(8,128)(2,1)S(1)}, bf16[128,512]{1,0:T(8,128)(2,1)S(1)}, u32[]{:S(2)}, u32[]{:S(2)}) %collective-permute-start.5) | collective-permute-done | bytes 131104 | tf_op jit(solution)/shard_map/ppermute | solution.py:425
  37.9 0.7 broadcast_select_fusion.3.own_ref
  38.5 0.0 collective-permute-start.6
  38.6 0.1 pad_maximum_fusion
  38.7 0.0 copy-start
  38.7 0.1 slice.24
  38.8 5.2 %collective-permute-start.7 = (bf16[9,128,512]{2,1,0:T(8,128)(2,1)S(1)}, bf16[9,128,512]{2,1,0:T(8,128)(2,1)}, u32[]{:S(2)}, u32[]{:S(2)}) collective-permute-start(bf16[9,128,512]{2,1,0:T(8,128)(2,1)S(1)} %slice.24), channel_id=1, source_target_pairs={{0,8},{5,13},{10,2},{15,7},{16,24},{21,29},{26,18},{31,23}} | collective-permute-start | bytes 3538952 | tf_op jit(solution)/shard_map/ppermute | solution.py:425
  44.0 4.4 %collective-permute-start.9 = (bf16[3,128,512]{2,1,0:T(8,128)(2,1)S(1)}, bf16[3,128,512]{2,1,0:T(8,128)(2,1)S(1)}, u32[]{:S(2)}, u32[]{:S(2)}) collective-permute-start(bf16[3,128,512]{2,1,0:T(8,128)(2,1)S(1)} %slice.25), channel_id=1, source_target_pairs={{0,16},{5,21},{10,26},{15,31},{16,0},{21,5},{26,10},{31,15}} | collective-permute-start | bytes 1179656 | tf_op jit(solution)/shard_map/ppermute | solution.py:425
  48.3 0.0 collective-permute-done.6.other_ref
  48.3 10.7 %factor.1 = (f32[256,256]{1,0:T(8,128)}, f32[8,256]{1,0:T(8,128)}, f32[8,256]{1,0:T(8,128)}, bf16[256,512]{1,0:T(8,128)(2,1)}) custom-call(s32[1]{0:T(128)} %bitcast.3.odd_ref, bf16[128,512]{1,0:T(8,128)(2,1)} %broadcast_select_fusion.3.own_ref, bf16[128,512]{1,0:T(8,128)(2,1)} %collective-permute-done.6.other_ref), custom_call_target="tpu_custom_call" | custom-call | flops 12000000000 | bytes 1000000 | tf_op jit(solution)/shard_map/factor/pallas_call | solution.py:149
  59.0 0.0 collective-permute-done.7
  59.1 0.0 copy-done
  59.1 0.1 broadcast_select_fusion.refs_0_
  59.2 0.0 copy-start.1
  59.2 1.9 %collective-permute-start.8 = (bf16[9,128,512]{2,1,0:T(8,128)(2,1)S(1)}, bf16[9,128,512]{2,1,0:T(8,128)(2,1)}, u32[]{:S(2)}, u32[]{:S(2)}) collective-permute-start(bf16[9,128,512]{2,1,0:T(8,128)(2,1)S(1)} %broadcast_select_fusion.refs_0_), channel_id=1, source_target_pairs={{0,16},{2,18},{5,21},{7,23},{8,24},{10,26},{13,29},{15,31},{16,0},... | collective-permute-start | bytes 3538952 | tf_op jit(solution)/shard_map/ppermute | solution.py:425
  61.1 0.0 collective-permute-done.9
  61.2 0.1 pad_maximum_fusion.1
  61.2 5.8 %collective-permute-start.10 = (bf16[2,3,128,512]{3,2,1,0:T(8,128)(2,1)S(1)}, bf16[2,3,128,512]{3,2,1,0:T(8,128)(2,1)S(1)}, u32[]{:S(2)}, u32[]{:S(2)}) collective-permute-start(bf16[2,3,128,512]{3,2,1,0:T(8,128)(2,1)S(1)} %pad_maximum_fusion.1), channel_id=1, source_target_pairs={{0,8},{5,13},{10,2},{15,7},{16,24},{21,29},{26,18},{31,23}} | collective-permute-start | bytes 2359304 | tf_op jit(solution)/shard_map/ppermute | solution.py:425
  67.0 7.2 %panel_rows.1 = (f32[1536,256]{1,0:T(8,128)}, bf16[1536,768]{1,0:T(8,128)(2,1)}, f32[1536,128]{1,0:T(8,128)}, f32[1536,128]{1,0:T(8,128)}, f32[1536,128]{1,0:T(8,128)}) custom-call(s32[1]{0:T(128)} %bitcast.tau_ref, bf16[1536,512]{1,0:T(8,128)(2,1)} %bitcast.46, bf16[256,512]{1,0:T(8,128)(2,1)} %get-tuple-element.19.pts_ref.refs_6_, ...), custom_call_target="tpu_custom_call" | custom-call | flops 9663676416 | bytes 6291456 | tf_op jit(solution)/shard_map/panel_rows/pallas_call | solution.py:228
  74.3 0.0 copy-done.1
  74.3 2.3 %collective-permute-start.11 = (bf16[9,128,512]{2,1,0:T(8,128)(2,1)S(1)}, bf16[9,128,512]{2,1,0:T(8,128)(2,1)}, u32[]{:S(2)}, u32[]{:S(2)}) collective-permute-start(bf16[9,128,512]{2,1,0:T(8,128)(2,1)S(1)} %broadcast_select_fusion.refs_0_), channel_id=1, source_target_pairs={{0,4},{2,6},{5,1},{7,3},{8,12},{10,14},{13,9},{15,11},{16,20},{18,... | collective-permute-start | bytes 3538952 | tf_op jit(solution)/shard_map/ppermute | solution.py:425
  76.6 0.8 collective-permute-done.8.refs_1_
  77.4 2.4 %collective-permute-start.12 = (bf16[9,128,512]{2,1,0:T(8,128)(2,1)}, bf16[9,128,512]{2,1,0:T(8,128)(2,1)}, u32[]{:S(2)}, u32[]{:S(2)}) collective-permute-start(bf16[9,128,512]{2,1,0:T(8,128)(2,1)} %collective-permute-done.8.refs_1_), channel_id=1, source_target_pairs={{0,4},{2,6},{5,1},{7,3},{8,12},{10,14},{13,9},{15,11},{16,20},{18,... | collective-permute-start | bytes 3538952 | tf_op jit(solution)/shard_map/ppermute | solution.py:425
  79.8 0.0 collective-permute-done.10
  79.8 0.1 broadcast_select_fusion.1.refs_2_
  79.9 0.0 copy-start.2
  79.9 1.5 %collective-permute-start.13 = (bf16[2,3,128,512]{3,2,1,0:T(8,128)(2,1)S(1)}, bf16[2,3,128,512]{3,2,1,0:T(8,128)(2,1)S(1)}, u32[]{:S(2)}, u32[]{:S(2)}) collective-permute-start(bf16[2,3,128,512]{3,2,1,0:T(8,128)(2,1)S(1)} %broadcast_select_fusion.1.refs_2_), channel_id=1, source_target_pairs={{0,4},{2,6},{5,1},{7,3},{8,12},{10,14},{13,9},{15,11},{16,20},{18,... | collective-permute-start | bytes 2359304 | tf_op jit(solution)/shard_map/ppermute | solution.py:425
  81.5 0.7 stack.36.info
  82.2 0.9 collective-permute-done.13.refs_5_
  83.1 0.0 copy-start.3
  83.1 0.0 collective-permute-done.11.refs_3_
  83.1 0.0 collective-permute-done.12.refs_4_
  83.1 0.0 copy-done.2
  83.1 0.9 copy-done.3
  84.0 42.0 %trailing.1 = f32[1536,24,128]{2,1,0:T(8,128)} custom-call(s32[5]{0:T(128)} %stack.36.info, bf16[9,128,512]{2,1,0:T(8,128)(2,1)} %copy-done.1, bf16[9,128,512]{2,1,0:T(8,128)(2,1)} %collective-permute-done.8.refs_1_, bf16[2,3,128,512]{3,2,1,0:T(8,128)(2,1)} %copy-done.2, bf16[9,128,512]{2,1,0:T(8,128)(2,1)} %collective-permute-done.11.refs_3_, ...), custom_call_target="tpu_custom_call" | custom-call | flops 48318382080 | bytes 18874368 | tf_op jit(solution)/shard_map/trailing/pallas_call | solution.py:383
  (4 shorter events, 0.1 us)
Async XLA Ops:
  0.6 15.3 %collective-permute-start = (bf16[12,32,512]{2,1,0:T(8,128)(2,1)}, bf16[12,32,512]{2,1,0:T(8,128)(2,1)S(1)}, u32[]{:S(2)}, u32[]{:S(2)}) collective-permute-start(bf16[12,32,512]{2,1,0:T(8,128)(2,1)} %bitcast.53), channel_id=1, source_target_pairs={{0,1},{1,2},{2,3},{3,0},{4,5},{5,6},{6,7},{7,4},{8,9},{9,10},{10,1... | collective-permute-start | bytes 1179656 | tf_op jit(solution)/shard_map/ppermute | solution.py:425
  3.7 22.0 %collective-permute-start.1 = (bf16[12,32,512]{2,1,0:T(8,128)(2,1)}, bf16[12,32,512]{2,1,0:T(8,128)(2,1)S(1)}, u32[]{:S(2)}, u32[]{:S(2)}) collective-permute-start(bf16[12,32,512]{2,1,0:T(8,128)(2,1)} %bitcast.54), channel_id=1, source_target_pairs={{0,3},{1,0},{2,1},{3,2},{4,7},{5,4},{6,5},{7,6},{8,11},{9,8},{10,9... | collective-permute-start | bytes 1179656 | tf_op jit(solution)/shard_map/ppermute | solution.py:425
  15.9 12.5 %collective-permute-start.3 = (bf16[32,512]{1,0:T(8,128)(2,1)S(1)}, bf16[32,512]{1,0:T(8,128)(2,1)S(1)}, u32[]{:S(2)}, u32[]{:S(2)}) collective-permute-start(bf16[32,512]{1,0:T(8,128)(2,1)S(1)} %slice_bitcast_fusion.1), channel_id=1, source_target_pairs={{0,1},{1,2},{2,3},{3,0},{4,5},{5,6},{6,7},{7,4}} | collective-permute-start | bytes 98312 | tf_op jit(solution)/shard_map/ppermute | solution.py:425
  17.9 15.9 %collective-permute-start.2 = (bf16[12,32,512]{2,1,0:T(8,128)(2,1)S(1)}, bf16[12,32,512]{2,1,0:T(8,128)(2,1)S(1)}, u32[]{:S(2)}, u32[]{:S(2)}) collective-permute-start(bf16[12,32,512]{2,1,0:T(8,128)(2,1)S(1)} %collective-permute-done), channel_id=1, source_target_pairs={{0,1},{1,2},{2,3},{3,0},{4,5},{5,6},{6,7},{7,4},{8,9},{9,10},{10,1... | collective-permute-start | bytes 1179656 | tf_op jit(solution)/shard_map/ppermute | solution.py:425
  30.0 3.8 %collective-permute-start.4 = (bf16[128,512]{1,0:T(8,128)(2,1)S(1)}, bf16[128,512]{1,0:T(8,128)(2,1)S(1)}, u32[]{:S(2)}, u32[]{:S(2)}) collective-permute-start(bf16[128,512]{1,0:T(8,128)(2,1)S(1)} %pad_maximum_fusion.2), channel_id=1, source_target_pairs={{0,8},{1,9},{2,10},{3,11},{4,12},{5,13},{6,14},{7,15}} | collective-permute-start | bytes 393224 | tf_op jit(solution)/shard_map/ppermute | solution.py:425
  33.9 4.0 %collective-permute-start.5 = (bf16[128,512]{1,0:T(8,128)(2,1)S(1)}, bf16[128,512]{1,0:T(8,128)(2,1)S(1)}, u32[]{:S(2)}, u32[]{:S(2)}) collective-permute-start(bf16[128,512]{1,0:T(8,128)(2,1)S(1)} %broadcast_select_fusion.2), channel_id=1, source_target_pairs={{0,16},{1,17},{2,18},{3,19},{4,20},{5,21},{6,22},{7,23},{8,24},{9,... | collective-permute-start | bytes 393224 | tf_op jit(solution)/shard_map/ppermute | solution.py:425
  38.5 9.8 %collective-permute-start.6 = (bf16[128,512]{1,0:T(8,128)(2,1)}, bf16[128,512]{1,0:T(8,128)(2,1)}, u32[]{:S(2)}, u32[]{:S(2)}) collective-permute-start(bf16[128,512]{1,0:T(8,128)(2,1)} %broadcast_select_fusion.3.own_ref), channel_id=1, source_target_pairs={{0,4},{1,5},{2,6},{3,7},{4,0},{5,1},{6,2},{7,3},{8,12},{9,13},{10,... | collective-permute-start | bytes 393224 | tf_op jit(solution)/shard_map/ppermute | solution.py:425
  38.7 20.4 %copy-start = (bf16[12,128,512]{2,1,0:T(8,128)(2,1)}, bf16[12,128,512]{2,1,0:T(8,128)(2,1)S(1)}, u32[]{:S(2)}) copy-start(bf16[12,128,512]{2,1,0:T(8,128)(2,1)S(1)} %pad_maximum_fusion) | copy-start | bytes 4718596
  38.8 20.3 %collective-permute-start.7 = (bf16[9,128,512]{2,1,0:T(8,128)(2,1)S(1)}, bf16[9,128,512]{2,1,0:T(8,128)(2,1)}, u32[]{:S(2)}, u32[]{:S(2)}) collective-permute-start(bf16[9,128,512]{2,1,0:T(8,128)(2,1)S(1)} %slice.24), channel_id=1, source_target_pairs={{0,8},{5,13},{10,2},{15,7},{16,24},{21,29},{26,18},{31,23}} | collective-permute-start | bytes 3538952 | tf_op jit(solution)/shard_map/ppermute | solution.py:425
  44.0 17.2 %collective-permute-start.9 = (bf16[3,128,512]{2,1,0:T(8,128)(2,1)S(1)}, bf16[3,128,512]{2,1,0:T(8,128)(2,1)S(1)}, u32[]{:S(2)}, u32[]{:S(2)}) collective-permute-start(bf16[3,128,512]{2,1,0:T(8,128)(2,1)S(1)} %slice.25), channel_id=1, source_target_pairs={{0,16},{5,21},{10,26},{15,31},{16,0},{21,5},{26,10},{31,15}} | collective-permute-start | bytes 1179656 | tf_op jit(solution)/shard_map/ppermute | solution.py:425
  59.2 15.1 %copy-start.1 = (bf16[9,128,512]{2,1,0:T(8,128)(2,1)}, bf16[9,128,512]{2,1,0:T(8,128)(2,1)S(1)}, u32[]{:S(2)}) copy-start(bf16[9,128,512]{2,1,0:T(8,128)(2,1)S(1)} %broadcast_select_fusion.refs_0_) | copy-start | bytes 3538948
  59.2 18.2 %collective-permute-start.8 = (bf16[9,128,512]{2,1,0:T(8,128)(2,1)S(1)}, bf16[9,128,512]{2,1,0:T(8,128)(2,1)}, u32[]{:S(2)}, u32[]{:S(2)}) collective-permute-start(bf16[9,128,512]{2,1,0:T(8,128)(2,1)S(1)} %broadcast_select_fusion.refs_0_), channel_id=1, source_target_pairs={{0,16},{2,18},{5,21},{7,23},{8,24},{10,26},{13,29},{15,31},{16,0},... | collective-permute-start | bytes 3538952 | tf_op jit(solution)/shard_map/ppermute | solution.py:425
  61.2 18.6 %collective-permute-start.10 = (bf16[2,3,128,512]{3,2,1,0:T(8,128)(2,1)S(1)}, bf16[2,3,128,512]{3,2,1,0:T(8,128)(2,1)S(1)}, u32[]{:S(2)}, u32[]{:S(2)}) collective-permute-start(bf16[2,3,128,512]{3,2,1,0:T(8,128)(2,1)S(1)} %pad_maximum_fusion.1), channel_id=1, source_target_pairs={{0,8},{5,13},{10,2},{15,7},{16,24},{21,29},{26,18},{31,23}} | collective-permute-start | bytes 2359304 | tf_op jit(solution)/shard_map/ppermute | solution.py:425
  74.3 8.9 %collective-permute-start.11 = (bf16[9,128,512]{2,1,0:T(8,128)(2,1)S(1)}, bf16[9,128,512]{2,1,0:T(8,128)(2,1)}, u32[]{:S(2)}, u32[]{:S(2)}) collective-permute-start(bf16[9,128,512]{2,1,0:T(8,128)(2,1)S(1)} %broadcast_select_fusion.refs_0_), channel_id=1, source_target_pairs={{0,4},{2,6},{5,1},{7,3},{8,12},{10,14},{13,9},{15,11},{16,20},{18,... | collective-permute-start | bytes 3538952 | tf_op jit(solution)/shard_map/ppermute | solution.py:425
  77.4 5.7 %collective-permute-start.12 = (bf16[9,128,512]{2,1,0:T(8,128)(2,1)}, bf16[9,128,512]{2,1,0:T(8,128)(2,1)}, u32[]{:S(2)}, u32[]{:S(2)}) collective-permute-start(bf16[9,128,512]{2,1,0:T(8,128)(2,1)} %collective-permute-done.8.refs_1_), channel_id=1, source_target_pairs={{0,4},{2,6},{5,1},{7,3},{8,12},{10,14},{13,9},{15,11},{16,20},{18,... | collective-permute-start | bytes 3538952 | tf_op jit(solution)/shard_map/ppermute | solution.py:425
  79.9 3.2 %copy-start.2 = (bf16[2,3,128,512]{3,2,1,0:T(8,128)(2,1)}, bf16[2,3,128,512]{3,2,1,0:T(8,128)(2,1)S(1)}, u32[]{:S(2)}) copy-start(bf16[2,3,128,512]{3,2,1,0:T(8,128)(2,1)S(1)} %broadcast_select_fusion.1.refs_2_) | copy-start | bytes 2359300
  79.9 3.2 %collective-permute-start.13 = (bf16[2,3,128,512]{3,2,1,0:T(8,128)(2,1)S(1)}, bf16[2,3,128,512]{3,2,1,0:T(8,128)(2,1)S(1)}, u32[]{:S(2)}, u32[]{:S(2)}) collective-permute-start(bf16[2,3,128,512]{3,2,1,0:T(8,128)(2,1)S(1)} %broadcast_select_fusion.1.refs_2_), channel_id=1, source_target_pairs={{0,4},{2,6},{5,1},{7,3},{8,12},{10,14},{13,9},{15,11},{16,20},{18,... | collective-permute-start | bytes 2359304 | tf_op jit(solution)/shard_map/ppermute | solution.py:425
  83.1 0.9 copy-start.3
